TPU v7x, 32 devices: a whole 2x2x4 slice. The times are simulated.
32 devices in a mesh: clip: 2 (over y), tile: 4 (over z), slab: 2 (over x), chan: 2 (over core).
Axes of the slice: x: 2, y: 2, z: 4, core: 2. Of those that a mesh axis runs over, the one named last changes fastest.
Arguments:
- video: bfloat16 [16, 16, 128, 128], P(('clip', 'slab'), 'tile'), parts along dimension 0, may hold values from -6 to 6
- first_weight: bfloat16 [3, 3, 3, 128, 128], P(None, None, None, None, 'chan'), may hold values from -0.109375 to 0.109375
- first_bias: float32 [128], P('chan'), may hold values from -3 to 3
- second_weight: bfloat16 [3, 3, 3, 128, 256], replicated, may hold values from -0.109375 to 0.109375
- second_bias: float32 [256], P('chan'), may hold values from -3 to 3
Outputs:
- latents: bfloat16 [8, 16, 128, 256], P(('clip', 'slab'), 'tile', None, 'chan'), parts along dimension 0
There are 2 independent parts, one for each index of `clip`. A program takes and returns all parts, laid end to end along the dimension named above; an argument that names none is the same for every part. Nothing has to cross between parts.
All inputs are finite; a program needn't handle non-finite values.
Results may differ from a plain program's by a relative error of at most 0.0095.
Values may be sent and summed in bfloat16 or wider, within the bound.
No kernel may reach another device: no remote copies, remote signals or barrier semaphores. Data moves between devices by JAX's collectives and lax.ppermute only.
A program may use at most 64 MiB of HBM per device.

v0:
```python
import jax
import jax.numpy as jnp
from jax import lax
from jax.sharding import PartitionSpec as P


def passed_along(value, axis, steps):
    count = lax.axis_size(axis)
    first, last = (max(0, -steps), min(count, count - steps))
    return lax.ppermute(value, axis, [(source, source + steps) for source in range(first, last)])


def padded_2(block, sides, width):
    for axis, dim in sides:
        count = lax.axis_size(axis)
        forward = [(i, i + 1) for i in range(count - 1)]
        backward = [(target, source) for source, target in forward]
        low = lax.ppermute(
            lax.slice_in_dim(block, block.shape[dim] - width, None, axis=dim), axis, forward
        )
        high = lax.ppermute(lax.slice_in_dim(block, 0, width, axis=dim), axis, backward)
        block = jnp.concatenate([low, block, high], axis=dim)
    return block


def convolve(extended, kernel, stride, frames):
    columns = extended.shape[2]
    height = extended.shape[1] - 2
    padded = jnp.pad(extended, ((0, 0), (0, 0), (1, 1), (0, 0)))
    stacked = jnp.concatenate(
        [padded[:, :, offset_col : offset_col + columns, :] for offset_col in range(3)], axis=3
    )
    accumulated = jnp.zeros((frames, height, columns, kernel.shape[4]), jnp.float32)
    for offset_time in range(3):
        for offset_row in range(3):
            window = stacked[
                offset_time : offset_time + stride * (frames - 1) + 1 : stride,
                offset_row : offset_row + height,
            ]
            matrix = kernel[offset_time, offset_row].reshape(3 * kernel.shape[3], kernel.shape[4])
            accumulated = accumulated + jnp.einsum(
                "fhwc,cd->fhwd", window, matrix, preferred_element_type=jnp.float32
            )
    return accumulated


def shards(video, first_weight, first_bias, second_weight, second_bias):
    frames = video.shape[0]
    cached = passed_along(video[-2:], "slab", 1)
    extended = padded_2(jnp.concatenate([cached, video], 0), (("tile", 1),), 1)
    hidden = jax.nn.silu(convolve(extended, first_weight, 1, frames) + first_bias).astype(
        jnp.bfloat16
    )
    member = lax.axis_index("chan")
    complete = lax.all_gather(hidden, "chan", axis=3, tiled=True)
    cached_hidden = passed_along(complete[-2:], "slab", 1)
    widened = padded_2(jnp.concatenate([cached_hidden, complete], 0), (("tile", 1),), 1)
    portion = second_bias.shape[0]
    kernel = lax.dynamic_slice_in_dim(second_weight, member * portion, portion, 4)
    summed = convolve(widened, kernel, 2, frames // 2)
    return jax.nn.silu(summed + second_bias).astype(jnp.bfloat16)


def solution(mesh):
    placed = (
        P(("clip", "slab"), "tile", None, None),
        P(None, None, None, None, "chan"),
        P("chan"),
        P(),
        P("chan"),
    )
    return jax.shard_map(
        shards,
        mesh=mesh,
        in_specs=placed,
        out_specs=P(("clip", "slab"), "tile", None, "chan"),
        check_vma=False,
    )
```

profile of v0, /device:TPU:0, one launch (start us, length us, event | category | flops | bytes accessed | tf_op | source)
XLA Modules:
  0.0 62.3 jit_solution(2933252282464434936)
XLA Ops:
  0.0 1.0 %slice.140 = bf16[2,4,128,128]{3,2,1,0:T(8,128)(2,1)S(1)} slice(bf16[4,4,128,128]{3,2,1,0:T(8,128)(2,1)} %param.5), slice={[2:4], [0:4], [0:128], [0:128]} | slice | bytes 524288 | tf_op jit(solution)/shard_map/slice | solution.py:49
  1.0 4.9 %collective-permute-start = (bf16[2,4,128,128]{3,2,1,0:T(8,128)(2,1)S(1)}, bf16[2,4,128,128]{3,2,1,0:T(8,128)(2,1)S(1)}, u32[]{:S(2)}, u32[]{:S(2)}) collective-permute-start(bf16[2,4,128,128]{3,2,1,0:T(8,128)(2,1)S(1)} %slice.140), channel_id=1, source_target_pairs={{0,2},{1,3},{4,6},{5,7},{8,10},{9,11},{12,14},{13,15},{16,18},{17,... | collective-permute-start | bytes 786440 | tf_op jit(solution)/shard_map/ppermute | solution.py:10
  5.8 5.5 %collective-permute-done = bf16[2,4,128,128]{3,2,1,0:T(8,128)(2,1)S(1)} collective-permute-done((bf16[2,4,128,128]{3,2,1,0:T(8,128)(2,1)S(1)}, bf16[2,4,128,128]{3,2,1,0:T(8,128)(2,1)S(1)}, u32[]{:S(2)}, u32[]{:S(2)}) %collective-permute-start) | collective-permute-done | bytes 262176 | tf_op jit(solution)/shard_map/ppermute | solution.py:10
  11.4 1.1 %constant_dynamic-update-slice_fusion = bf16[6,4,128,128]{3,2,1,0:T(8,128)(2,1)S(1)} fusion(bf16[6,4,128,128]{3,2,1,0:T(8,128)(2,1)S(1)} %constant_dynamic-update-slice_fusion.1, bf16[4,4,128,128]{3,2,1,0:T(8,128)(2,1)} %param.5), kind=kLoop, calls=%fused_computation.72 | loop fusion | bytes 1048576 | tf_op jit(solution)/shard_map/concatenate | solution.py:50
  12.6 3.5 %collective-permute-start.1 = (bf16[6,1,128,128]{3,2,1,0:T(8,128)(2,1)S(1)}, bf16[6,1,128,128]{3,2,1,0:T(8,128)(2,1)S(1)}, u32[]{:S(2)}, u32[]{:S(2)}) collective-permute-start(bf16[6,1,128,128]{3,2,1,0:T(8,128)(2,1)S(1)} %get-tuple-element.20), channel_id=1, source_target_pairs={{0,4},{4,8},{8,12},{1,5},{5,9},{9,13},{2,6},{6,10},{10,14},{3,7},{... | collective-permute-start | bytes 589832 | tf_op jit(solution)/shard_map/ppermute | solution.py:18
  16.1 1.3 %collective-permute-start.2 = (bf16[6,1,128,128]{3,2,1,0:T(8,128)(2,1)S(1)}, bf16[6,1,128,128]{3,2,1,0:T(8,128)(2,1)S(1)}, u32[]{:S(2)}, u32[]{:S(2)}) collective-permute-start(bf16[6,1,128,128]{3,2,1,0:T(8,128)(2,1)S(1)} %get-tuple-element.21), channel_id=1, source_target_pairs={{4,0},{8,4},{12,8},{5,1},{9,5},{13,9},{6,2},{10,6},{14,10},{7,3},{... | collective-permute-start | bytes 589832 | tf_op jit(solution)/shard_map/ppermute | solution.py:21
  17.4 1.0 %fusion.68 = (bf16[1,1,3,128,64]{3,4,2,1,0:T(8,128)(2,1)S(1)}, bf16[1,1,3,128,64]{3,4,2,1,0:T(8,128)(2,1)S(1)}, bf16[1,1,3,128,64]{3,4,2,1,0:T(8,128)(2,1)S(1)},...) fusion(bf16[3,3,3,128,64]{3,4,2,1,0:T(8,128)(2,1)} %param.6), kind=kLoop, calls=%fused_computation.89 | loop fusion | bytes 884736 | tf_op jit(solution)/shard_map/slice | solution.py:40
  19.3 4.3 %collective-permute-done.2 = bf16[6,1,128,128]{3,2,1,0:T(8,128)(2,1)S(1)} collective-permute-done((bf16[6,1,128,128]{3,2,1,0:T(8,128)(2,1)S(1)}, bf16[6,1,128,128]{3,2,1,0:T(8,128)(2,1)S(1)}, u32[]{:S(2)}, u32[]{:S(2)}) %collective-permute-start.2) | collective-permute-done | bytes 196640 | tf_op jit(solution)/shard_map/ppermute | solution.py:21
  24.1 0.7 %fusion.65 = (bf16[6,6,128,128]{3,2,1,0:T(8,128)(2,1)S(1)}, bf16[6,6,128,128]{3,2,1,0:T(8,128)(2,1)S(1)}) fusion(bf16[6,6,130,128]{3,2,1,0:T(8,128)(2,1)S(1)} %fusion.11), kind=kLoop, calls=%fused_computation.86 | loop fusion | bytes 4718592 | tf_op jit(solution)/shard_map/slice | solution.py:31
  26.0 0.6 fusion.49
  26.6 0.6 fusion.51
  27.2 0.6 fusion.53
  29.7 0.6 fusion.61
  30.3 0.8 %multiply_convert_fusion.1 = bf16[4,4,128,64]{2,3,1,0:T(8,128)(2,1)S(1)} fusion(f32[4,4,128,64]{2,3,1,0:T(8,128)S(1)} %fusion.47, f32[4,4,128,64]{2,3,1,0:T(8,128)S(1)} %fusion.49, f32[4,4,128,64]{2,3,1,0:T(8,128)S(1)} %fusion.51, f32[4,4,128,64]{2,3,1,0:T(8,128)S(1)} %fusion.53, f32[4,4,128,64]{2,3,1,0:T(8,128)S(1)} %fusion.55, ...), kind=kOutput, calls=%fused_computation.54 | convolution fusion | flops 102498304 | bytes 8044800 | tf_op jit(solution)/shard_map/fhwc,cd->fhwd/dot_general | solution.py:41
  31.1 2.3 %all_gather.3 = bf16[4,4,128,128]{2,3,1,0:T(8,128)(2,1)S(1)} all-gather(bf16[4,4,128,64]{2,3,1,0:T(8,128)(2,1)S(1)} %multiply_convert_fusion.1), channel_id=1, replica_groups=mesh['clip'=2,'tile'=4,'slab'=2,'chan'=2] {'chan'}, dimensions={3}, use_global_device_ids=true | all-gather | bytes 786432 | tf_op jit(solution)/shard_map/all_gather | solution.py:55
  33.4 4.4 %collective-permute-start.3 = (bf16[2,4,128,128]{2,3,1,0:T(8,128)(2,1)S(1)}, bf16[2,4,128,128]{2,3,1,0:T(8,128)(2,1)S(1)}, u32[]{:S(2)}, u32[]{:S(2)}) collective-permute-start(bf16[2,4,128,128]{2,3,1,0:T(8,128)(2,1)S(1)} %slice.190), channel_id=1, source_target_pairs={{0,2},{1,3},{4,6},{5,7},{8,10},{9,11},{12,14},{13,15},{16,18},{17,... | collective-permute-start | bytes 786440 | tf_op jit(solution)/shard_map/ppermute | solution.py:10
  37.9 5.8 %collective-permute-done.3 = bf16[2,4,128,128]{2,3,1,0:T(8,128)(2,1)S(1)} collective-permute-done((bf16[2,4,128,128]{2,3,1,0:T(8,128)(2,1)S(1)}, bf16[2,4,128,128]{2,3,1,0:T(8,128)(2,1)S(1)}, u32[]{:S(2)}, u32[]{:S(2)}) %collective-permute-start.3) | collective-permute-done | bytes 262176 | tf_op jit(solution)/shard_map/ppermute | solution.py:10
  43.8 3.5 %collective-permute-start.4 = (bf16[6,1,128,128]{2,3,1,0:T(8,128)(2,1)S(1)}, bf16[6,1,128,128]{2,3,1,0:T(8,128)(2,1)S(1)}, u32[]{:S(2)}, u32[]{:S(2)}) collective-permute-start(bf16[6,1,128,128]{2,3,1,0:T(8,128)(2,1)S(1)} %get-tuple-element.18), channel_id=1, source_target_pairs={{0,4},{4,8},{8,12},{1,5},{5,9},{9,13},{2,6},{6,10},{10,14},{3,7},{... | collective-permute-start | bytes 589832 | tf_op jit(solution)/shard_map/ppermute | solution.py:18
  47.3 1.3 %collective-permute-start.5 = (bf16[6,1,128,128]{2,3,1,0:T(8,128)(2,1)S(1)}, bf16[6,1,128,128]{2,3,1,0:T(8,128)(2,1)S(1)}, u32[]{:S(2)}, u32[]{:S(2)}) collective-permute-start(bf16[6,1,128,128]{2,3,1,0:T(8,128)(2,1)S(1)} %get-tuple-element.19), channel_id=1, source_target_pairs={{4,0},{8,4},{12,8},{5,1},{9,5},{13,9},{6,2},{10,6},{14,10},{7,3},{... | collective-permute-start | bytes 589832 | tf_op jit(solution)/shard_map/ppermute | solution.py:21
  48.8 2.1 %collective-permute-done.4 = bf16[6,1,128,128]{2,3,1,0:T(8,128)(2,1)S(1)} collective-permute-done((bf16[6,1,128,128]{2,3,1,0:T(8,128)(2,1)S(1)}, bf16[6,1,128,128]{2,3,1,0:T(8,128)(2,1)S(1)}, u32[]{:S(2)}, u32[]{:S(2)}) %collective-permute-start.4) | collective-permute-done | bytes 196640 | tf_op jit(solution)/shard_map/ppermute | solution.py:18
  50.9 4.1 %collective-permute-done.5 = bf16[6,1,128,128]{2,3,1,0:T(8,128)(2,1)S(1)} collective-permute-done((bf16[6,1,128,128]{2,3,1,0:T(8,128)(2,1)S(1)}, bf16[6,1,128,128]{2,3,1,0:T(8,128)(2,1)S(1)}, u32[]{:S(2)}, u32[]{:S(2)}) %collective-permute-start.5) | collective-permute-done | bytes 196640 | tf_op jit(solution)/shard_map/ppermute | solution.py:21
  55.1 1.6 %fusion.6 = bf16[6,6,130,128]{2,3,1,0:T(8,128)(2,1)S(1)} fusion(bf16[6,1,128,128]{2,3,1,0:T(8,128)(2,1)S(1)} %collective-permute-done.5, bf16[6,4,128,128]{2,3,1,0:T(8,128)(2,1)S(1)} %constant_dynamic-update-slice_fusion.2, bf16[6,1,128,128]{2,3,1,0:T(8,128)(2,1)S(1)} %collective-permute-done.4), kind=kLoop, calls=%fused_computation.12 | loop fusion | flops 7188480 | bytes 2377728 | tf_op jit(solution)/shard_map/concatenate | solution.py:22
  56.7 0.6 fusion.64
  61.1 1.3 %multiply_convert_fusion = bf16[2,4,128,128]{3,2,1,0:T(8,128)(2,1)} fusion(f32[2,4,128,128]{3,2,1,0:T(8,128)S(1)} %fusion.28, f32[2,4,128,128]{3,2,1,0:T(8,128)S(1)} %fusion.30, f32[2,4,128,128]{3,2,1,0:T(8,128)S(1)} %fusion.32, f32[2,4,128,128]{3,2,1,0:T(8,128)S(1)} %fusion.34, f32[2,4,128,128]{3,2,1,0:T(8,128)S(1)} %fusion.36, ...), kind=kOutput, calls=%fused_computation.53 | convolution fusion | flops 102498304 | bytes 5341696 | tf_op jit(solution)/shard_map/fhwc,cd->fhwd/dot_general | solution.py:41
  (47 shorter events, 8.4 us)
Async XLA Ops:
  1.0 10.4 %collective-permute-start = (bf16[2,4,128,128]{3,2,1,0:T(8,128)(2,1)S(1)}, bf16[2,4,128,128]{3,2,1,0:T(8,128)(2,1)S(1)}, u32[]{:S(2)}, u32[]{:S(2)}) collective-permute-start(bf16[2,4,128,128]{3,2,1,0:T(8,128)(2,1)S(1)} %slice.140), channel_id=1, source_target_pairs={{0,2},{1,3},{4,6},{5,7},{8,10},{9,11},{12,14},{13,15},{16,18},{17,... | collective-permute-start | bytes 786440 | tf_op jit(solution)/shard_map/ppermute | solution.py:10
  12.6 6.8 %collective-permute-start.1 = (bf16[6,1,128,128]{3,2,1,0:T(8,128)(2,1)S(1)}, bf16[6,1,128,128]{3,2,1,0:T(8,128)(2,1)S(1)}, u32[]{:S(2)}, u32[]{:S(2)}) collective-permute-start(bf16[6,1,128,128]{3,2,1,0:T(8,128)(2,1)S(1)} %get-tuple-element.20), channel_id=1, source_target_pairs={{0,4},{4,8},{8,12},{1,5},{5,9},{9,13},{2,6},{6,10},{10,14},{3,7},{... | collective-permute-start | bytes 589832 | tf_op jit(solution)/shard_map/ppermute | solution.py:18
  16.1 7.6 %collective-permute-start.2 = (bf16[6,1,128,128]{3,2,1,0:T(8,128)(2,1)S(1)}, bf16[6,1,128,128]{3,2,1,0:T(8,128)(2,1)S(1)}, u32[]{:S(2)}, u32[]{:S(2)}) collective-permute-start(bf16[6,1,128,128]{3,2,1,0:T(8,128)(2,1)S(1)} %get-tuple-element.21), channel_id=1, source_target_pairs={{4,0},{8,4},{12,8},{5,1},{9,5},{13,9},{6,2},{10,6},{14,10},{7,3},{... | collective-permute-start | bytes 589832 | tf_op jit(solution)/shard_map/ppermute | solution.py:21
  29.1 1.2 %copy-start.1 = (f32[64]{0:T(128)S(1)}, f32[64]{0:T(128)}, u32[]{:S(2)}) copy-start(f32[64]{0:T(128)} %param.7) | copy-start | bytes 772
  31.1 17.5 %copy-start = (bf16[3,3,3,128,256]{4,3,2,1,0:T(8,128)(2,1)S(1)}, bf16[3,3,3,128,256]{4,3,2,1,0:T(8,128)(2,1)}, u32[]{:S(2)}) copy-start(bf16[3,3,3,128,256]{4,3,2,1,0:T(8,128)(2,1)} %param.8) | copy-start | bytes 5308420
  33.4 10.2 %collective-permute-start.3 = (bf16[2,4,128,128]{2,3,1,0:T(8,128)(2,1)S(1)}, bf16[2,4,128,128]{2,3,1,0:T(8,128)(2,1)S(1)}, u32[]{:S(2)}, u32[]{:S(2)}) collective-permute-start(bf16[2,4,128,128]{2,3,1,0:T(8,128)(2,1)S(1)} %slice.190), channel_id=1, source_target_pairs={{0,2},{1,3},{4,6},{5,7},{8,10},{9,11},{12,14},{13,15},{16,18},{17,... | collective-permute-start | bytes 786440 | tf_op jit(solution)/shard_map/ppermute | solution.py:10
  43.8 7.1 %collective-permute-start.4 = (bf16[6,1,128,128]{2,3,1,0:T(8,128)(2,1)S(1)}, bf16[6,1,128,128]{2,3,1,0:T(8,128)(2,1)S(1)}, u32[]{:S(2)}, u32[]{:S(2)}) collective-permute-start(bf16[6,1,128,128]{2,3,1,0:T(8,128)(2,1)S(1)} %get-tuple-element.18), channel_id=1, source_target_pairs={{0,4},{4,8},{8,12},{1,5},{5,9},{9,13},{2,6},{6,10},{10,14},{3,7},{... | collective-permute-start | bytes 589832 | tf_op jit(solution)/shard_map/ppermute | solution.py:18
  47.3 7.7 %collective-permute-start.5 = (bf16[6,1,128,128]{2,3,1,0:T(8,128)(2,1)S(1)}, bf16[6,1,128,128]{2,3,1,0:T(8,128)(2,1)S(1)}, u32[]{:S(2)}, u32[]{:S(2)}) collective-permute-start(bf16[6,1,128,128]{2,3,1,0:T(8,128)(2,1)S(1)} %get-tuple-element.19), channel_id=1, source_target_pairs={{4,0},{8,4},{12,8},{5,1},{9,5},{13,9},{6,2},{10,6},{14,10},{7,3},{... | collective-permute-start | bytes 589832 | tf_op jit(solution)/shard_map/ppermute | solution.py:21
  59.0 2.1 %copy-start.2 = (f32[128]{0:T(128)S(1)}, f32[128]{0:T(128)}, u32[]{:S(2)}) copy-start(f32[128]{0:T(128)} %param.9) | copy-start | bytes 1540
where the time goes:
time: 62.7 us; the launch traced here: 62.3 us
  waiting for transfers between devices  21.9 us (35%)
  starting transfers between devices  18.8 us (30%)
  matrix products  10.2 us (16%)
  local copies, waits for them, and re-layouts  5.66 us (9%)
  other arithmetic  3.07 us (5%)
  blocking collectives  2.31 us (4%)
    ppermute x2, waiting for transfers between devices, passed_along(): lax.ppermute(value, axis, [(source, source + steps) for source in range(f...  11.4 us
    dot_general x18, matrix products, convolve(): jnp.einsum('fhwc,cd->fhwd', window, matrix, preferred_element_type=jnp.fl...  10.2 us
    ppermute x2, starting transfers between devices, passed_along(): lax.ppermute(value, axis, [(source, source + steps) for source in range(f...  9.26 us
    ppermute x2, waiting for transfers between devices, padded_2(): lax.ppermute(lax.slice_in_dim(block, 0, width, axis=dim), axis, backward)  8.42 us
    ppermute x2, starting transfers between devices, padded_2(): lax.ppermute(lax.slice_in_dim(block, block.shape[dim] - width, None, axis...  6.98 us
    ppermute x2, starting transfers between devices, padded_2(): lax.ppermute(lax.slice_in_dim(block, 0, width, axis=dim), axis, backward)  2.58 us
    all_gather x1, blocking collectives, shards(): complete = lax.all_gather(hidden, 'chan', axis=3, tiled=True)  2.31 us
    ppermute x2, waiting for transfers between devices, padded_2(): lax.ppermute(lax.slice_in_dim(block, block.shape[dim] - width, None, axis...  2.09 us
  transfers between devices with their start and end apart: 6, of which 5 were waited for; matrix products, arithmetic and copies ran while one was open for 3% of the time, Pallas kernels for 0%

commit v1 on v0

v1 whole, which is shorter than its diff:
```python
import functools

import jax
import jax.numpy as jnp
from jax import lax
from jax.experimental import pallas as pl
from jax.experimental.pallas import tpu as pltpu
from jax.sharding import PartitionSpec as P

VMEM = pl.BlockSpec(memory_space=pltpu.VMEM)
ANY = pl.BlockSpec(memory_space=pl.ANY)
LIMIT = 48 * 1024 * 1024


def silu(value):
    return value / (1.0 + jnp.exp(-value))


def shifted_sum(parts, columns):
    size = parts[0].shape[0]
    cell = lax.broadcasted_iota(jnp.int32, parts[0].shape, 0) % columns
    low = jnp.where(cell == 0, 0.0, pltpu.roll(parts[0], 1, 0))
    high = jnp.where(cell == columns - 1, 0.0, pltpu.roll(parts[2], size - 1, 0))
    return parts[1] + low + high


def side():
    core = lax.axis_index("chan")
    return core, 2 * (1 - core), 2 * core


def border_known():
    core, tile = lax.axis_index("chan"), lax.axis_index("tile")
    last = lax.axis_size("tile") - 1
    return jnp.logical_not(jnp.logical_or((core == 0) & (tile == 0), (core == 1) & (tile == last)))


def pack_kernel(own, other, packed):
    core = lax.axis_index("chan")
    taps = own.shape[0]
    width = own.shape[3]
    for a in range(taps):
        for e in range(taps):
            full = []
            for b in range(taps):
                mine, theirs = own[a, b, e], other[a, b, e]
                left = jnp.where(core == 0, mine, theirs)
                right = jnp.where(core == 0, theirs, mine)
                full.append(jnp.concatenate([left, right], axis=1))
            nothing = jnp.zeros_like(full[0])
            for i in range(taps + 1):
                pair = [full[i - j] if 0 <= i - j < taps else nothing for j in range(2)]
                packed[
                    (a * (taps + 1) + i) * width : (a * (taps + 1) + i + 1) * width,
                    e * 2 * width : (e + 1) * 2 * width,
                ] = jnp.concatenate(pair, axis=1)


def first_layer(stack, start, frames, packed, bias):
    rows, columns, width = stack.shape[1:]
    taps = 3
    left = jnp.concatenate(
        [
            stack[start + a : start + a + frames, i].reshape(frames * columns, width)
            for a in range(taps)
            for i in range(rows)
        ],
        axis=1,
    )
    double = packed.shape[1] // taps
    parts = [
        jnp.dot(left, packed[:, e * double : (e + 1) * double], preferred_element_type=jnp.float32)
        for e in range(taps)
    ]
    return silu(shifted_sum(parts, columns) + bias).astype(jnp.bfloat16)


def whole_bias(core, own, other):
    return jnp.where(
        core == 0,
        jnp.concatenate([own[...], other[...]], axis=1),
        jnp.concatenate([other[...], own[...]], axis=1),
    )


def run_copies(copies):
    for copy in copies:
        copy.start()
    for copy in copies:
        copy.wait()


def inner_kernel(video, beyond, passed, passed_other, packed, bias_own, bias_other, hidden, stack, edge, sems):
    core, mine, over = side()
    slab = lax.axis_index("slab")
    known = border_known()
    frames = video.shape[0]
    extra = edge.shape[0]
    half = beyond.shape[1]
    columns = video.shape[2]

    always = [
        pltpu.make_async_copy(video.at[0:extra], stack.at[frames : frames + extra], sems.at[0]),
        pltpu.make_async_copy(
            video.at[0:extra, pl.ds(core * half, half)], edge.at[:, pl.ds(mine, half)], sems.at[1]
        ),
    ]
    earlier = [
        pltpu.make_async_copy(passed, stack.at[0:frames, pl.ds(core * half, half)], sems.at[2]),
        pltpu.make_async_copy(
            passed_other, stack.at[0:frames, pl.ds((1 - core) * half, half)], sems.at[3]
        ),
    ]
    border = pltpu.make_async_copy(beyond.at[0:extra], edge.at[:, pl.ds(over, half)], sems.at[4])
    for copy in always:
        copy.start()

    @pl.when(slab > 0)
    def _():
        run_copies(earlier)

    @pl.when(slab == 0)
    def _():
        stack[0:frames] = jnp.zeros((frames,) + stack.shape[1:], stack.dtype)

    @pl.when(known)
    def _():
        run_copies([border])

    @pl.when(jnp.logical_not(known))
    def _():
        edge[:, pl.ds(over, half)] = jnp.zeros((extra, half) + edge.shape[2:], edge.dtype)

    for copy in always:
        copy.wait()

    bias = whole_bias(core, bias_own, bias_other)
    bias = jnp.concatenate([bias, bias], axis=1)
    count = hidden.shape[0]
    width = hidden.shape[3]
    inner = first_layer(stack, 0, count, packed, bias).reshape(count, columns, 2 * width)
    for n in range(count):
        for j in range(2):
            row = inner[n, :, j * width : (j + 1) * width]
            if n < count - extra:
                row = jnp.where(slab > 0, row, jnp.zeros_like(row))
            hidden[n, mine + j] = row
    outer = first_layer(edge, 0, 1, packed, bias)
    for j in range(2):
        row = outer[:, j * width : (j + 1) * width]
        inside = known | (core != j)
        hidden[count - 1, over + j] = jnp.where(inside, row, jnp.zeros_like(row))


def outer_kernel(
    own, beyond, passed, passed_beyond, started, packed, second, bias_own, bias_other, out_own, out_other,
    latents, given, hidden, edge, sems,
):
    core, mine, over = side()
    slab = lax.axis_index("slab")
    known = border_known()
    frames, half, columns, width = own.shape
    late = edge.shape[0] - frames
    count = hidden.shape[0]

    begun = pltpu.make_async_copy(started, hidden, sems.at[0])
    always = [
        pltpu.make_async_copy(own.at[0:late], edge.at[frames : frames + late, pl.ds(mine, half)], sems.at[1])
    ]
    earlier = [pltpu.make_async_copy(passed, edge.at[0:frames, pl.ds(mine, half)], sems.at[2])]
    border = [
        pltpu.make_async_copy(beyond.at[0:late], edge.at[frames : frames + late, pl.ds(over, half)], sems.at[3])
    ]
    corner = [pltpu.make_async_copy(passed_beyond, edge.at[0:frames, pl.ds(over, half)], sems.at[4])]
    begun.start()
    for copy in always:
        copy.start()

    @pl.when(slab > 0)
    def _():
        run_copies(earlier)

    @pl.when(slab == 0)
    def _():
        edge[0:frames] = jnp.zeros((frames,) + edge.shape[1:], edge.dtype)

    @pl.when(known)
    def _():
        run_copies(border)

    @pl.when(known & (slab > 0))
    def _():
        run_copies(corner)

    @pl.when(jnp.logical_not(known))
    def _():
        edge[:, pl.ds(over, half)] = jnp.zeros((edge.shape[0], half) + edge.shape[2:], edge.dtype)

    for copy in always:
        copy.wait()
    begun.wait()

    bias = whole_bias(core, bias_own, bias_other)
    bias = jnp.concatenate([bias, bias], axis=1)
    outer = first_layer(edge, 0, count - 1, packed, bias).reshape(count - 1, columns, 2 * width)
    for n in range(count - 1):
        for j in range(2):
            row = outer[n, :, j * width : (j + 1) * width]
            inside = known | (core != j)
            if n < 2:
                inside = inside & (slab > 0)
            hidden[n, over + j] = jnp.where(inside, row, jnp.zeros_like(row))

    taps = second.shape[0]
    results = given.shape[0]
    left = jnp.concatenate(
        [
            jnp.concatenate(
                [hidden[2 * t + a, b : b + half].reshape(half * columns, width) for t in range(results)], axis=0
            )
            for a in range(taps)
            for b in range(taps)
        ],
        axis=1,
    )
    parts = [
        jnp.dot(
            left,
            jnp.concatenate([second[a, b, e] for a in range(taps) for b in range(taps)], axis=0),
            preferred_element_type=jnp.float32,
        )
        for e in range(taps)
    ]
    total = silu(shifted_sum(parts, columns) + whole_bias(core, out_own, out_other)).astype(jnp.bfloat16)
    portion = given.shape[3]
    total = total.reshape(results, half, columns, 2 * portion)
    low, high = total[..., :portion], total[..., portion:]
    latents[:, pl.ds(core * half, half)] = jnp.where(core == 0, low, high)
    given[...] = jnp.where(core == 0, high, low)


def cycle(value, axis):
    count = lax.axis_size(axis)
    return lax.ppermute(value, axis, [(i, (i + 1) % count) for i in range(count)])


def across_border(value):
    clips, tiles = lax.axis_size("clip"), lax.axis_size("tile")
    pairs = []
    for clip in range(clips):
        at = lambda c, t, k: (c * tiles + t) * 2 + k
        for tile in range(tiles - 1):
            pairs.append((at(clip, tile, 1), at(clip, tile + 1, 0)))
            pairs.append((at(clip, tile + 1, 0), at(clip, tile, 1)))
        if clips > 1:
            pairs.append((at(clip, 0, 0), at((clip + 1) % clips, 0, 0)))
            pairs.append((at(clip, tiles - 1, 1), at((clip + 1) % clips, tiles - 1, 1)))
    return lax.ppermute(value, ("clip", "tile", "chan"), pairs)


def params():
    return pltpu.CompilerParams(vmem_limit_bytes=LIMIT)


def shards(video, first_weight, first_bias, second_weight, second_bias):
    frames, rows, columns, width = video.shape
    half = rows // 2
    taps = first_weight.shape[0]
    assert half == taps - 1 and frames == 2 * (taps - 1) and lax.axis_size("chan") == 2
    core = lax.axis_index("chan")
    bf16 = jnp.bfloat16
    own = lax.dynamic_slice_in_dim(video, core * half, half, 1)
    beyond = across_border(own)
    passed = cycle(own, "slab")
    first_other = cycle(first_weight, "chan")
    bias_other = cycle(first_bias, "chan")
    out_other = cycle(second_bias, "chan")
    passed_beyond = cycle(beyond, "slab")
    passed_other = cycle(passed, "chan")

    packed = pl.pallas_call(
        pack_kernel,
        out_shape=jax.ShapeDtypeStruct((taps * (taps + 1) * width, taps * 2 * width), bf16),
        in_specs=[VMEM] * 2,
        out_specs=VMEM,
        compiler_params=params(),
        name="pack",
    )(first_weight, first_other)
    line = lambda v: v.reshape(1, -1)
    count = frames + 1
    started = pl.pallas_call(
        inner_kernel,
        out_shape=jax.ShapeDtypeStruct((count, rows, columns, width), bf16),
        in_specs=[ANY] * 4 + [VMEM] * 3,
        out_specs=VMEM,
        scratch_shapes=[
            pltpu.VMEM((frames + taps, rows, columns, width), bf16),
            pltpu.VMEM((taps, rows, columns, width), bf16),
            pltpu.SemaphoreType.DMA((5,)),
        ],
        compiler_params=params(),
        cost_estimate=pl.CostEstimate(flops=3_000_000_000, bytes_accessed=4_000_000, transcendentals=0),
        name="inner",
    )(video, beyond, passed, passed_other, packed, line(first_bias), line(bias_other))
    portion = second_bias.shape[0]
    latents, given = pl.pallas_call(
        outer_kernel,
        out_shape=[
            jax.ShapeDtypeStruct((frames // 2, rows, columns, portion), bf16),
            jax.ShapeDtypeStruct((frames // 2, half, columns, portion), bf16),
        ],
        in_specs=[ANY] * 5 + [VMEM] * 6,
        out_specs=[VMEM] * 2,
        scratch_shapes=[
            pltpu.VMEM((count, rows, columns, width), bf16),
            pltpu.VMEM((frames + taps - 1, rows, columns, width), bf16),
            pltpu.SemaphoreType.DMA((5,)),
        ],
        compiler_params=params(),
        cost_estimate=pl.CostEstimate(flops=3_000_000_000, bytes_accessed=4_000_000, transcendentals=0),
        name="outer",
    )(
        own, beyond, passed, passed_beyond, started, packed, second_weight,
        line(first_bias), line(bias_other), line(second_bias), line(out_other),
    )
    taken = cycle(given, "chan")
    return lax.dynamic_update_slice_in_dim(latents, taken, (1 - core) * half, 1)


def solution(mesh):
    placed = (
        P(("clip", "slab"), "tile", None, None),
        P(None, None, None, None, "chan"),
        P("chan"),
        P(),
        P("chan"),
    )
    return jax.shard_map(
        shards,
        mesh=mesh,
        in_specs=placed,
        out_specs=P(("clip", "slab"), "tile", None, "chan"),
        check_vma=False,
    )
```

time: 62.7 us -> 27.8 us (0.44)
  waiting for transfers between devices: 21.9 us -> 9.06 us
  starting transfers between devices: 18.8 us -> 6.92 us
  matrix products: 10.2 us -> 0 us
  Pallas kernels: 0 us -> 7.38 us
  other arithmetic: 3.07 us -> 0 us
  blocking collectives: 2.31 us -> 0 us
  local copies, waits for them, and re-layouts: 5.66 us -> 4.13 us
    ppermute x6 -> x8, waiting for transfers between devices: 21.9 us -> 9.06 us  [the longest x7 9.06 us: cycle(): lax.ppermute(value, axis, [(i, (i + 1) % count) for i in range(count)])]
    ppermute x6 -> x8, starting transfers between devices: 18.8 us -> 6.92 us  [the longest x7 5.4 us: cycle(): lax.ppermute(value, axis, [(i, (i + 1) % count) for i in range(count)])]
    dot_general x18 -> x0, matrix products: 10.2 us -> none  [convolve(): jnp.einsum('fhwc,cd->fhwd', window, matrix, preferred_element_type=jnp.fl...]
    pallas_call x0 -> x3, Pallas kernels: none -> 7.38 us  [the longest x1 4.46 us: shards(): pl.pallas_call(outer_kernel, out_shape=[jax.ShapeDtypeStruct((frames // 2...]
    slice x17 -> x0, local copies, waits for them, and re-layouts: 3.97 us -> none  [the longest x11 1.62 us: convolve(): kernel[offset_time, offset_row]]
    concatenate x4 -> x0, other arithmetic: 3.07 us -> none  [the longest x2 2.07 us: padded_2(): block = jnp.concatenate([low, block, high], axis=dim)]
    all_gather x1 -> x0, blocking collectives: 2.31 us -> none  [shards(): complete = lax.all_gather(hidden, 'chan', axis=3, tiled=True)]
    unnamed x8 -> x9, local copies, waits for them, and re-layouts: 0.05 us -> 2.05 us
  transfers between devices with their start and end apart: 6 -> 8, of which waited for: 5 -> 3; matrix products, arithmetic and copies ran while one was open for 3% -> 7% of each run, Pallas kernels for 0% -> 11%
where the time goes in v1:
time: 27.8 us; the launch traced here: 27.6 us
  waiting for transfers between devices  9.06 us (33%)
  Pallas kernels  7.38 us (27%)
  starting transfers between devices  6.92 us (25%)
  local copies, waits for them, and re-layouts  4.13 us (15%)
    ppermute x7, waiting for transfers between devices, cycle(): lax.ppermute(value, axis, [(i, (i + 1) % count) for i in range(count)])  9.06 us
    ppermute x7, starting transfers between devices, cycle(): lax.ppermute(value, axis, [(i, (i + 1) % count) for i in range(count)])  5.4 us
    pallas_call x1, Pallas kernels, shards(): pl.pallas_call(outer_kernel, out_shape=[jax.ShapeDtypeStruct((frames // 2...  4.46 us
    pallas_call x1, Pallas kernels, shards(): pl.pallas_call(inner_kernel, out_shape=jax.ShapeDtypeStruct((count, rows,...  2.53 us
    unnamed x9, local copies, waits for them, and re-layouts  2.05 us
    ppermute x1, starting transfers between devices, across_border(): return lax.ppermute(value, ('clip', 'tile', 'chan'), pairs)  1.52 us
    dynamic_slice x1, local copies, waits for them, and re-layouts, shards(): own = lax.dynamic_slice_in_dim(video, core * half, half, 1)  0.97 us
    dynamic_update_slice x1, local copies, waits for them, and re-layouts, shards(): return lax.dynamic_update_slice_in_dim(latents, taken, (1 - core) * half, 1)  0.68 us
  transfers between devices with their start and end apart: 8, of which 3 were waited for; matrix products, arithmetic and copies ran while one was open for 7% of the time, Pallas kernels for 11%

profile of v1, /device:TPU:0, one launch (start us, length us, event | category | flops | bytes accessed | tf_op | source)
XLA Modules:
  0.0 27.6 jit_solution(11077375422899363101)
XLA Ops:
  0.0 1.0 %constant_dynamic-slice_fusion.own = bf16[4,2,128,128]{3,2,1,0:T(8,128)(2,1)S(1)} fusion(bf16[4,4,128,128]{3,2,1,0:T(8,128)(2,1)} %video.1, s32[]{:T(128)S(6)} %select_n.6), kind=kLoop, calls=%fused_computation.1 | loop fusion | bytes 524292 | tf_op jit(solution)/shard_map/dynamic_slice | solution.py:272
  1.0 3.0 %collective-permute-start.1 = (bf16[4,2,128,128]{3,2,1,0:T(8,128)(2,1)S(1)}, bf16[4,2,128,128]{3,2,1,0:T(8,128)(2,1)S(1)}, u32[]{:S(2)}, u32[]{:S(2)}) collective-permute-start(bf16[4,2,128,128]{3,2,1,0:T(8,128)(2,1)S(1)} %constant_dynamic-slice_fusion.own), channel_id=1, source_target_pairs={{0,2},{2,0},{1,3},{3,1},{4,6},{6,4},{5,7},{7,5},{8,10},{10,8},{9,1... | collective-permute-start | bytes 786440 | tf_op jit(solution)/shard_map/ppermute | solution.py:244
  4.0 0.0 collective-permute-start.4
  4.0 1.5 %collective-permute-start = (bf16[4,2,128,128]{3,2,1,0:T(8,128)(2,1)S(1)}, bf16[4,2,128,128]{3,2,1,0:T(8,128)(2,1)S(1)}, u32[]{:S(2)}, u32[]{:S(2)}) collective-permute-start(bf16[4,2,128,128]{3,2,1,0:T(8,128)(2,1)S(1)} %constant_dynamic-slice_fusion.own), channel_id=1, source_target_pairs={{1,4},{4,1},{5,8},{8,5},{9,12},{12,9},{0,16},{13,29},{17,20},{20,1... | collective-permute-start | bytes 786440 | tf_op jit(solution)/shard_map/ppermute | solution.py:258
  5.5 4.8 %collective-permute-done.1.passed = bf16[4,2,128,128]{3,2,1,0:T(8,128)(2,1)S(1)} collective-permute-done((bf16[4,2,128,128]{3,2,1,0:T(8,128)(2,1)S(1)}, bf16[4,2,128,128]{3,2,1,0:T(8,128)(2,1)S(1)}, u32[]{:S(2)}, u32[]{:S(2)}) %collective-permute-start.1) | collective-permute-done | bytes 262176 | tf_op jit(solution)/shard_map/ppermute | solution.py:244
  10.3 0.0 collective-permute-start.3
  10.3 0.5 %collective-permute-start.5 = (f32[64]{0:T(128)}, f32[64]{0:T(128)S(1)}, u32[]{:S(2)}, u32[]{:S(2)}) collective-permute-start(f32[64]{0:T(128)} %param.7), channel_id=1, source_target_pairs={{0,1},{1,0},{2,3},{3,2},{4,5},{5,4},{6,7},{7,6},{8,9},{9,8},{10,11... | collective-permute-start | bytes 776 | tf_op jit(solution)/shard_map/ppermute | solution.py:244
  10.8 0.0 collective-permute-start.6
  10.8 1.4 %copy.8.own = bf16[3,3,3,128,64]{4,3,2,1,0:T(8,128)(2,1)S(1)} copy(bf16[3,3,3,128,64]{3,4,2,1,0:T(8,128)(2,1)} %param.6) | data formatting | bytes 884736 | tf_op args[1]
  12.2 0.0 collective-permute-done.beyond
  12.2 1.8 %collective-permute-start.2 = (bf16[4,2,128,128]{3,2,1,0:T(8,128)(2,1)S(1)}, bf16[4,2,128,128]{3,2,1,0:T(8,128)(2,1)S(1)}, u32[]{:S(2)}, u32[]{:S(2)}) collective-permute-start(bf16[4,2,128,128]{3,2,1,0:T(8,128)(2,1)S(1)} %collective-permute-done.beyond), channel_id=1, source_target_pairs={{0,2},{2,0},{1,3},{3,1},{4,6},{6,4},{5,7},{7,5},{8,10},{10,8},{9,1... | collective-permute-start | bytes 786440 | tf_op jit(solution)/shard_map/ppermute | solution.py:244
  14.1 0.0 collective-permute-done.4
  14.1 0.4 %copy.9.other = bf16[3,3,3,128,64]{4,3,2,1,0:T(8,128)(2,1)S(1)} copy(bf16[3,3,3,128,64]{3,4,2,1,0:T(8,128)(2,1)S(1)} %collective-permute-done.4) | data formatting | bytes 884736 | tf_op jit(solution)/shard_map/ppermute | solution.py:244
  14.5 0.0 copy-start
  14.5 0.0 copy-start.2
  14.5 0.4 %pack.1.packed = bf16[1536,768]{1,0:T(8,128)(2,1)S(1)} custom-call(bf16[3,3,3,128,64]{4,3,2,1,0:T(8,128)(2,1)S(1)} %copy.8.own, bf16[3,3,3,128,64]{4,3,2,1,0:T(8,128)(2,1)S(1)} %copy.9.other), custom_call_target="tpu_custom_call" | custom-call | tf_op jit(solution)/shard_map/pack/pallas_call | solution.py:281
  14.9 0.0 collective-permute-done.5
  14.9 0.6 %copy-done = bf16[4,4,128,128]{3,2,1,0:T(8,128)(2,1)S(1)} copy-done((bf16[4,4,128,128]{3,2,1,0:T(8,128)(2,1)S(1)}, bf16[4,4,128,128]{3,2,1,0:T(8,128)(2,1)}, u32[]{:S(2)}) %copy-start) | copy-done | bytes 524312
  15.5 2.5 %inner.1.started = bf16[5,4,128,128]{3,2,1,0:T(8,128)(2,1)S(1)} custom-call(bf16[4,4,128,128]{3,2,1,0:T(8,128)(2,1)S(1)} %copy-done, bf16[4,2,128,128]{3,2,1,0:T(8,128)(2,1)S(1)} %collective-permute-done.beyond, bf16[4,2,128,128]{3,2,1,0:T(8,128)(2,1)S(1)} %collective-permute-done.1.passed, bf16[4,2,128,128]{3,2,1,0:T(8,128)(2,1)S(1)} %collective-permute-done.3.passed_other, ...), custom_call_target="tpu_custom_call" | custom-call | flops 3000000000 | bytes 4000000 | tf_op jit(solution)/shard_map/inner/pallas_call | solution.py:291
  18.1 2.9 %collective-permute-done.2.passed_beyond = bf16[4,2,128,128]{3,2,1,0:T(8,128)(2,1)S(1)} collective-permute-done((bf16[4,2,128,128]{3,2,1,0:T(8,128)(2,1)S(1)}, bf16[4,2,128,128]{3,2,1,0:T(8,128)(2,1)S(1)}, u32[]{:S(2)}, u32[]{:S(2)}) %collective-permute-start.2) | collective-permute-done | bytes 262176 | tf_op jit(solution)/shard_map/ppermute | solution.py:244
  21.0 4.5 %outer.1 = (bf16[2,4,128,128]{3,2,1,0:T(8,128)(2,1)}, bf16[2,2,128,128]{3,2,1,0:T(8,128)(2,1)S(1)}) custom-call(bf16[4,2,128,128]{3,2,1,0:T(8,128)(2,1)S(1)} %constant_dynamic-slice_fusion.own, bf16[4,2,128,128]{3,2,1,0:T(8,128)(2,1)S(1)} %collective-permute-done.beyond, bf16[4,2,128,128]{3,2,1,0:T(8,128)(2,1)S(1)} %collective-permute-done.1.passed, ...), custom_call_target="tpu_custom_call" | custom-call | flops 3000000000 | bytes 4000000 | tf_op jit(solution)/shard_map/outer/pallas_call | solution.py:306
  25.5 0.1 collective-permute-start.7
  25.6 1.3 %collective-permute-done.7 = bf16[2,2,128,128]{3,2,1,0:T(8,128)(2,1)S(1)} collective-permute-done((bf16[2,2,128,128]{3,2,1,0:T(8,128)(2,1)S(1)}, bf16[2,2,128,128]{3,2,1,0:T(8,128)(2,1)S(1)}, u32[]{:S(2)}, u32[]{:S(2)}) %collective-permute-start.7) | collective-permute-done | bytes 131104 | tf_op jit(solution)/shard_map/ppermute | solution.py:244
  26.9 0.7 %constant_dynamic-update-slice_fusion = bf16[2,4,128,128]{3,2,1,0:T(8,128)(2,1)} fusion(bf16[2,4,128,128]{3,2,1,0:T(8,128)(2,1)} %get-tuple-element.7, bf16[2,2,128,128]{3,2,1,0:T(8,128)(2,1)S(1)} %collective-permute-done.7, s32[]{:T(128)S(6)} %select_n.7), kind=kLoop, calls=%fused_computation | loop fusion | bytes 262148 | tf_op jit(solution)/shard_map/dynamic_update_slice | solution.py:327
  (7 shorter events, 0.0 us)
Async XLA Ops:
  1.0 9.3 %collective-permute-start.1 = (bf16[4,2,128,128]{3,2,1,0:T(8,128)(2,1)S(1)}, bf16[4,2,128,128]{3,2,1,0:T(8,128)(2,1)S(1)}, u32[]{:S(2)}, u32[]{:S(2)}) collective-permute-start(bf16[4,2,128,128]{3,2,1,0:T(8,128)(2,1)S(1)} %constant_dynamic-slice_fusion.own), channel_id=1, source_target_pairs={{0,2},{2,0},{1,3},{3,1},{4,6},{6,4},{5,7},{7,5},{8,10},{10,8},{9,1... | collective-permute-start | bytes 786440 | tf_op jit(solution)/shard_map/ppermute | solution.py:244
  4.0 10.1 %collective-permute-start.4 = (bf16[3,3,3,128,64]{3,4,2,1,0:T(8,128)(2,1)}, bf16[3,3,3,128,64]{3,4,2,1,0:T(8,128)(2,1)S(1)}, u32[]{:S(2)}, u32[]{:S(2)}) collective-permute-start(bf16[3,3,3,128,64]{3,4,2,1,0:T(8,128)(2,1)} %param.6), channel_id=1, source_target_pairs={{0,1},{1,0},{2,3},{3,2},{4,5},{5,4},{6,7},{7,6},{8,9},{9,8},{10,11... | collective-permute-start | bytes 1327112 | tf_op jit(solution)/shard_map/ppermute | solution.py:244
  4.0 8.3 %collective-permute-start = (bf16[4,2,128,128]{3,2,1,0:T(8,128)(2,1)S(1)}, bf16[4,2,128,128]{3,2,1,0:T(8,128)(2,1)S(1)}, u32[]{:S(2)}, u32[]{:S(2)}) collective-permute-start(bf16[4,2,128,128]{3,2,1,0:T(8,128)(2,1)S(1)} %constant_dynamic-slice_fusion.own), channel_id=1, source_target_pairs={{1,4},{4,1},{5,8},{8,5},{9,12},{12,9},{0,16},{13,29},{17,20},{20,1... | collective-permute-start | bytes 786440 | tf_op jit(solution)/shard_map/ppermute | solution.py:258
  10.3 4.6 %collective-permute-start.3 = (bf16[4,2,128,128]{3,2,1,0:T(8,128)(2,1)S(1)}, bf16[4,2,128,128]{3,2,1,0:T(8,128)(2,1)S(1)}, u32[]{:S(2)}, u32[]{:S(2)}) collective-permute-start(bf16[4,2,128,128]{3,2,1,0:T(8,128)(2,1)S(1)} %collective-permute-done.1.passed), channel_id=1, source_target_pairs={{0,1},{1,0},{2,3},{3,2},{4,5},{5,4},{6,7},{7,6},{8,9},{9,8},{10,11... | collective-permute-start | bytes 786440 | tf_op jit(solution)/shard_map/ppermute | solution.py:244
  10.3 4.6 %collective-permute-start.5 = (f32[64]{0:T(128)}, f32[64]{0:T(128)S(1)}, u32[]{:S(2)}, u32[]{:S(2)}) collective-permute-start(f32[64]{0:T(128)} %param.7), channel_id=1, source_target_pairs={{0,1},{1,0},{2,3},{3,2},{4,5},{5,4},{6,7},{7,6},{8,9},{9,8},{10,11... | collective-permute-start | bytes 776 | tf_op jit(solution)/shard_map/ppermute | solution.py:244
  10.8 7.3 %collective-permute-start.6 = (f32[128]{0:T(128)}, f32[128]{0:T(128)S(1)}, u32[]{:S(2)}, u32[]{:S(2)}) collective-permute-start(f32[128]{0:T(128)} %param.9), channel_id=1, source_target_pairs={{0,1},{1,0},{2,3},{3,2},{4,5},{5,4},{6,7},{7,6},{8,9},{9,8},{10,11... | collective-permute-start | bytes 1544 | tf_op jit(solution)/shard_map/ppermute | solution.py:244
  12.2 8.8 %collective-permute-start.2 = (bf16[4,2,128,128]{3,2,1,0:T(8,128)(2,1)S(1)}, bf16[4,2,128,128]{3,2,1,0:T(8,128)(2,1)S(1)}, u32[]{:S(2)}, u32[]{:S(2)}) collective-permute-start(bf16[4,2,128,128]{3,2,1,0:T(8,128)(2,1)S(1)} %collective-permute-done.beyond), channel_id=1, source_target_pairs={{0,2},{2,0},{1,3},{3,1},{4,6},{6,4},{5,7},{7,5},{8,10},{10,8},{9,1... | collective-permute-start | bytes 786440 | tf_op jit(solution)/shard_map/ppermute | solution.py:244
  14.5 1.0 %copy-start = (bf16[4,4,128,128]{3,2,1,0:T(8,128)(2,1)S(1)}, bf16[4,4,128,128]{3,2,1,0:T(8,128)(2,1)}, u32[]{:S(2)}) copy-start(bf16[4,4,128,128]{3,2,1,0:T(8,128)(2,1)} %video.1) | copy-start | bytes 1572868
  14.5 1.0 %copy-start.2 = (f32[64]{0:T(128)S(1)}, f32[64]{0:T(128)}, u32[]{:S(2)}) copy-start(f32[64]{0:T(128)} %param.7) | copy-start | bytes 772
  15.5 5.5 %copy-start.1 = (bf16[3,3,3,128,256]{4,3,2,1,0:T(8,128)(2,1)S(1)}, bf16[3,3,3,128,256]{4,3,2,1,0:T(8,128)(2,1)}, u32[]{:S(2)}) copy-start(bf16[3,3,3,128,256]{4,3,2,1,0:T(8,128)(2,1)} %second.1) | copy-start | bytes 5308420
  15.5 5.5 %copy-start.3 = (f32[128]{0:T(128)S(1)}, f32[128]{0:T(128)}, u32[]{:S(2)}) copy-start(f32[128]{0:T(128)} %param.9) | copy-start | bytes 1540
  25.5 1.4 %collective-permute-start.7 = (bf16[2,2,128,128]{3,2,1,0:T(8,128)(2,1)S(1)}, bf16[2,2,128,128]{3,2,1,0:T(8,128)(2,1)S(1)}, u32[]{:S(2)}, u32[]{:S(2)}) collective-permute-start(bf16[2,2,128,128]{3,2,1,0:T(8,128)(2,1)S(1)} %get-tuple-element.8), channel_id=1, source_target_pairs={{0,1},{1,0},{2,3},{3,2},{4,5},{5,4},{6,7},{7,6},{8,9},{9,8},{10,11... | collective-permute-start | bytes 393224 | tf_op jit(solution)/shard_map/ppermute | solution.py:244

commit v2 on v0

v2 whole, which is shorter than its diff:
```python
import jax
import jax.numpy as jnp
from jax import lax
from jax.experimental import pallas as pl
from jax.experimental.pallas import tpu as pltpu
from jax.sharding import PartitionSpec as P

VMEM = pl.BlockSpec(memory_space=pltpu.VMEM)
ANY = pl.BlockSpec(memory_space=pl.ANY)
HBM = pl.BlockSpec(memory_space=pltpu.HBM)
LIMIT = 20 * 1024 * 1024
TAIL = 16


def silu(value):
    return value / (1.0 + jnp.exp(-value))


def shifted_sum(parts, columns):
    size = parts[0].shape[0]
    cell = lax.broadcasted_iota(jnp.int32, parts[0].shape, 0) % columns
    low = jnp.where(cell == 0, 0.0, pltpu.roll(parts[0], 1, 0))
    high = jnp.where(cell == columns - 1, 0.0, pltpu.roll(parts[2], size - 1, 0))
    return parts[1] + low + high


def border_known():
    core, tile = lax.axis_index("chan"), lax.axis_index("tile")
    last = lax.axis_size("tile") - 1
    return jnp.logical_not(jnp.logical_or((core == 0) & (tile == 0), (core == 1) & (tile == last)))


def thirds(value):
    high = value.astype(jnp.bfloat16)
    left = value - high.astype(jnp.float32)
    middle = left.astype(jnp.bfloat16)
    return [high, middle, (left - middle.astype(jnp.float32)).astype(jnp.bfloat16)]


def stage_kernel(video, weight, first_bias, second_bias, own, rest, staged, first_line, second_line, sems):
    core = lax.axis_index("chan")
    half = own.shape[1]
    size = weight.shape[0]
    pairs = (
        (video.at[:, pl.ds(core * half, half)], own),
        (video.at[:, pl.ds((1 - core) * half, half)], rest),
        (weight, staged.at[0:size]),
        (first_bias, first_line),
        (second_bias, second_line),
    )
    copies = [pltpu.make_async_copy(source, target, sems.at[k]) for k, (source, target) in enumerate(pairs)]
    for copy in copies:
        copy.start()
    for copy in copies[3:]:
        copy.wait()
    width = staged.shape[1]
    first = first_line[...]
    first = jnp.concatenate([first, jnp.zeros((1, width - first.shape[1]), first.dtype)], axis=1)
    rows = thirds(first) + thirds(second_line[...])
    rows.append(jnp.zeros((TAIL - len(rows), width), jnp.bfloat16))
    staged[size:] = jnp.concatenate(rows, axis=0)
    for copy in copies[:3]:
        copy.wait()


def join_kernel(kept, taken, latents, sems):
    core = lax.axis_index("chan")
    half = kept.shape[1]
    copies = [
        pltpu.make_async_copy(part, latents.at[:, pl.ds(place * half, half)], sems.at[k])
        for k, (part, place) in enumerate(((kept, core), (taken, 1 - core)))
    ]
    for copy in copies:
        copy.start()
    for copy in copies:
        copy.wait()


def pack_kernel(own, other, inner, outer, bias_first, bias_second):
    core = lax.axis_index("chan")
    known = border_known()
    taps = 3
    rows = taps + 1
    width = own.shape[1]
    size = own.shape[0] - TAIL
    channels = size // taps**3

    def lines(source):
        last = source[size:].astype(jnp.float32)
        added = [last[3 * k : 3 * k + 1] + last[3 * k + 1 : 3 * k + 2] + last[3 * k + 2 : 3 * k + 3] for k in range(2)]
        return added[0][:, :channels], added[1]

    mine, theirs = lines(own), lines(other)
    low = [jnp.where(core == 0, m, t) for m, t in zip(mine, theirs)]
    high = [jnp.where(core == 0, t, m) for m, t in zip(mine, theirs)]
    once = jnp.concatenate([low[0], high[0]], axis=1)
    bias_first[...] = jnp.concatenate([once, once], axis=1)
    bias_second[...] = jnp.concatenate([low[1], high[1]], axis=1)
    for a in range(taps):
        for e in range(taps):
            full = []
            for b in range(taps):
                at = ((a * taps + b) * taps + e) * channels
                mine, theirs = own[at : at + channels], other[at : at + channels]
                low = jnp.where(core == 0, mine, theirs)
                high = jnp.where(core == 0, theirs, mine)
                full.append(jnp.concatenate([low, high], axis=0).T)
            nothing = jnp.zeros_like(full[0])
            across = slice(e * 2 * width, (e + 1) * 2 * width)
            for i in range(rows):
                pair = [full[i - j] if 0 <= i - j < taps else nothing for j in range(2)]
                pair = jnp.concatenate(pair, axis=1)
                upper = i < rows // 2
                at = lax.rem(i + 2 * core, rows) + a * rows
                inner[pl.ds(pl.multiple_of(at * width, width), width), across] = pair
                at = lax.rem(i + 2 * (1 - core), rows) + a * rows
                used = known | (core == (1 if upper else 0))
                outer[pl.ds(pl.multiple_of(at * width, width), width), across] = jnp.where(
                    used, pair, jnp.zeros_like(pair)
                )


def first_layer(tile, frames, packed, bias):
    taps = 3
    rows = taps + 1
    left = jnp.concatenate(
        [
            jnp.concatenate([tile(f + a, k) for f in frames], axis=0)
            for a in range(taps)
            for k in range(rows)
        ],
        axis=1,
    )
    double = packed.shape[1] // taps
    columns = left.shape[0] // len(frames)
    parts = [
        jnp.dot(left, packed[:, e * double : (e + 1) * double], preferred_element_type=jnp.float32)
        for e in range(taps)
    ]
    return silu(shifted_sum(parts, columns) + bias).astype(jnp.bfloat16)


def second_layer(hidden, place, late, second):
    taps = second.shape[0]
    columns, width = hidden.shape[2:]
    results = (hidden.shape[0] - 1) // 2

    def added(rows):
        left = jnp.concatenate(
            [
                jnp.concatenate([hidden[2 * t + a, place + j] for t in range(results)], axis=0)
                for a in range(taps)
                for j, _ in rows
            ],
            axis=1,
        )
        parts = [
            jnp.dot(
                left,
                jnp.concatenate([second[a, b, e] for a in range(taps) for _, b in rows], axis=0),
                preferred_element_type=jnp.float32,
            )
            for e in range(taps)
        ]
        return shifted_sum(parts, columns)

    return added([(0, 1 - late), (1, 2 - late)]), added([(late, 2 * (1 - late))])


def inner_kernel(own, rest, beyond, passed, passed_other, packed, packed_outer, bias, second, hidden, partial):
    core = lax.axis_index("chan")
    slab = lax.axis_index("slab")
    known = border_known()
    frames, half, columns, width = own.shape
    mine, over = half * (1 - core), half * core

    def tile(f, k):
        if f >= frames:
            return own[f - frames, k] if k < half else rest[f - frames, k - half]
        row = passed[f, k] if k < half else passed_other[f, k - half]
        return jnp.where(slab > 0, row, jnp.zeros_like(row))

    count = hidden.shape[0]
    result = first_layer(tile, range(count), packed, bias[...])
    for n in range(count):
        for j in range(2):
            row = result[n * columns : (n + 1) * columns, j * width : (j + 1) * width]
            if n < 2:
                row = jnp.where(slab > 0, row, jnp.zeros_like(row))
            hidden[n, mine + j] = row

    def edge(f, k):
        return own[f - frames, k] if k < half else beyond[f - frames, k - half]

    result = first_layer(edge, [count - 1], packed_outer, bias[...])
    for j in range(2):
        row = result[:, j * width : (j + 1) * width]
        hidden[count - 1, over + j] = jnp.where(known | (core != j), row, jnp.zeros_like(row))
    both, one = second_layer(hidden, mine, core, second)
    partial[1 - core] = both
    partial[core] = one


def outer_kernel(
    own, beyond, passed, passed_beyond, started, partial, packed, second, bias, bias_second, kept, given, hidden
):
    core = lax.axis_index("chan")
    slab = lax.axis_index("slab")
    known = border_known()
    frames, half, columns, width = own.shape
    mine, over = half * (1 - core), half * core
    count = hidden.shape[0]
    def tile(f, k):
        if f >= frames:
            return own[f - frames, k] if k < half else beyond[f - frames, k - half]
        row = passed[f, k] if k < half else passed_beyond[f, k - half]
        return jnp.where(slab > 0, row, jnp.zeros_like(row))

    result = first_layer(tile, range(count - 1), packed, bias[...])
    for n in range(count - 1):
        for j in range(2):
            row = result[n * columns : (n + 1) * columns, j * width : (j + 1) * width]
            inside = known | (core != j)
            if n < 2:
                inside = inside & (slab > 0)
            hidden[n, over + j] = jnp.where(inside, row, jnp.zeros_like(row))
    for j in range(half):
        hidden[count - 1, over + j] = started[count - 1, over + j]
    portion = given.shape[3]
    results = given.shape[0]
    for row, value in zip((core, 1 - core), second_layer(hidden, over, 1 - core, second)):
        total = silu(value + partial[row] + bias_second[...]).astype(jnp.bfloat16)
        total = total.reshape(results, columns, 2 * portion)
        low, high = total[..., :portion], total[..., portion:]
        kept[:, row] = jnp.where(core == 0, low, high)
        given[:, row] = jnp.where(core == 0, high, low)


def cycle(value, axis):
    count = lax.axis_size(axis)
    return lax.ppermute(value, axis, [(i, (i + 1) % count) for i in range(count)])


def across_border(value):
    clips, tiles = lax.axis_size("clip"), lax.axis_size("tile")
    pairs = []
    for clip in range(clips):
        at = lambda c, t, k: (c * tiles + t) * 2 + k
        for tile in range(tiles - 1):
            pairs.append((at(clip, tile, 1), at(clip, tile + 1, 0)))
            pairs.append((at(clip, tile + 1, 0), at(clip, tile, 1)))
        if clips > 1:
            pairs.append((at(clip, 0, 0), at((clip + 1) % clips, 0, 0)))
            pairs.append((at(clip, tiles - 1, 1), at((clip + 1) % clips, tiles - 1, 1)))
    return lax.ppermute(value, ("clip", "tile", "chan"), pairs)


def shards(video, first_weight, first_bias, second_weight, second_bias):
    frames, rows, columns, width = video.shape
    half = rows // 2
    taps = first_weight.shape[0]
    assert half == taps - 1 and frames == 2 * (taps - 1) and lax.axis_size("chan") == 2
    bf16 = jnp.bfloat16
    shape = jax.ShapeDtypeStruct
    small = pl.CostEstimate(flops=1000, bytes_accessed=1000, transcendentals=0)

    def call(kernel, outs, ins, scratch, *operands, out_specs=None, limit=LIMIT):
        return pl.pallas_call(
            kernel,
            out_shape=outs,
            in_specs=ins,
            out_specs=[VMEM] * len(outs) if out_specs is None else out_specs,
            scratch_shapes=scratch,
            compiler_params=pltpu.CompilerParams(vmem_limit_bytes=limit),
            cost_estimate=small,
        )(*operands)

    tall = shape((frames, half, columns, width), bf16)
    turned = jnp.swapaxes(first_weight, 3, 4).reshape(-1, width)
    near = lambda value: pltpu.with_memory_space_constraint(value, pltpu.HBM)
    own, rest, staged = call(
        stage_kernel,
        [
            pltpu.VMEM(tall.shape, bf16),
            pltpu.VMEM(tall.shape, bf16),
            pltpu.VMEM((turned.shape[0] + TAIL, width), bf16),
        ],
        [HBM] * 4,
        [
            pltpu.VMEM((1, first_bias.shape[0]), jnp.float32),
            pltpu.VMEM((1, second_bias.shape[0]), jnp.float32),
            pltpu.SemaphoreType.DMA((5,)),
        ],
        near(video), near(turned), near(first_bias.reshape(1, -1)), near(second_bias.reshape(1, -1)),
    )
    passed = cycle(own, "slab")
    beyond = across_border(own)
    staged_other = cycle(staged, "chan")
    matrix = shape((taps * (taps + 1) * width, taps * 2 * width), bf16)
    packed, packed_outer, bias_first, bias_last = call(
        pack_kernel,
        [matrix, matrix, shape((1, 2 * width), jnp.float32), shape((1, second_weight.shape[4]), jnp.float32)],
        [VMEM] * 2,
        [],
        staged, staged_other,
    )
    passed_beyond = across_border(passed)
    passed_other = cycle(passed, "chan")
    count = frames + 1
    started, partial = call(
        inner_kernel,
        [
            shape((count, rows, columns, width), bf16),
            shape((half, frames // 2 * columns, second_weight.shape[4]), jnp.float32),
        ],
        [VMEM] * 9,
        [],
        own, rest, beyond, passed, passed_other, packed, packed_outer, bias_first, second_weight,
    )
    part = shape((frames // 2, half, columns, second_bias.shape[0]), bf16)
    kept, given = call(
        outer_kernel,
        [part, part],
        [VMEM] * 10,
        [pltpu.VMEM((count, rows, columns, width), bf16)],
        own, beyond, passed, passed_beyond, started, partial, packed_outer, second_weight, bias_first, bias_last,
    )
    taken = cycle(given, "chan")
    (latents,) = call(
        join_kernel,
        [shape((frames // 2, rows, columns, second_bias.shape[0]), bf16)],
        [VMEM] * 2,
        [pltpu.SemaphoreType.DMA((2,))],
        kept, taken,
        out_specs=[ANY],
    )
    return latents


def solution(mesh):
    placed = (
        P(("clip", "slab"), "tile", None, None),
        P(None, None, None, None, "chan"),
        P("chan"),
        P(),
        P("chan"),
    )
    return jax.shard_map(
        shards,
        mesh=mesh,
        in_specs=placed,
        out_specs=P(("clip", "slab"), "tile", None, "chan"),
        check_vma=False,
    )
```

time: 62.7 us -> 22.2 us (0.35)
  waiting for transfers between devices: 21.9 us -> 7.16 us
  starting transfers between devices: 18.8 us -> 6.47 us
  matrix products: 10.2 us -> 0 us
  Pallas kernels: 0 us -> 8.35 us
  local copies, waits for them, and re-layouts: 5.66 us -> 0.01 us
  other arithmetic: 3.07 us -> 0 us
  blocking collectives: 2.31 us -> 0 us
    ppermute x6, waiting for transfers between devices: 21.9 us -> 7.16 us  [the longest x4 6.02 us: cycle(): lax.ppermute(value, axis, [(i, (i + 1) % count) for i in range(count)])]
    ppermute x6, starting transfers between devices: 18.8 us -> 6.47 us  [the longest x2 3.29 us: across_border(): return lax.ppermute(value, ('clip', 'tile', 'chan'), pairs)]
    dot_general x18 -> x0, matrix products: 10.2 us -> none  [convolve(): jnp.einsum('fhwc,cd->fhwd', window, matrix, preferred_element_type=jnp.fl...]
    pallas_call x0 -> x5, Pallas kernels: none -> 8.35 us  [call(): pl.pallas_call(kernel, out_shape=outs, in_specs=ins, out_specs=[VMEM] * l...]
    slice x17 -> x0, local copies, waits for them, and re-layouts: 3.97 us -> none  [the longest x11 1.62 us: convolve(): kernel[offset_time, offset_row]]
    concatenate x4 -> x0, other arithmetic: 3.07 us -> none  [the longest x2 2.07 us: padded_2(): block = jnp.concatenate([low, block, high], axis=dim)]
    all_gather x1 -> x0, blocking collectives: 2.31 us -> none  [shards(): complete = lax.all_gather(hidden, 'chan', axis=3, tiled=True)]
    concatenate x2 -> x0, local copies, waits for them, and re-layouts: 1.19 us -> none  [the longest x1 1.12 us: shards(): extended = padded_2(jnp.concatenate([cached, video], 0), (('tile', 1),), 1)]
  transfers between devices with their start and end apart: 6 -> 6, of which waited for: 5 -> 3; matrix products, arithmetic and copies ran while one was open for 3% -> 0% of each run, Pallas kernels for 0% -> 16%
where the time goes in v2:
time: 22.2 us; the launch traced here: 22 us
  Pallas kernels  8.35 us (38%)
  waiting for transfers between devices  7.16 us (32%)
  starting transfers between devices  6.47 us (29%)
    pallas_call x5, Pallas kernels, call(): pl.pallas_call(kernel, out_shape=outs, in_specs=ins, out_specs=[VMEM] * l...  8.35 us
    ppermute x4, waiting for transfers between devices, cycle(): lax.ppermute(value, axis, [(i, (i + 1) % count) for i in range(count)])  6.02 us
    ppermute x2, starting transfers between devices, across_border(): return lax.ppermute(value, ('clip', 'tile', 'chan'), pairs)  3.29 us
    ppermute x4, starting transfers between devices, cycle(): lax.ppermute(value, axis, [(i, (i + 1) % count) for i in range(count)])  3.19 us
    ppermute x2, waiting for transfers between devices, across_border(): return lax.ppermute(value, ('clip', 'tile', 'chan'), pairs)  1.13 us
  transfers between devices with their start and end apart: 6, of which 3 were waited for; matrix products, arithmetic and copies ran while one was open for 0% of the time, Pallas kernels for 16%

profile of v2, /device:TPU:0, one launch (start us, length us, event | category | flops | bytes accessed | tf_op | source)
XLA Modules:
  0.0 22.0 jit_solution(10276904044873798057)
XLA Ops:
  0.0 0.0 copy-start
  0.0 1.3 %shard_map.55 = (bf16[4,2,128,128]{3,2,1,0:T(8,128)(2,1)S(1)}, bf16[4,2,128,128]{3,2,1,0:T(8,128)(2,1)S(1)}, bf16[1744,128]{1,0:T(8,128)(2,1)S(1)}) custom-call(bf16[4,4,128,128]{3,2,1,0:T(8,128)(2,1)} %video.1, bf16[1728,128]{1,0:T(8,128)(2,1)} %bitcast.5, f32[1,64]{1,0:T(1,128)} %bitcast.6, f32[1,128]{1,0:T(1,128)} %bitcast.7), custom_call_target="tpu_custom_call" | custom-call | flops 1000 | bytes 1000 | tf_op jit(solution)/shard_map/pallas_call | solution.py:268
  1.4 3.0 %collective-permute-start.1 = (bf16[4,2,128,128]{3,2,1,0:T(8,128)(2,1)S(1)}, bf16[4,2,128,128]{3,2,1,0:T(8,128)(2,1)S(1)}, u32[]{:S(2)}, u32[]{:S(2)}) collective-permute-start(bf16[4,2,128,128]{3,2,1,0:T(8,128)(2,1)S(1)} %get-tuple-element.16.own), channel_id=1, source_target_pairs={{0,2},{2,0},{1,3},{3,1},{4,6},{6,4},{5,7},{7,5},{8,10},{10,8},{9,1... | collective-permute-start | bytes 786440 | tf_op jit(solution)/shard_map/ppermute | solution.py:241
  4.4 0.0 collective-permute-start.4
  4.4 1.5 %collective-permute-start = (bf16[4,2,128,128]{3,2,1,0:T(8,128)(2,1)S(1)}, bf16[4,2,128,128]{3,2,1,0:T(8,128)(2,1)S(1)}, u32[]{:S(2)}, u32[]{:S(2)}) collective-permute-start(bf16[4,2,128,128]{3,2,1,0:T(8,128)(2,1)S(1)} %get-tuple-element.16.own), channel_id=1, source_target_pairs={{1,4},{4,1},{5,8},{8,5},{9,12},{12,9},{0,16},{13,29},{17,20},{20,1... | collective-permute-start | bytes 786440 | tf_op jit(solution)/shard_map/ppermute | solution.py:255
  5.9 4.8 %collective-permute-done.1.passed = bf16[4,2,128,128]{3,2,1,0:T(8,128)(2,1)S(1)} collective-permute-done((bf16[4,2,128,128]{3,2,1,0:T(8,128)(2,1)S(1)}, bf16[4,2,128,128]{3,2,1,0:T(8,128)(2,1)S(1)}, u32[]{:S(2)}, u32[]{:S(2)}) %collective-permute-start.1) | collective-permute-done | bytes 262176 | tf_op jit(solution)/shard_map/ppermute | solution.py:241
  10.7 0.0 collective-permute-start.3
  10.7 1.8 %collective-permute-start.2 = (bf16[4,2,128,128]{3,2,1,0:T(8,128)(2,1)S(1)}, bf16[4,2,128,128]{3,2,1,0:T(8,128)(2,1)S(1)}, u32[]{:S(2)}, u32[]{:S(2)}) collective-permute-start(bf16[4,2,128,128]{3,2,1,0:T(8,128)(2,1)S(1)} %collective-permute-done.1.passed), channel_id=1, source_target_pairs={{1,4},{4,1},{5,8},{8,5},{9,12},{12,9},{0,16},{13,29},{17,20},{20,1... | collective-permute-start | bytes 786440 | tf_op jit(solution)/shard_map/ppermute | solution.py:255
  12.4 0.0 collective-permute-done.4.other
  12.4 0.4 %shard_map.56 = (bf16[1536,768]{1,0:T(8,128)(2,1)S(1)}, bf16[1536,768]{1,0:T(8,128)(2,1)S(1)}, f32[1,256]{1,0:T(1,128)S(1)}, f32[1,256]{1,0:T(1,128)S(1)}) custom-call(bf16[1744,128]{1,0:T(8,128)(2,1)S(1)} %get-tuple-element.18.own, bf16[1744,128]{1,0:T(8,128)(2,1)S(1)} %collective-permute-done.4.other), custom_call_target="tpu_custom_call" | custom-call | flops 1000 | bytes 1000 | tf_op jit(solution)/shard_map/pallas_call | solution.py:268
  12.8 0.0 collective-permute-done.beyond
  12.8 0.0 collective-permute-done.3.passed_other
  12.9 0.0 copy-done
  12.9 3.0 %shard_map.57 = (bf16[5,4,128,128]{3,2,1,0:T(8,128)(2,1)S(1)}, f32[2,256,256]{2,1,0:T(8,128)S(1)}) custom-call(bf16[4,2,128,128]{3,2,1,0:T(8,128)(2,1)S(1)} %get-tuple-element.16.own, bf16[4,2,128,128]{3,2,1,0:T(8,128)(2,1)S(1)} %get-tuple-element.17.rest, bf16[4,2,128,128]{3,2,1,0:T(8,128)(2,1)S(1)} %collective-permute-done.beyond, ...), custom_call_target="tpu_custom_call" | custom-call | flops 1000 | bytes 1000 | tf_op jit(solution)/shard_map/pallas_call | solution.py:268
  15.9 1.1 %collective-permute-done.2.passed_beyond = bf16[4,2,128,128]{3,2,1,0:T(8,128)(2,1)S(1)} collective-permute-done((bf16[4,2,128,128]{3,2,1,0:T(8,128)(2,1)S(1)}, bf16[4,2,128,128]{3,2,1,0:T(8,128)(2,1)S(1)}, u32[]{:S(2)}, u32[]{:S(2)}) %collective-permute-start.2) | collective-permute-done | bytes 262176 | tf_op jit(solution)/shard_map/ppermute | solution.py:255
  17.0 2.9 %shard_map.58 = (bf16[2,2,128,128]{3,2,1,0:T(8,128)(2,1)S(1)}, bf16[2,2,128,128]{3,2,1,0:T(8,128)(2,1)S(1)}) custom-call(bf16[4,2,128,128]{3,2,1,0:T(8,128)(2,1)S(1)} %get-tuple-element.16.own, bf16[4,2,128,128]{3,2,1,0:T(8,128)(2,1)S(1)} %collective-permute-done.beyond, bf16[4,2,128,128]{3,2,1,0:T(8,128)(2,1)S(1)} %collective-permute-done.1.passed, ...), custom_call_target="tpu_custom_call" | custom-call | flops 1000 | bytes 1000 | tf_op jit(solution)/shard_map/pallas_call | solution.py:268
  19.9 0.2 collective-permute-start.5
  20.1 1.2 %collective-permute-done.5.taken = bf16[2,2,128,128]{3,2,1,0:T(8,128)(2,1)S(1)} collective-permute-done((bf16[2,2,128,128]{3,2,1,0:T(8,128)(2,1)S(1)}, bf16[2,2,128,128]{3,2,1,0:T(8,128)(2,1)S(1)}, u32[]{:S(2)}, u32[]{:S(2)}) %collective-permute-start.5) | collective-permute-done | bytes 131104 | tf_op jit(solution)/shard_map/ppermute | solution.py:241
  21.3 0.7 %shard_map.59 = bf16[2,4,128,128]{3,2,1,0:T(8,128)(2,1)} custom-call(bf16[2,2,128,128]{3,2,1,0:T(8,128)(2,1)S(1)} %get-tuple-element.25.kept, bf16[2,2,128,128]{3,2,1,0:T(8,128)(2,1)S(1)} %collective-permute-done.5.taken), custom_call_target="tpu_custom_call" | custom-call | flops 1000 | bytes 1000 | tf_op jit(solution)/shard_map/pallas_call | solution.py:268
Async XLA Ops:
  0.0 12.9 %copy-start = (bf16[3,3,3,128,256]{4,3,2,1,0:T(8,128)(2,1)S(1)}, bf16[3,3,3,128,256]{4,3,2,1,0:T(8,128)(2,1)}, u32[]{:S(2)}) copy-start(bf16[3,3,3,128,256]{4,3,2,1,0:T(8,128)(2,1)} %second.3) | copy-start | bytes 5308420
  1.4 9.3 %collective-permute-start.1 = (bf16[4,2,128,128]{3,2,1,0:T(8,128)(2,1)S(1)}, bf16[4,2,128,128]{3,2,1,0:T(8,128)(2,1)S(1)}, u32[]{:S(2)}, u32[]{:S(2)}) collective-permute-start(bf16[4,2,128,128]{3,2,1,0:T(8,128)(2,1)S(1)} %get-tuple-element.16.own), channel_id=1, source_target_pairs={{0,2},{2,0},{1,3},{3,1},{4,6},{6,4},{5,7},{7,5},{8,10},{10,8},{9,1... | collective-permute-start | bytes 786440 | tf_op jit(solution)/shard_map/ppermute | solution.py:241
  4.4 8.1 %collective-permute-start.4 = (bf16[1744,128]{1,0:T(8,128)(2,1)S(1)}, bf16[1744,128]{1,0:T(8,128)(2,1)S(1)}, u32[]{:S(2)}, u32[]{:S(2)}) collective-permute-start(bf16[1744,128]{1,0:T(8,128)(2,1)S(1)} %get-tuple-element.18.own), channel_id=1, source_target_pairs={{0,1},{1,0},{2,3},{3,2},{4,5},{5,4},{6,7},{7,6},{8,9},{9,8},{10,11... | collective-permute-start | bytes 1339400 | tf_op jit(solution)/shard_map/ppermute | solution.py:241
  4.4 8.5 %collective-permute-start = (bf16[4,2,128,128]{3,2,1,0:T(8,128)(2,1)S(1)}, bf16[4,2,128,128]{3,2,1,0:T(8,128)(2,1)S(1)}, u32[]{:S(2)}, u32[]{:S(2)}) collective-permute-start(bf16[4,2,128,128]{3,2,1,0:T(8,128)(2,1)S(1)} %get-tuple-element.16.own), channel_id=1, source_target_pairs={{1,4},{4,1},{5,8},{8,5},{9,12},{12,9},{0,16},{13,29},{17,20},{20,1... | collective-permute-start | bytes 786440 | tf_op jit(solution)/shard_map/ppermute | solution.py:255
  10.7 2.2 %collective-permute-start.3 = (bf16[4,2,128,128]{3,2,1,0:T(8,128)(2,1)S(1)}, bf16[4,2,128,128]{3,2,1,0:T(8,128)(2,1)S(1)}, u32[]{:S(2)}, u32[]{:S(2)}) collective-permute-start(bf16[4,2,128,128]{3,2,1,0:T(8,128)(2,1)S(1)} %collective-permute-done.1.passed), channel_id=1, source_target_pairs={{0,1},{1,0},{2,3},{3,2},{4,5},{5,4},{6,7},{7,6},{8,9},{9,8},{10,11... | collective-permute-start | bytes 786440 | tf_op jit(solution)/shard_map/ppermute | solution.py:241
  10.7 6.4 %collective-permute-start.2 = (bf16[4,2,128,128]{3,2,1,0:T(8,128)(2,1)S(1)}, bf16[4,2,128,128]{3,2,1,0:T(8,128)(2,1)S(1)}, u32[]{:S(2)}, u32[]{:S(2)}) collective-permute-start(bf16[4,2,128,128]{3,2,1,0:T(8,128)(2,1)S(1)} %collective-permute-done.1.passed), channel_id=1, source_target_pairs={{1,4},{4,1},{5,8},{8,5},{9,12},{12,9},{0,16},{13,29},{17,20},{20,1... | collective-permute-start | bytes 786440 | tf_op jit(solution)/shard_map/ppermute | solution.py:255
  19.9 1.4 %collective-permute-start.5 = (bf16[2,2,128,128]{3,2,1,0:T(8,128)(2,1)S(1)}, bf16[2,2,128,128]{3,2,1,0:T(8,128)(2,1)S(1)}, u32[]{:S(2)}, u32[]{:S(2)}) collective-permute-start(bf16[2,2,128,128]{3,2,1,0:T(8,128)(2,1)S(1)} %get-tuple-element.26), channel_id=1, source_target_pairs={{0,1},{1,0},{2,3},{3,2},{4,5},{5,4},{6,7},{7,6},{8,9},{9,8},{10,11... | collective-permute-start | bytes 393224 | tf_op jit(solution)/shard_map/ppermute | solution.py:241

commit v3 on v2

v3 whole, which is shorter than its diff:
```python
import functools

import jax
import jax.numpy as jnp
from jax import lax
from jax.experimental import pallas as pl
from jax.experimental.pallas import tpu as pltpu
from jax.sharding import PartitionSpec as P

VMEM = pl.BlockSpec(memory_space=pltpu.VMEM)
ANY = pl.BlockSpec(memory_space=pl.ANY)
HBM = pl.BlockSpec(memory_space=pltpu.HBM)
LIMIT = 20 * 1024 * 1024
TAIL = 16


def silu(value):
    half = 0.5 * value
    return half + half * jnp.tanh(half)


def shifted_sum(parts, columns):
    size, width = parts[0].shape
    before, here, after = (part.reshape(size // columns, columns, width) for part in parts)
    cell = lax.broadcasted_iota(jnp.int32, (1, columns, width), 1)
    before = jnp.where(cell == 0, 0.0, pltpu.roll(before, 1, 1))
    after = jnp.where(cell == columns - 1, 0.0, pltpu.roll(after, columns - 1, 1))
    return (here + before + after).reshape(size, width)


def border_known():
    core, tile = lax.axis_index("chan"), lax.axis_index("tile")
    last = lax.axis_size("tile") - 1
    return jnp.logical_not(jnp.logical_or((core == 0) & (tile == 0), (core == 1) & (tile == last)))


def thirds(value):
    high = value.astype(jnp.bfloat16)
    left = value - high.astype(jnp.float32)
    middle = left.astype(jnp.bfloat16)
    return [high, middle, (left - middle.astype(jnp.float32)).astype(jnp.bfloat16)]


def stage_kernel(video, weight, first_bias, second_bias, own, late, rest, staged, first_line, second_line, sems):
    core = lax.axis_index("chan")
    half = own.shape[1]
    size = weight.shape[0]
    pairs = (
        (video.at[:, pl.ds(core * half, half)], own),
        (video.at[video.shape[0] - late.shape[0] :, pl.ds(core * half, half)], late),
        (video.at[:, pl.ds((1 - core) * half, half)], rest),
        (weight, staged.at[0:size]),
        (first_bias, first_line),
        (second_bias, second_line),
    )
    copies = [pltpu.make_async_copy(source, target, sems.at[k]) for k, (source, target) in enumerate(pairs)]
    for copy in copies:
        copy.start()
    for copy in copies[4:]:
        copy.wait()
    width = staged.shape[1]
    first = first_line[...]
    first = jnp.concatenate([first, jnp.zeros((1, width - first.shape[1]), first.dtype)], axis=1)
    rows = thirds(first) + thirds(second_line[...])
    rows.append(jnp.zeros((TAIL - len(rows), width), jnp.bfloat16))
    staged[size:] = jnp.concatenate(rows, axis=0)
    for copy in copies[:4]:
        copy.wait()


def join_kernel(*refs):
    frames = len(refs) // 2 - 1
    latents, sems = refs[2 * frames :]
    core = lax.axis_index("chan")
    half = refs[0].shape[0]
    copies = []
    for t in range(frames):
        for k, place in enumerate((core, 1 - core)):
            target = latents.at[t, pl.ds(place * half, half)]
            copies.append(pltpu.make_async_copy(refs[2 * t + k], target, sems.at[2 * t + k]))
    for copy in copies:
        copy.start()
    for copy in copies:
        copy.wait()


def pack_kernel(own, other, inner, outer, bias_first, bias_second):
    core = lax.axis_index("chan")
    known = border_known()
    taps = 3
    rows = taps + 1
    width = own.shape[1]
    size = own.shape[0] - TAIL
    channels = size // taps**3

    def lines(source):
        last = source[size:].astype(jnp.float32)
        added = [last[3 * k : 3 * k + 1] + last[3 * k + 1 : 3 * k + 2] + last[3 * k + 2 : 3 * k + 3] for k in range(2)]
        return added[0][:, :channels], added[1]

    mine, theirs = lines(own), lines(other)
    low = [jnp.where(core == 0, m, t) for m, t in zip(mine, theirs)]
    high = [jnp.where(core == 0, t, m) for m, t in zip(mine, theirs)]
    once = jnp.concatenate([low[0], high[0]], axis=1)
    bias_first[...] = jnp.concatenate([once, once], axis=1)
    bias_second[...] = jnp.concatenate([low[1], high[1]], axis=1)
    for a in range(taps):
        for e in range(taps):
            full = []
            for b in range(taps):
                at = ((a * taps + b) * taps + e) * channels
                mine, theirs = own[at : at + channels], other[at : at + channels]
                low = jnp.where(core == 0, mine, theirs)
                high = jnp.where(core == 0, theirs, mine)
                full.append(jnp.concatenate([low, high], axis=0).T)
            nothing = jnp.zeros_like(full[0])
            across = slice(e * 2 * width, (e + 1) * 2 * width)
            for i in range(rows):
                pair = [full[i - j] if 0 <= i - j < taps else nothing for j in range(2)]
                pair = jnp.concatenate(pair, axis=1)
                upper = i < rows // 2
                at = lax.rem(i + 2 * core, rows) + a * rows
                inner[pl.ds(pl.multiple_of(at * width, width), width), across] = pair
                at = lax.rem(i + 2 * (1 - core), rows) + a * rows
                used = known | (core == (1 if upper else 0))
                outer[pl.ds(pl.multiple_of(at * width, width), width), across] = jnp.where(
                    used, pair, jnp.zeros_like(pair)
                )


def first_layer(tile, frames, packed, bias):
    taps = 3
    rows = taps + 1
    left = jnp.concatenate(
        [
            jnp.concatenate([tile(f + a, k) for f in frames], axis=0)
            for a in range(taps)
            for k in range(rows)
        ],
        axis=1,
    )
    double = packed.shape[1] // taps
    columns = left.shape[0] // len(frames)
    parts = [
        jnp.dot(left, packed[:, e * double : (e + 1) * double], preferred_element_type=jnp.float32)
        for e in range(taps)
    ]
    return silu(shifted_sum(parts, columns) + bias).astype(jnp.bfloat16)


def second_layer(tile, frames, late, second):
    def added(rows):
        left = jnp.concatenate(
            [jnp.concatenate([tile(n, j) for n in frames[a]], axis=0) for a in frames for j, _ in rows], axis=1
        )
        parts = [
            jnp.dot(
                left,
                jnp.concatenate([second[a, b, e] for a in frames for _, b in rows], axis=0),
                preferred_element_type=jnp.float32,
            )
            for e in range(second.shape[2])
        ]
        return shifted_sum(parts, tile(frames[next(iter(frames))][0], 0).shape[0])

    return (1 - late, added([(0, 1 - late), (1, 2 - late)])), (late, added([(late, 2 * (1 - late))]))


def put_rows(result, target, start, columns, masks):
    width = target.shape[-1]
    for n in range(result.shape[0] // columns):
        for j in range(2):
            row = result[n * columns : (n + 1) * columns, j * width : (j + 1) * width]
            target[start + n, j] = row if masks is None else jnp.where(masks[j], row, jnp.zeros_like(row))


def border_masks():
    core, known = lax.axis_index("chan"), border_known()
    return [known | (core != j) for j in range(2)]


def ahead_kernel(own, beside, packed, bias, hidden, *, border):
    half, columns = own.shape[1:3]

    def tile(f, k):
        return own[f, k] if k < half else beside[f, k - half]

    result = first_layer(tile, range(hidden.shape[0]), packed, bias[...])
    put_rows(result, hidden, 0, columns, border_masks() if border else None)


def behind(own, beside, passed, passed_beside, packed, bias, hidden, start, masks):
    early, half, columns = passed.shape[:3]
    follows = lax.axis_index("slab") > 0

    def tile(f, k):
        if f >= early:
            return own[f - early, k] if k < half else beside[f - early, k - half]
        row = passed[f, k] if k < half else passed_beside[f, k - half]
        return jnp.where(follows, row, jnp.zeros_like(row))

    put_rows(first_layer(tile, range(early), packed, bias[...]), hidden, start, columns, masks)


def inner_kernel(own, rest, passed, passed_other, packed, bias, ahead, second, partial, hidden):
    early, _, columns = passed.shape[:3]
    behind(own, rest, passed, passed_other, packed, bias, hidden, 0, None)
    hidden[early] = ahead[0]
    add_layers(hidden, lax.axis_index("chan"), second, partial, None)


def add_layers(hidden, late, second, target, base):
    columns = hidden.shape[2]
    tile = lambda n, j: hidden[n, j]
    ends = second_layer(tile, {2: [0, 2]}, late, second)
    starts = second_layer(tile, {0: [0], 1: [1]}, late, second)
    for (row, end), (_, start) in zip(ends, starts):
        first, later = end[:columns], end[columns:] + start
        if base is not None:
            first, later = first + base[row, :columns], later + base[row, columns:]
        target[row, :columns] = first
        target[row, columns:] = later


def from_earlier(handed):
    follows = lax.axis_index("slab") > 0

    def tile(n, j):
        row = handed[n, j]
        return jnp.where(follows, row, jnp.zeros_like(row))

    return tile


def finish(value, bias, row, kept, given):
    core = lax.axis_index("chan")
    total = silu(value + bias[...]).astype(jnp.bfloat16)
    portion = kept.shape[-1]
    low, high = total[:, :portion], total[:, portion:]
    kept[row] = jnp.where(core == 0, low, high)
    given[row] = jnp.where(core == 0, high, low)


def outer_kernel(
    handed, own, beyond, passed, packed, bias, ahead, second, bias_second, partial, passed_beyond,
    kept, given, left, hidden, total,
):
    core = lax.axis_index("chan")
    early, _, columns = passed.shape[:3]
    behind(own, beyond, passed, passed_beyond, packed, bias, hidden, 0, border_masks())
    hidden[early] = ahead[0]
    add_layers(hidden, 1 - core, second, total, partial)
    for row, value in second_layer(from_earlier(handed), {0: [0], 1: [1]}, core, second):
        left[row] = total[row, :columns] + value
    for row in range(total.shape[0]):
        finish(total[row, columns:], bias_second, row, kept, given)


def last_kernel(handed, second, bias_second, left, kept, given):
    for row, value in second_layer(from_earlier(handed), {0: [0], 1: [1]}, 1 - lax.axis_index("chan"), second):
        finish(left[row] + value, bias_second, row, kept, given)


def cycle(value, axis):
    count = lax.axis_size(axis)
    return lax.ppermute(value, axis, [(i, (i + 1) % count) for i in range(count)])


def across_border(value):
    clips, tiles = lax.axis_size("clip"), lax.axis_size("tile")
    pairs = []
    for clip in range(clips):
        at = lambda c, t, k: (c * tiles + t) * 2 + k
        for tile in range(tiles - 1):
            pairs.append((at(clip, tile, 1), at(clip, tile + 1, 0)))
            pairs.append((at(clip, tile + 1, 0), at(clip, tile, 1)))
        if clips > 1:
            pairs.append((at(clip, 0, 0), at((clip + 1) % clips, 0, 0)))
            pairs.append((at(clip, tiles - 1, 1), at((clip + 1) % clips, tiles - 1, 1)))
    return lax.ppermute(value, ("clip", "tile", "chan"), pairs)


def shards(video, first_weight, first_bias, second_weight, second_bias):
    frames, rows, columns, width = video.shape
    half = rows // 2
    taps = first_weight.shape[0]
    assert half == taps - 1 and frames == 2 * (taps - 1) and lax.axis_size("chan") == 2
    bf16 = jnp.bfloat16
    shape = jax.ShapeDtypeStruct
    small = pl.CostEstimate(flops=1000, bytes_accessed=1000, transcendentals=0)

    def call(kernel, outs, ins, scratch, *operands, out_specs=None, limit=LIMIT):
        return pl.pallas_call(
            kernel,
            out_shape=outs,
            in_specs=ins,
            out_specs=[VMEM] * len(outs) if out_specs is None else out_specs,
            scratch_shapes=scratch,
            compiler_params=pltpu.CompilerParams(vmem_limit_bytes=limit),
            cost_estimate=small,
        )(*operands)

    early = frames // 2
    tall, short = (shape((count, half, columns, width), bf16) for count in (frames, early))
    turned = jnp.swapaxes(first_weight, 3, 4).reshape(-1, width)
    far = lambda value: pltpu.with_memory_space_constraint(value, pltpu.HBM)
    own, late, rest, staged = call(
        stage_kernel,
        [
            pltpu.VMEM(tall.shape, bf16),
            pltpu.VMEM(short.shape, bf16),
            pltpu.VMEM(tall.shape, bf16),
            pltpu.VMEM((turned.shape[0] + TAIL, width), bf16),
        ],
        [HBM] * 4,
        [
            pltpu.VMEM((1, first_bias.shape[0]), jnp.float32),
            pltpu.VMEM((1, second_bias.shape[0]), jnp.float32),
            pltpu.SemaphoreType.DMA((6,)),
        ],
        far(video), far(turned), far(first_bias.reshape(1, -1)), far(second_bias.reshape(1, -1)),
    )
    beyond = across_border(own)
    passed = cycle(late, "slab")
    staged_other = cycle(staged, "chan")
    matrix = shape((taps * (taps + 1) * width, taps * 2 * width), bf16)
    channels = second_weight.shape[4]
    packed, packed_outer, bias_first, bias_last = call(
        pack_kernel,
        [matrix, matrix, shape((1, 2 * width), jnp.float32), shape((1, channels), jnp.float32)],
        [VMEM] * 2,
        [],
        staged, staged_other,
    )
    (ahead_inner,) = call(
        functools.partial(ahead_kernel, border=False), [short], [VMEM] * 4, [], own, rest, packed, bias_first
    )
    handed_inner = cycle(ahead_inner, "slab")
    passed, _ = lax.optimization_barrier((passed, ahead_inner))
    passed_beyond = across_border(passed)
    passed_other = cycle(passed, "chan")
    beyond, passed_other = lax.optimization_barrier((beyond, passed_other))
    (ahead_outer,) = call(
        functools.partial(ahead_kernel, border=True), [short], [VMEM] * 4, [], own, beyond, packed_outer, bias_first
    )
    handed_outer = cycle(ahead_outer, "slab")
    (partial,) = call(
        inner_kernel,
        [shape((half, early * columns, channels), jnp.float32)],
        [VMEM] * 8,
        [pltpu.VMEM((early + 1, half, columns, width), bf16)],
        own, rest, passed, passed_other, packed, bias_first, ahead_inner, second_weight,
    )
    part = shape((half, columns, second_bias.shape[0]), bf16)
    handed_inner, partial = lax.optimization_barrier((handed_inner, partial))
    kept_second, given_second, left = call(
        outer_kernel,
        [part, part, shape((half, columns, channels), jnp.float32)],
        [VMEM] * 11,
        [
            pltpu.VMEM((early + 1, half, columns, width), bf16),
            pltpu.VMEM((half, early * columns, channels), jnp.float32),
        ],
        handed_inner, own, beyond, passed, packed_outer, bias_first, ahead_outer, second_weight,
        bias_last, partial, passed_beyond,
    )
    taken_second = cycle(given_second, "chan")
    kept_first, given_first = call(
        last_kernel, [part, part], [VMEM] * 4, [], handed_outer, second_weight, bias_last, left
    )
    taken_first = cycle(given_first, "chan")
    (latents,) = call(
        join_kernel,
        [shape((early, rows, columns, second_bias.shape[0]), bf16)],
        [VMEM] * 4,
        [pltpu.SemaphoreType.DMA((4,))],
        kept_first, taken_first, kept_second, taken_second,
        out_specs=[ANY],
    )
    return latents


def solution(mesh):
    placed = (
        P(("clip", "slab"), "tile", None, None),
        P(None, None, None, None, "chan"),
        P("chan"),
        P(),
        P("chan"),
    )
    return jax.shard_map(
        shards,
        mesh=mesh,
        in_specs=placed,
        out_specs=P(("clip", "slab"), "tile", None, "chan"),
        check_vma=False,
    )
```

time: 22.2 us -> 20.8 us (0.937)
  waiting for transfers between devices: 7.16 us -> 3.87 us
  starting transfers between devices: 6.47 us -> 8.62 us
  Pallas kernels: 8.35 us -> 8.09 us
    ppermute x4 -> x7, waiting for transfers between devices: 6.02 us -> 3.56 us  [cycle(): lax.ppermute(value, axis, [(i, (i + 1) % count) for i in range(count)])]
    ppermute x4 -> x7, starting transfers between devices: 3.19 us -> 5.58 us  [cycle(): lax.ppermute(value, axis, [(i, (i + 1) % count) for i in range(count)])]
    ppermute x2, waiting for transfers between devices: 1.13 us -> 0.31 us  [across_border(): return lax.ppermute(value, ('clip', 'tile', 'chan'), pairs)]
    pallas_call x5 -> x8, Pallas kernels: 8.35 us -> 8.09 us  [call(): pl.pallas_call(kernel, out_shape=outs, in_specs=ins, out_specs=[VMEM] * l...]
    ppermute x2, starting transfers between devices: 3.29 us -> 3.04 us  [across_border(): return lax.ppermute(value, ('clip', 'tile', 'chan'), pairs)]
  transfers between devices with their start and end apart: 6 -> 9, of which waited for: 3 -> 4; matrix products, arithmetic and copies ran while one was open for 0% -> 0% of each run, Pallas kernels for 16% -> 29%
where the time goes in v3:
time: 20.8 us; the launch traced here: 20.7 us
  starting transfers between devices  8.62 us (41%)
  Pallas kernels  8.09 us (39%)
  waiting for transfers between devices  3.87 us (19%)
    pallas_call x8, Pallas kernels, call(): pl.pallas_call(kernel, out_shape=outs, in_specs=ins, out_specs=[VMEM] * l...  8.09 us
    ppermute x7, starting transfers between devices, cycle(): lax.ppermute(value, axis, [(i, (i + 1) % count) for i in range(count)])  5.58 us
    ppermute x7, waiting for transfers between devices, cycle(): lax.ppermute(value, axis, [(i, (i + 1) % count) for i in range(count)])  3.56 us
    ppermute x2, starting transfers between devices, across_border(): return lax.ppermute(value, ('clip', 'tile', 'chan'), pairs)  3.04 us
  transfers between devices with their start and end apart: 9, of which 4 were waited for; matrix products, arithmetic and copies ran while one was open for 0% of the time, Pallas kernels for 29%

profile of v3, /device:TPU:0, one launch (start us, length us, event | category | flops | bytes accessed | tf_op | source)
XLA Modules:
  0.0 20.7 jit_solution(1886033889897539233)
XLA Ops:
  0.0 1.3 %shard_map.55 = (bf16[4,2,128,128]{3,2,1,0:T(8,128)(2,1)S(1)}, bf16[2,2,128,128]{3,2,1,0:T(8,128)(2,1)S(1)}, bf16[4,2,128,128]{3,2,1,0:T(8,128)(2,1)S(1)}, bf16[1744,128]{1,0:T(8,128)(2,1)S(1)}) custom-call(bf16[4,4,128,128]{3,2,1,0:T(8,128)(2,1)} %video.1, bf16[1728,128]{1,0:T(8,128)(2,1)} %bitcast.5, f32[1,64]{1,0:T(1,128)} %bitcast.6, f32[1,128]{1,0:T(1,128)} %bitcast.7), custom_call_target="tpu_custom_call" | custom-call | flops 1000 | bytes 1000 | tf_op jit(solution)/shard_map/pallas_call | solution.py:293
  1.3 0.5 %collective-permute-start.2 = (bf16[1744,128]{1,0:T(8,128)(2,1)S(1)}, bf16[1744,128]{1,0:T(8,128)(2,1)S(1)}, u32[]{:S(2)}, u32[]{:S(2)}) collective-permute-start(bf16[1744,128]{1,0:T(8,128)(2,1)S(1)} %get-tuple-element.26.own), channel_id=1, source_target_pairs={{0,1},{1,0},{2,3},{3,2},{4,5},{5,4},{6,7},{7,6},{8,9},{9,8},{10,11... | collective-permute-start | bytes 1339400 | tf_op jit(solution)/shard_map/ppermute | solution.py:266
  1.8 2.6 %collective-permute-start.1 = (bf16[2,2,128,128]{3,2,1,0:T(8,128)(2,1)S(1)}, bf16[2,2,128,128]{3,2,1,0:T(8,128)(2,1)S(1)}, u32[]{:S(2)}, u32[]{:S(2)}) collective-permute-start(bf16[2,2,128,128]{3,2,1,0:T(8,128)(2,1)S(1)} %get-tuple-element.24), channel_id=1, source_target_pairs={{0,2},{2,0},{1,3},{3,1},{4,6},{6,4},{5,7},{7,5},{8,10},{10,8},{9,1... | collective-permute-start | bytes 393224 | tf_op jit(solution)/shard_map/ppermute | solution.py:266
  4.4 1.5 %collective-permute-start = (bf16[4,2,128,128]{3,2,1,0:T(8,128)(2,1)S(1)}, bf16[4,2,128,128]{3,2,1,0:T(8,128)(2,1)S(1)}, u32[]{:S(2)}, u32[]{:S(2)}) collective-permute-start(bf16[4,2,128,128]{3,2,1,0:T(8,128)(2,1)S(1)} %get-tuple-element.23.own), channel_id=1, source_target_pairs={{1,4},{4,1},{5,8},{8,5},{9,12},{12,9},{0,16},{13,29},{17,20},{20,1... | collective-permute-start | bytes 786440 | tf_op jit(solution)/shard_map/ppermute | solution.py:280
  5.9 0.0 collective-permute-done.2.other
  5.9 0.4 %shard_map.56 = (bf16[1536,768]{1,0:T(8,128)(2,1)S(1)}, bf16[1536,768]{1,0:T(8,128)(2,1)S(1)}, f32[1,256]{1,0:T(1,128)S(1)}, f32[1,256]{1,0:T(1,128)S(1)}) custom-call(bf16[1744,128]{1,0:T(8,128)(2,1)S(1)} %get-tuple-element.26.own, bf16[1744,128]{1,0:T(8,128)(2,1)S(1)} %collective-permute-done.2.other), custom_call_target="tpu_custom_call" | custom-call | flops 1000 | bytes 1000 | tf_op jit(solution)/shard_map/pallas_call | solution.py:293
  6.3 0.0 copy-start
  6.3 0.8 %shard_map.57.ahead = bf16[2,2,128,128]{3,2,1,0:T(8,128)(2,1)S(1)} custom-call(bf16[4,2,128,128]{3,2,1,0:T(8,128)(2,1)S(1)} %get-tuple-element.23.own, bf16[4,2,128,128]{3,2,1,0:T(8,128)(2,1)S(1)} %get-tuple-element.25.beside.rest, bf16[1536,768]{1,0:T(8,128)(2,1)S(1)} %get-tuple-element.27.packed, f32[1,256]{1,0:T(1,128)S(1)} %get-tuple-element.28.bias), custom_call_target="tpu_custom_call" | custom-call | flops 1000 | bytes 1000 | tf_op jit(solution)/shard_map/pallas_call | solution.py:293
  7.2 1.3 %collective-permute-done.1.passed = bf16[2,2,128,128]{3,2,1,0:T(8,128)(2,1)S(1)} collective-permute-done((bf16[2,2,128,128]{3,2,1,0:T(8,128)(2,1)S(1)}, bf16[2,2,128,128]{3,2,1,0:T(8,128)(2,1)S(1)}, u32[]{:S(2)}, u32[]{:S(2)}) %collective-permute-start.1) | collective-permute-done | bytes 131104 | tf_op jit(solution)/shard_map/ppermute | solution.py:266
  8.5 0.0 collective-permute-start.3
  8.5 1.8 %collective-permute-start.5 = (bf16[2,2,128,128]{3,2,1,0:T(8,128)(2,1)S(1)}, bf16[2,2,128,128]{3,2,1,0:T(8,128)(2,1)S(1)}, u32[]{:S(2)}, u32[]{:S(2)}) collective-permute-start(bf16[2,2,128,128]{3,2,1,0:T(8,128)(2,1)S(1)} %shard_map.57.ahead), channel_id=1, source_target_pairs={{0,2},{2,0},{1,3},{3,1},{4,6},{6,4},{5,7},{7,5},{8,10},{10,8},{9,1... | collective-permute-start | bytes 393224 | tf_op jit(solution)/shard_map/ppermute | solution.py:266
  10.2 1.5 %collective-permute-start.6 = (bf16[2,2,128,128]{3,2,1,0:T(8,128)(2,1)S(1)}, bf16[2,2,128,128]{3,2,1,0:T(8,128)(2,1)S(1)}, u32[]{:S(2)}, u32[]{:S(2)}) collective-permute-start(bf16[2,2,128,128]{3,2,1,0:T(8,128)(2,1)S(1)} %collective-permute-done.1.passed), channel_id=1, source_target_pairs={{1,4},{4,1},{5,8},{8,5},{9,12},{12,9},{0,16},{13,29},{17,20},{20,1... | collective-permute-start | bytes 393224 | tf_op jit(solution)/shard_map/ppermute | solution.py:280
  11.8 0.0 collective-permute-done.beside.beyond
  11.8 0.8 %shard_map.58.ahead = bf16[2,2,128,128]{3,2,1,0:T(8,128)(2,1)S(1)} custom-call(bf16[4,2,128,128]{3,2,1,0:T(8,128)(2,1)S(1)} %get-tuple-element.23.own, bf16[4,2,128,128]{3,2,1,0:T(8,128)(2,1)S(1)} %collective-permute-done.beside.beyond, bf16[1536,768]{1,0:T(8,128)(2,1)S(1)} %get-tuple-element.31.packed, f32[1,256]{1,0:T(1,128)S(1)} %get-tuple-element.28.bias), custom_call_target="tpu_custom_call" | custom-call | flops 1000 | bytes 1000 | tf_op jit(solution)/shard_map/pallas_call | solution.py:293
  12.6 0.6 %collective-permute-start.4 = (bf16[2,2,128,128]{3,2,1,0:T(8,128)(2,1)S(1)}, bf16[2,2,128,128]{3,2,1,0:T(8,128)(2,1)S(1)}, u32[]{:S(2)}, u32[]{:S(2)}) collective-permute-start(bf16[2,2,128,128]{3,2,1,0:T(8,128)(2,1)S(1)} %shard_map.58.ahead), channel_id=1, source_target_pairs={{0,2},{2,0},{1,3},{3,1},{4,6},{6,4},{5,7},{7,5},{8,10},{10,8},{9,1... | collective-permute-start | bytes 393224 | tf_op jit(solution)/shard_map/ppermute | solution.py:266
  13.2 1.7 %shard_map.59.partial = f32[2,256,256]{2,1,0:T(8,128)S(1)} custom-call(bf16[4,2,128,128]{3,2,1,0:T(8,128)(2,1)S(1)} %get-tuple-element.23.own, bf16[4,2,128,128]{3,2,1,0:T(8,128)(2,1)S(1)} %get-tuple-element.25.beside.rest, bf16[2,2,128,128]{3,2,1,0:T(8,128)(2,1)S(1)} %collective-permute-done.1.passed, ...), custom_call_target="tpu_custom_call" | custom-call | flops 1000 | bytes 1000 | tf_op jit(solution)/shard_map/pallas_call | solution.py:293
  14.9 0.3 %collective-permute-done.6.passed_beyond = bf16[2,2,128,128]{3,2,1,0:T(8,128)(2,1)S(1)} collective-permute-done((bf16[2,2,128,128]{3,2,1,0:T(8,128)(2,1)S(1)}, bf16[2,2,128,128]{3,2,1,0:T(8,128)(2,1)S(1)}, u32[]{:S(2)}, u32[]{:S(2)}) %collective-permute-start.6) | collective-permute-done | bytes 131104 | tf_op jit(solution)/shard_map/ppermute | solution.py:280
  15.2 1.9 %shard_map.60 = (bf16[2,128,128]{2,1,0:T(8,128)(2,1)S(1)}, bf16[2,128,128]{2,1,0:T(8,128)(2,1)S(1)}, f32[2,128,256]{2,1,0:T(8,128)S(1)}) custom-call(bf16[2,2,128,128]{3,2,1,0:T(8,128)(2,1)S(1)} %collective-permute-done.5.handed, bf16[4,2,128,128]{3,2,1,0:T(8,128)(2,1)S(1)} %get-tuple-element.23.own, ...), custom_call_target="tpu_custom_call" | custom-call | flops 1000 | bytes 1000 | tf_op jit(solution)/shard_map/pallas_call | solution.py:293
  17.2 0.1 collective-permute-start.8
  17.2 1.0 %collective-permute-done.4.handed = bf16[2,2,128,128]{3,2,1,0:T(8,128)(2,1)S(1)} collective-permute-done((bf16[2,2,128,128]{3,2,1,0:T(8,128)(2,1)S(1)}, bf16[2,2,128,128]{3,2,1,0:T(8,128)(2,1)S(1)}, u32[]{:S(2)}, u32[]{:S(2)}) %collective-permute-start.4) | collective-permute-done | bytes 131104 | tf_op jit(solution)/shard_map/ppermute | solution.py:266
  18.2 0.4 %shard_map.61 = (bf16[2,128,128]{2,1,0:T(8,128)(2,1)S(1)}, bf16[2,128,128]{2,1,0:T(8,128)(2,1)S(1)}) custom-call(bf16[2,2,128,128]{3,2,1,0:T(8,128)(2,1)S(1)} %collective-permute-done.4.handed, bf16[3,3,3,128,256]{4,3,2,1,0:T(8,128)(2,1)S(1)} %copy-done, f32[1,256]{1,0:T(1,128)S(1)} %get-tuple-element.32.bias_second, f32[2,128,256]{2,1,0:T(8,128)S(1)} %get-tuple-element.36.left), custom_call_target="tpu_custom_call" | custom-call | flops 1000 | bytes 1000 | tf_op jit(solution)/shard_map/pallas_call | solution.py:293
  18.6 0.1 collective-permute-start.7
  18.7 1.2 %collective-permute-done.7.refs_1_ = bf16[2,128,128]{2,1,0:T(8,128)(2,1)S(1)} collective-permute-done((bf16[2,128,128]{2,1,0:T(8,128)(2,1)S(1)}, bf16[2,128,128]{2,1,0:T(8,128)(2,1)S(1)}, u32[]{:S(2)}, u32[]{:S(2)}) %collective-permute-start.7) | collective-permute-done | bytes 65568 | tf_op jit(solution)/shard_map/ppermute | solution.py:266
  20.0 0.7 %shard_map.62 = bf16[2,4,128,128]{3,2,1,0:T(8,128)(2,1)} custom-call(bf16[2,128,128]{2,1,0:T(8,128)(2,1)S(1)} %get-tuple-element.37.refs_0_, bf16[2,128,128]{2,1,0:T(8,128)(2,1)S(1)} %collective-permute-done.7.refs_1_, bf16[2,128,128]{2,1,0:T(8,128)(2,1)S(1)} %get-tuple-element.39.refs_2_, bf16[2,128,128]{2,1,0:T(8,128)(2,1)S(1)} %collective-permute-done.8.refs_3_), custom_call_target="tpu_custom_call" | custom-call | flops 1000 | bytes 1000 | tf_op jit(solution)/shard_map/pallas_call | solution.py:293
  (4 shorter events, 0.0 us)
Async XLA Ops:
  1.3 4.6 %collective-permute-start.2 = (bf16[1744,128]{1,0:T(8,128)(2,1)S(1)}, bf16[1744,128]{1,0:T(8,128)(2,1)S(1)}, u32[]{:S(2)}, u32[]{:S(2)}) collective-permute-start(bf16[1744,128]{1,0:T(8,128)(2,1)S(1)} %get-tuple-element.26.own), channel_id=1, source_target_pairs={{0,1},{1,0},{2,3},{3,2},{4,5},{5,4},{6,7},{7,6},{8,9},{9,8},{10,11... | collective-permute-start | bytes 1339400 | tf_op jit(solution)/shard_map/ppermute | solution.py:266
  1.8 6.7 %collective-permute-start.1 = (bf16[2,2,128,128]{3,2,1,0:T(8,128)(2,1)S(1)}, bf16[2,2,128,128]{3,2,1,0:T(8,128)(2,1)S(1)}, u32[]{:S(2)}, u32[]{:S(2)}) collective-permute-start(bf16[2,2,128,128]{3,2,1,0:T(8,128)(2,1)S(1)} %get-tuple-element.24), channel_id=1, source_target_pairs={{0,2},{2,0},{1,3},{3,1},{4,6},{6,4},{5,7},{7,5},{8,10},{10,8},{9,1... | collective-permute-start | bytes 393224 | tf_op jit(solution)/shard_map/ppermute | solution.py:266
  4.4 7.4 %collective-permute-start = (bf16[4,2,128,128]{3,2,1,0:T(8,128)(2,1)S(1)}, bf16[4,2,128,128]{3,2,1,0:T(8,128)(2,1)S(1)}, u32[]{:S(2)}, u32[]{:S(2)}) collective-permute-start(bf16[4,2,128,128]{3,2,1,0:T(8,128)(2,1)S(1)} %get-tuple-element.23.own), channel_id=1, source_target_pairs={{1,4},{4,1},{5,8},{8,5},{9,12},{12,9},{0,16},{13,29},{17,20},{20,1... | collective-permute-start | bytes 786440 | tf_op jit(solution)/shard_map/ppermute | solution.py:280
  6.3 6.9 %copy-start = (bf16[3,3,3,128,256]{4,3,2,1,0:T(8,128)(2,1)S(1)}, bf16[3,3,3,128,256]{4,3,2,1,0:T(8,128)(2,1)}, u32[]{:S(2)}) copy-start(bf16[3,3,3,128,256]{4,3,2,1,0:T(8,128)(2,1)} %second.5) | copy-start | bytes 5308420
  8.5 3.3 %collective-permute-start.3 = (bf16[2,2,128,128]{3,2,1,0:T(8,128)(2,1)S(1)}, bf16[2,2,128,128]{3,2,1,0:T(8,128)(2,1)S(1)}, u32[]{:S(2)}, u32[]{:S(2)}) collective-permute-start(bf16[2,2,128,128]{3,2,1,0:T(8,128)(2,1)S(1)} %collective-permute-done.1.passed), channel_id=1, source_target_pairs={{0,1},{1,0},{2,3},{3,2},{4,5},{5,4},{6,7},{7,6},{8,9},{9,8},{10,11... | collective-permute-start | bytes 393224 | tf_op jit(solution)/shard_map/ppermute | solution.py:266
  8.5 6.4 %collective-permute-start.5 = (bf16[2,2,128,128]{3,2,1,0:T(8,128)(2,1)S(1)}, bf16[2,2,128,128]{3,2,1,0:T(8,128)(2,1)S(1)}, u32[]{:S(2)}, u32[]{:S(2)}) collective-permute-start(bf16[2,2,128,128]{3,2,1,0:T(8,128)(2,1)S(1)} %shard_map.57.ahead), channel_id=1, source_target_pairs={{0,2},{2,0},{1,3},{3,1},{4,6},{6,4},{5,7},{7,5},{8,10},{10,8},{9,1... | collective-permute-start | bytes 393224 | tf_op jit(solution)/shard_map/ppermute | solution.py:266
  10.2 5.0 %collective-permute-start.6 = (bf16[2,2,128,128]{3,2,1,0:T(8,128)(2,1)S(1)}, bf16[2,2,128,128]{3,2,1,0:T(8,128)(2,1)S(1)}, u32[]{:S(2)}, u32[]{:S(2)}) collective-permute-start(bf16[2,2,128,128]{3,2,1,0:T(8,128)(2,1)S(1)} %collective-permute-done.1.passed), channel_id=1, source_target_pairs={{1,4},{4,1},{5,8},{8,5},{9,12},{12,9},{0,16},{13,29},{17,20},{20,1... | collective-permute-start | bytes 393224 | tf_op jit(solution)/shard_map/ppermute | solution.py:280
  12.6 5.6 %collective-permute-start.4 = (bf16[2,2,128,128]{3,2,1,0:T(8,128)(2,1)S(1)}, bf16[2,2,128,128]{3,2,1,0:T(8,128)(2,1)S(1)}, u32[]{:S(2)}, u32[]{:S(2)}) collective-permute-start(bf16[2,2,128,128]{3,2,1,0:T(8,128)(2,1)S(1)} %shard_map.58.ahead), channel_id=1, source_target_pairs={{0,2},{2,0},{1,3},{3,1},{4,6},{6,4},{5,7},{7,5},{8,10},{10,8},{9,1... | collective-permute-start | bytes 393224 | tf_op jit(solution)/shard_map/ppermute | solution.py:266
  17.2 1.6 %collective-permute-start.8 = (bf16[2,128,128]{2,1,0:T(8,128)(2,1)S(1)}, bf16[2,128,128]{2,1,0:T(8,128)(2,1)S(1)}, u32[]{:S(2)}, u32[]{:S(2)}) collective-permute-start(bf16[2,128,128]{2,1,0:T(8,128)(2,1)S(1)} %get-tuple-element.40), channel_id=1, source_target_pairs={{0,1},{1,0},{2,3},{3,2},{4,5},{5,4},{6,7},{7,6},{8,9},{9,8},{10,11... | collective-permute-start | bytes 196616 | tf_op jit(solution)/shard_map/ppermute | solution.py:266
  18.6 1.3 %collective-permute-start.7 = (bf16[2,128,128]{2,1,0:T(8,128)(2,1)S(1)}, bf16[2,128,128]{2,1,0:T(8,128)(2,1)S(1)}, u32[]{:S(2)}, u32[]{:S(2)}) collective-permute-start(bf16[2,128,128]{2,1,0:T(8,128)(2,1)S(1)} %get-tuple-element.38), channel_id=1, source_target_pairs={{0,1},{1,0},{2,3},{3,2},{4,5},{5,4},{6,7},{7,6},{8,9},{9,8},{10,11... | collective-permute-start | bytes 196616 | tf_op jit(solution)/shard_map/ppermute | solution.py:266

commit v4 on v3

--- a/solution.py
+++ b/solution.py
@@ -41,14 +41,15 @@
     return [high, middle, (left - middle.astype(jnp.float32)).astype(jnp.bfloat16)]
 
 
-def stage_kernel(video, weight, first_bias, second_bias, own, late, rest, staged, first_line, second_line, sems):
+def stage_kernel(video, weight, first_bias, second_bias, front, late, rest_front, rest_late, staged, first_line, second_line, sems):
     core = lax.axis_index("chan")
-    half = own.shape[1]
+    early, half = front.shape[:2]
     size = weight.shape[0]
     pairs = (
-        (video.at[:, pl.ds(core * half, half)], own),
-        (video.at[video.shape[0] - late.shape[0] :, pl.ds(core * half, half)], late),
-        (video.at[:, pl.ds((1 - core) * half, half)], rest),
+        (video.at[:early, pl.ds(core * half, half)], front),
+        (video.at[early:, pl.ds(core * half, half)], late),
+        (video.at[:early, pl.ds((1 - core) * half, half)], rest_front),
+        (video.at[early:, pl.ds((1 - core) * half, half)], rest_late),
         (weight, staged.at[0:size]),
         (first_bias, first_line),
         (second_bias, second_line),
@@ -56,7 +57,7 @@
     copies = [pltpu.make_async_copy(source, target, sems.at[k]) for k, (source, target) in enumerate(pairs)]
     for copy in copies:
         copy.start()
-    for copy in copies[4:]:
+    for copy in copies[5:]:
         copy.wait()
     width = staged.shape[1]
     first = first_line[...]
@@ -64,7 +65,7 @@
     rows = thirds(first) + thirds(second_line[...])
     rows.append(jnp.zeros((TAIL - len(rows), width), jnp.bfloat16))
     staged[size:] = jnp.concatenate(rows, axis=0)
-    for copy in copies[:4]:
+    for copy in copies[:5]:
         copy.wait()
 
 
@@ -148,22 +149,22 @@
     return silu(shifted_sum(parts, columns) + bias).astype(jnp.bfloat16)
 
 
-def second_layer(tile, frames, late, second):
-    def added(rows):
-        left = jnp.concatenate(
-            [jnp.concatenate([tile(n, j) for n in frames[a]], axis=0) for a in frames for j, _ in rows], axis=1
+def second_layer(terms, second):
+    left = jnp.concatenate([tile for tile, _, _ in terms], axis=1)
+    parts = [
+        jnp.dot(
+            left,
+            jnp.concatenate([second[a, b, e] for _, a, b in terms], axis=0),
+            preferred_element_type=jnp.float32,
         )
-        parts = [
-            jnp.dot(
-                left,
-                jnp.concatenate([second[a, b, e] for a in frames for _, b in rows], axis=0),
-                preferred_element_type=jnp.float32,
-            )
-            for e in range(second.shape[2])
-        ]
-        return shifted_sum(parts, tile(frames[next(iter(frames))][0], 0).shape[0])
-
-    return (1 - late, added([(0, 1 - late), (1, 2 - late)])), (late, added([(late, 2 * (1 - late))]))
+        for e in range(second.shape[2])
+    ]
+    return shifted_sum(parts, left.shape[0])
+
+
+def terms_of(tile, frames, late):
+    both = [(tile(n, j), a, 1 - late + j) for n, a in frames for j in range(2)]
+    return both, [(tile(n, late), a, 2 * (1 - late)) for n, a in frames]
 
 
 def put_rows(result, target, start, columns, masks):
@@ -179,11 +180,16 @@
     return [known | (core != j) for j in range(2)]
 
 
-def ahead_kernel(own, beside, packed, bias, hidden, *, border):
-    half, columns = own.shape[1:3]
+def ahead_kernel(front, late, *refs, border):
+    *beside, packed, bias, hidden = refs
+    half, columns = front.shape[1:3]
+
+    def frame(parts, f):
+        return (parts[0], f) if f < parts[0].shape[0] else frame(parts[1:], f - parts[0].shape[0])
 
     def tile(f, k):
-        return own[f, k] if k < half else beside[f, k - half]
+        part, at = frame((front, late) if k < half else beside, f)
+        return part[at, k % half]
 
     result = first_layer(tile, range(hidden.shape[0]), packed, bias[...])
     put_rows(result, hidden, 0, columns, border_masks() if border else None)
@@ -203,23 +209,20 @@
 
 
 def inner_kernel(own, rest, passed, passed_other, packed, bias, ahead, second, partial, hidden):
-    early, _, columns = passed.shape[:3]
     behind(own, rest, passed, passed_other, packed, bias, hidden, 0, None)
-    hidden[early] = ahead[0]
-    add_layers(hidden, lax.axis_index("chan"), second, partial, None)
-
-
-def add_layers(hidden, late, second, target, base):
-    columns = hidden.shape[2]
+    hidden[passed.shape[0]] = ahead[0]
+
+    def store(t, row, value):
+        partial[t, row] = value
+
+    add_layers(hidden, lax.axis_index("chan"), second, store)
+
+
+def add_layers(hidden, late, second, store):
     tile = lambda n, j: hidden[n, j]
-    ends = second_layer(tile, {2: [0, 2]}, late, second)
-    starts = second_layer(tile, {0: [0], 1: [1]}, late, second)
-    for (row, end), (_, start) in zip(ends, starts):
-        first, later = end[:columns], end[columns:] + start
-        if base is not None:
-            first, later = first + base[row, :columns], later + base[row, columns:]
-        target[row, :columns] = first
-        target[row, columns:] = later
+    for t, frames in enumerate(([(0, 2)], [(0, 0), (1, 1), (2, 2)])):
+        for row, terms in zip((1 - late, late), terms_of(tile, frames, late)):
+            store(t, row, second_layer(terms, second))
 
 
 def from_earlier(handed):
@@ -242,23 +245,27 @@
 
 
 def outer_kernel(
-    handed, own, beyond, passed, packed, bias, ahead, second, bias_second, partial, passed_beyond,
-    kept, given, left, hidden, total,
+    own, beyond, passed, passed_beyond, packed, bias, ahead, second, bias_second, partial, kept, given, left, hidden
 ):
+    behind(own, beyond, passed, passed_beyond, packed, bias, hidden, 0, border_masks())
+    hidden[passed.shape[0]] = ahead[0]
+
+    def store(t, row, value):
+        if t == 0:
+            left[row] = partial[t, row] + value
+        else:
+            finish(partial[t, row] + value, bias_second, row, kept, given)
+
+    add_layers(hidden, 1 - lax.axis_index("chan"), second, store)
+
+
+def last_kernel(handed_inner, handed_outer, second, bias_second, left, kept, given):
     core = lax.axis_index("chan")
-    early, _, columns = passed.shape[:3]
-    behind(own, beyond, passed, passed_beyond, packed, bias, hidden, 0, border_masks())
-    hidden[early] = ahead[0]
-    add_layers(hidden, 1 - core, second, total, partial)
-    for row, value in second_layer(from_earlier(handed), {0: [0], 1: [1]}, core, second):
-        left[row] = total[row, :columns] + value
-    for row in range(total.shape[0]):
-        finish(total[row, columns:], bias_second, row, kept, given)
-
-
-def last_kernel(handed, second, bias_second, left, kept, given):
-    for row, value in second_layer(from_earlier(handed), {0: [0], 1: [1]}, 1 - lax.axis_index("chan"), second):
-        finish(left[row] + value, bias_second, row, kept, given)
+    frames = [(0, 0), (1, 1)]
+    inner_both, inner_one = terms_of(from_earlier(handed_inner), frames, core)
+    outer_both, outer_one = terms_of(from_earlier(handed_outer), frames, 1 - core)
+    for row, terms in ((1 - core, inner_both + outer_one), (core, outer_both + inner_one)):
+        finish(left[row] + second_layer(terms, second), bias_second, row, kept, given)
 
 
 def cycle(value, axis):
@@ -301,27 +308,29 @@
         )(*operands)
 
     early = frames // 2
-    tall, short = (shape((count, half, columns, width), bf16) for count in (frames, early))
+    short = shape((early, half, columns, width), bf16)
     turned = jnp.swapaxes(first_weight, 3, 4).reshape(-1, width)
     far = lambda value: pltpu.with_memory_space_constraint(value, pltpu.HBM)
-    own, late, rest, staged = call(
+    front, late, rest_front, rest_late, staged = call(
         stage_kernel,
         [
-            pltpu.VMEM(tall.shape, bf16),
             pltpu.VMEM(short.shape, bf16),
-            pltpu.VMEM(tall.shape, bf16),
+            pltpu.VMEM(short.shape, bf16),
+            pltpu.VMEM(short.shape, bf16),
+            pltpu.VMEM(short.shape, bf16),
             pltpu.VMEM((turned.shape[0] + TAIL, width), bf16),
         ],
         [HBM] * 4,
         [
             pltpu.VMEM((1, first_bias.shape[0]), jnp.float32),
             pltpu.VMEM((1, second_bias.shape[0]), jnp.float32),
-            pltpu.SemaphoreType.DMA((6,)),
+            pltpu.SemaphoreType.DMA((7,)),
         ],
         far(video), far(turned), far(first_bias.reshape(1, -1)), far(second_bias.reshape(1, -1)),
     )
-    beyond = across_border(own)
+    beyond_front, beyond_late = across_border(front), across_border(late)
     passed = cycle(late, "slab")
+    passed_other = cycle(rest_late, "slab")
     staged_other = cycle(staged, "chan")
     matrix = shape((taps * (taps + 1) * width, taps * 2 * width), bf16)
     channels = second_weight.shape[4]
@@ -333,40 +342,39 @@
         staged, staged_other,
     )
     (ahead_inner,) = call(
-        functools.partial(ahead_kernel, border=False), [short], [VMEM] * 4, [], own, rest, packed, bias_first
+        functools.partial(ahead_kernel, border=False), [short], [VMEM] * 6, [], front, late, rest_front, rest_late,
+        packed, bias_first
     )
     handed_inner = cycle(ahead_inner, "slab")
     passed, _ = lax.optimization_barrier((passed, ahead_inner))
     passed_beyond = across_border(passed)
-    passed_other = cycle(passed, "chan")
-    beyond, passed_other = lax.optimization_barrier((beyond, passed_other))
     (ahead_outer,) = call(
-        functools.partial(ahead_kernel, border=True), [short], [VMEM] * 4, [], own, beyond, packed_outer, bias_first
+        functools.partial(ahead_kernel, border=True),
+        [short],
+        [VMEM] * 6,
+        [],
+        front, late, beyond_front, beyond_late, packed_outer, bias_first,
     )
     handed_outer = cycle(ahead_outer, "slab")
     (partial,) = call(
         inner_kernel,
-        [shape((half, early * columns, channels), jnp.float32)],
+        [shape((early, half, columns, channels), jnp.float32)],
         [VMEM] * 8,
         [pltpu.VMEM((early + 1, half, columns, width), bf16)],
-        own, rest, passed, passed_other, packed, bias_first, ahead_inner, second_weight,
+        front, rest_front, passed, passed_other, packed, bias_first, ahead_inner, second_weight,
     )
     part = shape((half, columns, second_bias.shape[0]), bf16)
     handed_inner, partial = lax.optimization_barrier((handed_inner, partial))
     kept_second, given_second, left = call(
         outer_kernel,
         [part, part, shape((half, columns, channels), jnp.float32)],
-        [VMEM] * 11,
-        [
-            pltpu.VMEM((early + 1, half, columns, width), bf16),
-            pltpu.VMEM((half, early * columns, channels), jnp.float32),
-        ],
-        handed_inner, own, beyond, passed, packed_outer, bias_first, ahead_outer, second_weight,
-        bias_last, partial, passed_beyond,
+        [VMEM] * 10,
+        [pltpu.VMEM((early + 1, half, columns, width), bf16)],
+        front, beyond_front, passed, passed_beyond, packed_outer, bias_first, ahead_outer, second_weight, bias_last, partial,
     )
     taken_second = cycle(given_second, "chan")
     kept_first, given_first = call(
-        last_kernel, [part, part], [VMEM] * 4, [], handed_outer, second_weight, bias_last, left
+        last_kernel, [part, part], [VMEM] * 5, [], handed_inner, handed_outer, second_weight, bias_last, left
     )
     taken_first = cycle(given_first, "chan")
     (latents,) = call(

time: 20.8 us -> 20.4 us (0.981)
  waiting for transfers between devices: 3.87 us -> 1.82 us
  starting transfers between devices: 8.62 us -> 10.3 us
    ppermute x7, waiting for transfers between devices: 3.56 us -> 1.82 us  [cycle(): lax.ppermute(value, axis, [(i, (i + 1) % count) for i in range(count)])]
    ppermute x7, starting transfers between devices: 5.58 us -> 6.73 us  [cycle(): lax.ppermute(value, axis, [(i, (i + 1) % count) for i in range(count)])]
    ppermute x2 -> x3, starting transfers between devices: 3.04 us -> 3.55 us  [across_border(): return lax.ppermute(value, ('clip', 'tile', 'chan'), pairs)]
    ppermute x2 -> x3, waiting for transfers between devices: 0.31 us -> 0.01 us  [across_border(): return lax.ppermute(value, ('clip', 'tile', 'chan'), pairs)]
  transfers between devices with their start and end apart: 9 -> 10, of which waited for: 4 -> 3; matrix products, arithmetic and copies ran while one was open for 0% -> 0% of each run, Pallas kernels for 29% -> 27%
where the time goes in v4:
time: 20.4 us; the launch traced here: 20.3 us
  starting transfers between devices  10.3 us (50%)
  Pallas kernels  8.06 us (40%)
  waiting for transfers between devices  1.82 us (9%)
    pallas_call x8, Pallas kernels, call(): pl.pallas_call(kernel, out_shape=outs, in_specs=ins, out_specs=[VMEM] * l...  8.06 us
    ppermute x7, starting transfers between devices, cycle(): lax.ppermute(value, axis, [(i, (i + 1) % count) for i in range(count)])  6.73 us
    ppermute x3, starting transfers between devices, across_border(): return lax.ppermute(value, ('clip', 'tile', 'chan'), pairs)  3.55 us
    ppermute x7, waiting for transfers between devices, cycle(): lax.ppermute(value, axis, [(i, (i + 1) % count) for i in range(count)])  1.82 us
  transfers between devices with their start and end apart: 10, of which 3 were waited for; matrix products, arithmetic and copies ran while one was open for 0% of the time, Pallas kernels for 27%

profile of v4, /device:TPU:0, one launch (start us, length us, event | category | flops | bytes accessed | tf_op | source)
XLA Modules:
  0.0 20.3 jit_solution(10217669228370545681)
XLA Ops:
  0.0 1.3 %shard_map.55 = (bf16[2,2,128,128]{3,2,1,0:T(8,128)(2,1)S(1)}, bf16[2,2,128,128]{3,2,1,0:T(8,128)(2,1)S(1)}, bf16[2,2,128,128]{3,2,1,0:T(8,128)(2,1)S(1)}, bf16[...) custom-call(bf16[4,4,128,128]{3,2,1,0:T(8,128)(2,1)} %video.1, bf16[1728,128]{1,0:T(8,128)(2,1)} %bitcast.5, ...), custom_call_target="tpu_custom_call" | custom-call | flops 1000 | bytes 1000 | tf_op jit(solution)/shard_map/pallas_call | solution.py:300
  1.3 0.5 %collective-permute-start = (bf16[1744,128]{1,0:T(8,128)(2,1)S(1)}, bf16[1744,128]{1,0:T(8,128)(2,1)S(1)}, u32[]{:S(2)}, u32[]{:S(2)}) collective-permute-start(bf16[1744,128]{1,0:T(8,128)(2,1)S(1)} %get-tuple-element.26.own), channel_id=1, source_target_pairs={{0,1},{1,0},{2,3},{3,2},{4,5},{5,4},{6,7},{7,6},{8,9},{9,8},{10,11... | collective-permute-start | bytes 1339400 | tf_op jit(solution)/shard_map/ppermute | solution.py:273
  1.9 2.6 %collective-permute-start.2 = (bf16[2,2,128,128]{3,2,1,0:T(8,128)(2,1)S(1)}, bf16[2,2,128,128]{3,2,1,0:T(8,128)(2,1)S(1)}, u32[]{:S(2)}, u32[]{:S(2)}) collective-permute-start(bf16[2,2,128,128]{3,2,1,0:T(8,128)(2,1)S(1)} %get-tuple-element.23.late), channel_id=1, source_target_pairs={{0,2},{2,0},{1,3},{3,1},{4,6},{6,4},{5,7},{7,5},{8,10},{10,8},{9,1... | collective-permute-start | bytes 393224 | tf_op jit(solution)/shard_map/ppermute | solution.py:273
  4.4 1.5 %collective-permute-start.4 = (bf16[2,2,128,128]{3,2,1,0:T(8,128)(2,1)S(1)}, bf16[2,2,128,128]{3,2,1,0:T(8,128)(2,1)S(1)}, u32[]{:S(2)}, u32[]{:S(2)}) collective-permute-start(bf16[2,2,128,128]{3,2,1,0:T(8,128)(2,1)S(1)} %get-tuple-element.22.front.own), channel_id=1, source_target_pairs={{1,4},{4,1},{5,8},{8,5},{9,12},{12,9},{0,16},{13,29},{17,20},{20,1... | collective-permute-start | bytes 393224 | tf_op jit(solution)/shard_map/ppermute | solution.py:287
  5.9 0.5 %collective-permute-start.5 = (bf16[2,2,128,128]{3,2,1,0:T(8,128)(2,1)S(1)}, bf16[2,2,128,128]{3,2,1,0:T(8,128)(2,1)S(1)}, u32[]{:S(2)}, u32[]{:S(2)}) collective-permute-start(bf16[2,2,128,128]{3,2,1,0:T(8,128)(2,1)S(1)} %get-tuple-element.23.late), channel_id=1, source_target_pairs={{1,4},{4,1},{5,8},{8,5},{9,12},{12,9},{0,16},{13,29},{17,20},{20,1... | collective-permute-start | bytes 393224 | tf_op jit(solution)/shard_map/ppermute | solution.py:287
  6.5 0.1 collective-permute-start.3
  6.5 0.0 collective-permute-done.other
  6.5 0.4 %shard_map.56 = (bf16[1536,768]{1,0:T(8,128)(2,1)S(1)}, bf16[1536,768]{1,0:T(8,128)(2,1)S(1)}, f32[1,256]{1,0:T(1,128)S(1)}, f32[1,256]{1,0:T(1,128)S(1)}) custom-call(bf16[1744,128]{1,0:T(8,128)(2,1)S(1)} %get-tuple-element.26.own, bf16[1744,128]{1,0:T(8,128)(2,1)S(1)} %collective-permute-done.other), custom_call_target="tpu_custom_call" | custom-call | flops 1000 | bytes 1000 | tf_op jit(solution)/shard_map/pallas_call | solution.py:300
  6.9 0.0 copy-start
  7.0 0.8 %shard_map.57.ahead = bf16[2,2,128,128]{3,2,1,0:T(8,128)(2,1)S(1)} custom-call(bf16[2,2,128,128]{3,2,1,0:T(8,128)(2,1)S(1)} %get-tuple-element.22.front.own, bf16[2,2,128,128]{3,2,1,0:T(8,128)(2,1)S(1)} %get-tuple-element.23.late, bf16[2,2,128,128]{3,2,1,0:T(8,128)(2,1)S(1)} %get-tuple-element.24.refs_0_.rest, ...), custom_call_target="tpu_custom_call" | custom-call | flops 1000 | bytes 1000 | tf_op jit(solution)/shard_map/pallas_call | solution.py:300
  7.8 2.0 %collective-permute-start.1 = (bf16[2,2,128,128]{3,2,1,0:T(8,128)(2,1)S(1)}, bf16[2,2,128,128]{3,2,1,0:T(8,128)(2,1)S(1)}, u32[]{:S(2)}, u32[]{:S(2)}) collective-permute-start(bf16[2,2,128,128]{3,2,1,0:T(8,128)(2,1)S(1)} %shard_map.57.ahead), channel_id=1, source_target_pairs={{0,2},{2,0},{1,3},{3,1},{4,6},{6,4},{5,7},{7,5},{8,10},{10,8},{9,1... | collective-permute-start | bytes 393224 | tf_op jit(solution)/shard_map/ppermute | solution.py:273
  9.8 0.0 collective-permute-done.2.passed
  9.8 1.5 %collective-permute-start.7 = (bf16[2,2,128,128]{3,2,1,0:T(8,128)(2,1)S(1)}, bf16[2,2,128,128]{3,2,1,0:T(8,128)(2,1)S(1)}, u32[]{:S(2)}, u32[]{:S(2)}) collective-permute-start(bf16[2,2,128,128]{3,2,1,0:T(8,128)(2,1)S(1)} %collective-permute-done.2.passed), channel_id=1, source_target_pairs={{1,4},{4,1},{5,8},{8,5},{9,12},{12,9},{0,16},{13,29},{17,20},{20,1... | collective-permute-start | bytes 393224 | tf_op jit(solution)/shard_map/ppermute | solution.py:287
  11.3 0.8 %shard_map.59.ahead = bf16[2,2,128,128]{3,2,1,0:T(8,128)(2,1)S(1)} custom-call(bf16[2,2,128,128]{3,2,1,0:T(8,128)(2,1)S(1)} %get-tuple-element.22.front.own, bf16[2,2,128,128]{3,2,1,0:T(8,128)(2,1)S(1)} %get-tuple-element.23.late, bf16[2,2,128,128]{3,2,1,0:T(8,128)(2,1)S(1)} %collective-permute-done.4.refs_0_.beyond, ...), custom_call_target="tpu_custom_call" | custom-call | flops 1000 | bytes 1000 | tf_op jit(solution)/shard_map/pallas_call | solution.py:300
  12.2 1.0 %collective-permute-start.6 = (bf16[2,2,128,128]{3,2,1,0:T(8,128)(2,1)S(1)}, bf16[2,2,128,128]{3,2,1,0:T(8,128)(2,1)S(1)}, u32[]{:S(2)}, u32[]{:S(2)}) collective-permute-start(bf16[2,2,128,128]{3,2,1,0:T(8,128)(2,1)S(1)} %shard_map.59.ahead), channel_id=1, source_target_pairs={{0,2},{2,0},{1,3},{3,1},{4,6},{6,4},{5,7},{7,5},{8,10},{10,8},{9,1... | collective-permute-start | bytes 393224 | tf_op jit(solution)/shard_map/ppermute | solution.py:273
  13.2 1.7 %shard_map.58.partial = f32[2,2,128,256]{3,2,1,0:T(8,128)S(1)} custom-call(bf16[2,2,128,128]{3,2,1,0:T(8,128)(2,1)S(1)} %get-tuple-element.22.front.own, bf16[2,2,128,128]{3,2,1,0:T(8,128)(2,1)S(1)} %get-tuple-element.24.refs_0_.rest, bf16[2,2,128,128]{3,2,1,0:T(8,128)(2,1)S(1)} %collective-permute-done.2.passed, ...), custom_call_target="tpu_custom_call" | custom-call | flops 1000 | bytes 1000 | tf_op jit(solution)/shard_map/pallas_call | solution.py:300
  14.9 1.7 %shard_map.60 = (bf16[2,128,128]{2,1,0:T(8,128)(2,1)S(1)}, bf16[2,128,128]{2,1,0:T(8,128)(2,1)S(1)}, f32[2,128,256]{2,1,0:T(8,128)S(1)}) custom-call(bf16[2,2,128,128]{3,2,1,0:T(8,128)(2,1)S(1)} %get-tuple-element.22.front.own, bf16[2,2,128,128]{3,2,1,0:T(8,128)(2,1)S(1)} %collective-permute-done.4.refs_0_.beyond, ...), custom_call_target="tpu_custom_call" | custom-call | flops 1000 | bytes 1000 | tf_op jit(solution)/shard_map/pallas_call | solution.py:300
  16.6 0.9 %collective-permute-done.6.handed_outer = bf16[2,2,128,128]{3,2,1,0:T(8,128)(2,1)S(1)} collective-permute-done((bf16[2,2,128,128]{3,2,1,0:T(8,128)(2,1)S(1)}, bf16[2,2,128,128]{3,2,1,0:T(8,128)(2,1)S(1)}, u32[]{:S(2)}, u32[]{:S(2)}) %collective-permute-start.6) | collective-permute-done | bytes 131104 | tf_op jit(solution)/shard_map/ppermute | solution.py:273
  17.5 0.5 %shard_map.61 = (bf16[2,128,128]{2,1,0:T(8,128)(2,1)S(1)}, bf16[2,128,128]{2,1,0:T(8,128)(2,1)S(1)}) custom-call(bf16[2,2,128,128]{3,2,1,0:T(8,128)(2,1)S(1)} %collective-permute-done.1.handed_inner, bf16[2,2,128,128]{3,2,1,0:T(8,128)(2,1)S(1)} %collective-permute-done.6.handed_outer, bf16[3,3,3,128,256]{4,3,2,1,0:T(8,128)(2,1)S(1)} %copy-done, ...), custom_call_target="tpu_custom_call" | custom-call | flops 1000 | bytes 1000 | tf_op jit(solution)/shard_map/pallas_call | solution.py:300
  18.1 0.1 collective-permute-start.8
  18.1 0.5 %collective-permute-start.9 = (bf16[2,128,128]{2,1,0:T(8,128)(2,1)S(1)}, bf16[2,128,128]{2,1,0:T(8,128)(2,1)S(1)}, u32[]{:S(2)}, u32[]{:S(2)}) collective-permute-start(bf16[2,128,128]{2,1,0:T(8,128)(2,1)S(1)} %get-tuple-element.38), channel_id=1, source_target_pairs={{0,1},{1,0},{2,3},{3,2},{4,5},{5,4},{6,7},{7,6},{8,9},{9,8},{10,11... | collective-permute-start | bytes 196616 | tf_op jit(solution)/shard_map/ppermute | solution.py:273
  18.6 0.7 %collective-permute-done.8.refs_1_ = bf16[2,128,128]{2,1,0:T(8,128)(2,1)S(1)} collective-permute-done((bf16[2,128,128]{2,1,0:T(8,128)(2,1)S(1)}, bf16[2,128,128]{2,1,0:T(8,128)(2,1)S(1)}, u32[]{:S(2)}, u32[]{:S(2)}) %collective-permute-start.8) | collective-permute-done | bytes 65568 | tf_op jit(solution)/shard_map/ppermute | solution.py:273
  19.4 0.2 collective-permute-done.9.refs_3_
  19.5 0.7 %shard_map.62 = bf16[2,4,128,128]{3,2,1,0:T(8,128)(2,1)} custom-call(bf16[2,128,128]{2,1,0:T(8,128)(2,1)S(1)} %get-tuple-element.35.refs_0_, bf16[2,128,128]{2,1,0:T(8,128)(2,1)S(1)} %collective-permute-done.8.refs_1_, bf16[2,128,128]{2,1,0:T(8,128)(2,1)S(1)} %get-tuple-element.37.refs_2_, bf16[2,128,128]{2,1,0:T(8,128)(2,1)S(1)} %collective-permute-done.9.refs_3_), custom_call_target="tpu_custom_call" | custom-call | flops 1000 | bytes 1000 | tf_op jit(solution)/shard_map/pallas_call | solution.py:300
  (6 shorter events, 0.0 us)
Async XLA Ops:
  1.3 5.2 %collective-permute-start = (bf16[1744,128]{1,0:T(8,128)(2,1)S(1)}, bf16[1744,128]{1,0:T(8,128)(2,1)S(1)}, u32[]{:S(2)}, u32[]{:S(2)}) collective-permute-start(bf16[1744,128]{1,0:T(8,128)(2,1)S(1)} %get-tuple-element.26.own), channel_id=1, source_target_pairs={{0,1},{1,0},{2,3},{3,2},{4,5},{5,4},{6,7},{7,6},{8,9},{9,8},{10,11... | collective-permute-start | bytes 1339400 | tf_op jit(solution)/shard_map/ppermute | solution.py:273
  1.9 7.9 %collective-permute-start.2 = (bf16[2,2,128,128]{3,2,1,0:T(8,128)(2,1)S(1)}, bf16[2,2,128,128]{3,2,1,0:T(8,128)(2,1)S(1)}, u32[]{:S(2)}, u32[]{:S(2)}) collective-permute-start(bf16[2,2,128,128]{3,2,1,0:T(8,128)(2,1)S(1)} %get-tuple-element.23.late), channel_id=1, source_target_pairs={{0,2},{2,0},{1,3},{3,1},{4,6},{6,4},{5,7},{7,5},{8,10},{10,8},{9,1... | collective-permute-start | bytes 393224 | tf_op jit(solution)/shard_map/ppermute | solution.py:273
  4.4 6.9 %collective-permute-start.4 = (bf16[2,2,128,128]{3,2,1,0:T(8,128)(2,1)S(1)}, bf16[2,2,128,128]{3,2,1,0:T(8,128)(2,1)S(1)}, u32[]{:S(2)}, u32[]{:S(2)}) collective-permute-start(bf16[2,2,128,128]{3,2,1,0:T(8,128)(2,1)S(1)} %get-tuple-element.22.front.own), channel_id=1, source_target_pairs={{1,4},{4,1},{5,8},{8,5},{9,12},{12,9},{0,16},{13,29},{17,20},{20,1... | collective-permute-start | bytes 393224 | tf_op jit(solution)/shard_map/ppermute | solution.py:287
  5.9 5.4 %collective-permute-start.5 = (bf16[2,2,128,128]{3,2,1,0:T(8,128)(2,1)S(1)}, bf16[2,2,128,128]{3,2,1,0:T(8,128)(2,1)S(1)}, u32[]{:S(2)}, u32[]{:S(2)}) collective-permute-start(bf16[2,2,128,128]{3,2,1,0:T(8,128)(2,1)S(1)} %get-tuple-element.23.late), channel_id=1, source_target_pairs={{1,4},{4,1},{5,8},{8,5},{9,12},{12,9},{0,16},{13,29},{17,20},{20,1... | collective-permute-start | bytes 393224 | tf_op jit(solution)/shard_map/ppermute | solution.py:287
  6.5 6.7 %collective-permute-start.3 = (bf16[2,2,128,128]{3,2,1,0:T(8,128)(2,1)S(1)}, bf16[2,2,128,128]{3,2,1,0:T(8,128)(2,1)S(1)}, u32[]{:S(2)}, u32[]{:S(2)}) collective-permute-start(bf16[2,2,128,128]{3,2,1,0:T(8,128)(2,1)S(1)} %get-tuple-element.25.refs_1_), channel_id=1, source_target_pairs={{0,2},{2,0},{1,3},{3,1},{4,6},{6,4},{5,7},{7,5},{8,10},{10,8},{9,1... | collective-permute-start | bytes 393224 | tf_op jit(solution)/shard_map/ppermute | solution.py:273
  6.9 6.2 %copy-start = (bf16[3,3,3,128,256]{4,3,2,1,0:T(8,128)(2,1)S(1)}, bf16[3,3,3,128,256]{4,3,2,1,0:T(8,128)(2,1)}, u32[]{:S(2)}) copy-start(bf16[3,3,3,128,256]{4,3,2,1,0:T(8,128)(2,1)} %second.5) | copy-start | bytes 5308420
  7.8 7.1 %collective-permute-start.1 = (bf16[2,2,128,128]{3,2,1,0:T(8,128)(2,1)S(1)}, bf16[2,2,128,128]{3,2,1,0:T(8,128)(2,1)S(1)}, u32[]{:S(2)}, u32[]{:S(2)}) collective-permute-start(bf16[2,2,128,128]{3,2,1,0:T(8,128)(2,1)S(1)} %shard_map.57.ahead), channel_id=1, source_target_pairs={{0,2},{2,0},{1,3},{3,1},{4,6},{6,4},{5,7},{7,5},{8,10},{10,8},{9,1... | collective-permute-start | bytes 393224 | tf_op jit(solution)/shard_map/ppermute | solution.py:273
  9.8 5.1 %collective-permute-start.7 = (bf16[2,2,128,128]{3,2,1,0:T(8,128)(2,1)S(1)}, bf16[2,2,128,128]{3,2,1,0:T(8,128)(2,1)S(1)}, u32[]{:S(2)}, u32[]{:S(2)}) collective-permute-start(bf16[2,2,128,128]{3,2,1,0:T(8,128)(2,1)S(1)} %collective-permute-done.2.passed), channel_id=1, source_target_pairs={{1,4},{4,1},{5,8},{8,5},{9,12},{12,9},{0,16},{13,29},{17,20},{20,1... | collective-permute-start | bytes 393224 | tf_op jit(solution)/shard_map/ppermute | solution.py:287
  12.2 5.4 %collective-permute-start.6 = (bf16[2,2,128,128]{3,2,1,0:T(8,128)(2,1)S(1)}, bf16[2,2,128,128]{3,2,1,0:T(8,128)(2,1)S(1)}, u32[]{:S(2)}, u32[]{:S(2)}) collective-permute-start(bf16[2,2,128,128]{3,2,1,0:T(8,128)(2,1)S(1)} %shard_map.59.ahead), channel_id=1, source_target_pairs={{0,2},{2,0},{1,3},{3,1},{4,6},{6,4},{5,7},{7,5},{8,10},{10,8},{9,1... | collective-permute-start | bytes 393224 | tf_op jit(solution)/shard_map/ppermute | solution.py:273
  18.1 1.3 %collective-permute-start.8 = (bf16[2,128,128]{2,1,0:T(8,128)(2,1)S(1)}, bf16[2,128,128]{2,1,0:T(8,128)(2,1)S(1)}, u32[]{:S(2)}, u32[]{:S(2)}) collective-permute-start(bf16[2,128,128]{2,1,0:T(8,128)(2,1)S(1)} %get-tuple-element.36), channel_id=1, source_target_pairs={{0,1},{1,0},{2,3},{3,2},{4,5},{5,4},{6,7},{7,6},{8,9},{9,8},{10,11... | collective-permute-start | bytes 196616 | tf_op jit(solution)/shard_map/ppermute | solution.py:273
  18.1 1.4 %collective-permute-start.9 = (bf16[2,128,128]{2,1,0:T(8,128)(2,1)S(1)}, bf16[2,128,128]{2,1,0:T(8,128)(2,1)S(1)}, u32[]{:S(2)}, u32[]{:S(2)}) collective-permute-start(bf16[2,128,128]{2,1,0:T(8,128)(2,1)S(1)} %get-tuple-element.38), channel_id=1, source_target_pairs={{0,1},{1,0},{2,3},{3,2},{4,5},{5,4},{6,7},{7,6},{8,9},{9,8},{10,11... | collective-permute-start | bytes 196616 | tf_op jit(solution)/shard_map/ppermute | solution.py:273

commit v5 on v4

--- a/solution.py
+++ b/solution.py
@@ -28,10 +28,14 @@
     return (here + before + after).reshape(size, width)
 
 
+def lower_half():
+    return lax.rem(lax.axis_index("chan") + lax.axis_index("tile"), 2)
+
+
 def border_known():
-    core, tile = lax.axis_index("chan"), lax.axis_index("tile")
+    lower, tile = lower_half(), lax.axis_index("tile")
     last = lax.axis_size("tile") - 1
-    return jnp.logical_not(jnp.logical_or((core == 0) & (tile == 0), (core == 1) & (tile == last)))
+    return jnp.logical_not(jnp.logical_or((lower == 0) & (tile == 0), (lower == 1) & (tile == last)))
 
 
 def thirds(value):
@@ -42,14 +46,14 @@
 
 
 def stage_kernel(video, weight, first_bias, second_bias, front, late, rest_front, rest_late, staged, first_line, second_line, sems):
-    core = lax.axis_index("chan")
+    lower = lower_half()
     early, half = front.shape[:2]
     size = weight.shape[0]
     pairs = (
-        (video.at[:early, pl.ds(core * half, half)], front),
-        (video.at[early:, pl.ds(core * half, half)], late),
-        (video.at[:early, pl.ds((1 - core) * half, half)], rest_front),
-        (video.at[early:, pl.ds((1 - core) * half, half)], rest_late),
+        (video.at[:early, pl.ds(lower * half, half)], front),
+        (video.at[early:, pl.ds(lower * half, half)], late),
+        (video.at[:early, pl.ds((1 - lower) * half, half)], rest_front),
+        (video.at[early:, pl.ds((1 - lower) * half, half)], rest_late),
         (weight, staged.at[0:size]),
         (first_bias, first_line),
         (second_bias, second_line),
@@ -69,16 +73,13 @@
         copy.wait()
 
 
-def join_kernel(*refs):
-    frames = len(refs) // 2 - 1
-    latents, sems = refs[2 * frames :]
-    core = lax.axis_index("chan")
-    half = refs[0].shape[0]
-    copies = []
-    for t in range(frames):
-        for k, place in enumerate((core, 1 - core)):
-            target = latents.at[t, pl.ds(place * half, half)]
-            copies.append(pltpu.make_async_copy(refs[2 * t + k], target, sems.at[2 * t + k]))
+def join_kernel(kept, taken, latents, sems):
+    lower = lower_half()
+    half = kept.shape[1]
+    copies = [
+        pltpu.make_async_copy(part, latents.at[:, pl.ds(place * half, half)], sems.at[k])
+        for k, (part, place) in enumerate(((kept, lower), (taken, 1 - lower)))
+    ]
     for copy in copies:
         copy.start()
     for copy in copies:
@@ -86,7 +87,7 @@
 
 
 def pack_kernel(own, other, inner, outer, bias_first, bias_second):
-    core = lax.axis_index("chan")
+    core, lower = lax.axis_index("chan"), lower_half()
     known = border_known()
     taps = 3
     rows = taps + 1
@@ -120,10 +121,10 @@
                 pair = [full[i - j] if 0 <= i - j < taps else nothing for j in range(2)]
                 pair = jnp.concatenate(pair, axis=1)
                 upper = i < rows // 2
-                at = lax.rem(i + 2 * core, rows) + a * rows
+                at = lax.rem(i + 2 * lower, rows) + a * rows
                 inner[pl.ds(pl.multiple_of(at * width, width), width), across] = pair
-                at = lax.rem(i + 2 * (1 - core), rows) + a * rows
-                used = known | (core == (1 if upper else 0))
+                at = lax.rem(i + 2 * (1 - lower), rows) + a * rows
+                used = known | (lower == (1 if upper else 0))
                 outer[pl.ds(pl.multiple_of(at * width, width), width), across] = jnp.where(
                     used, pair, jnp.zeros_like(pair)
                 )
@@ -176,8 +177,8 @@
 
 
 def border_masks():
-    core, known = lax.axis_index("chan"), border_known()
-    return [known | (core != j) for j in range(2)]
+    lower, known = lower_half(), border_known()
+    return [known | (lower != j) for j in range(2)]
 
 
 def ahead_kernel(front, late, *refs, border):
@@ -191,8 +192,19 @@
         part, at = frame((front, late) if k < half else beside, f)
         return part[at, k % half]
 
-    result = first_layer(tile, range(hidden.shape[0]), packed, bias[...])
-    put_rows(result, hidden, 0, columns, border_masks() if border else None)
+    count = hidden.shape[0]
+    last = lax.axis_index("slab") == lax.axis_size("slab") - 1
+
+    def fill(frames):
+        result = first_layer(tile, range(frames), packed, bias[...])
+        put_rows(result, hidden, 0, columns, border_masks() if border else None)
+
+    pl.when(jnp.logical_not(last))(lambda: fill(count))
+
+    @pl.when(last)
+    def _():
+        fill(count - 1)
+        hidden[count - 1] = jnp.zeros(hidden.shape[1:], hidden.dtype)
 
 
 def behind(own, beside, passed, passed_beside, packed, bias, hidden, start, masks):
@@ -215,7 +227,7 @@
     def store(t, row, value):
         partial[t, row] = value
 
-    add_layers(hidden, lax.axis_index("chan"), second, store)
+    add_layers(hidden, lower_half(), second, store)
 
 
 def add_layers(hidden, late, second, store):
@@ -223,16 +235,6 @@
     for t, frames in enumerate(([(0, 2)], [(0, 0), (1, 1), (2, 2)])):
         for row, terms in zip((1 - late, late), terms_of(tile, frames, late)):
             store(t, row, second_layer(terms, second))
-
-
-def from_earlier(handed):
-    follows = lax.axis_index("slab") > 0
-
-    def tile(n, j):
-        row = handed[n, j]
-        return jnp.where(follows, row, jnp.zeros_like(row))
-
-    return tile
 
 
 def finish(value, bias, row, kept, given):
@@ -256,16 +258,29 @@
         else:
             finish(partial[t, row] + value, bias_second, row, kept, given)
 
-    add_layers(hidden, 1 - lax.axis_index("chan"), second, store)
-
-
-def last_kernel(handed_inner, handed_outer, second, bias_second, left, kept, given):
-    core = lax.axis_index("chan")
+    add_layers(hidden, 1 - lower_half(), second, store)
+
+
+def last_kernel(
+    handed_inner, handed_outer, second, bias_second, left, kept_second, given_second, kept, given
+):
+    lower = lower_half()
+    follows = lax.axis_index("slab") > 0
     frames = [(0, 0), (1, 1)]
-    inner_both, inner_one = terms_of(from_earlier(handed_inner), frames, core)
-    outer_both, outer_one = terms_of(from_earlier(handed_outer), frames, 1 - core)
-    for row, terms in ((1 - core, inner_both + outer_one), (core, outer_both + inner_one)):
-        finish(left[row] + second_layer(terms, second), bias_second, row, kept, given)
+    kept[1] = kept_second[...]
+    given[1] = given_second[...]
+
+    @pl.when(follows)
+    def _():
+        inner_both, inner_one = terms_of(lambda n, j: handed_inner[n, j], frames, lower)
+        outer_both, outer_one = terms_of(lambda n, j: handed_outer[n, j], frames, 1 - lower)
+        for row, terms in ((1 - lower, inner_both + outer_one), (lower, outer_both + inner_one)):
+            finish(left[row] + second_layer(terms, second), bias_second, row, kept.at[0], given.at[0])
+
+    @pl.when(jnp.logical_not(follows))
+    def _():
+        for row in range(left.shape[0]):
+            finish(left[row], bias_second, row, kept.at[0], given.at[0])
 
 
 def cycle(value, axis):
@@ -275,15 +290,16 @@
 
 def across_border(value):
     clips, tiles = lax.axis_size("clip"), lax.axis_size("tile")
+    at = lambda c, t, k: (c * tiles + t) * 2 + k
     pairs = []
     for clip in range(clips):
-        at = lambda c, t, k: (c * tiles + t) * 2 + k
         for tile in range(tiles - 1):
-            pairs.append((at(clip, tile, 1), at(clip, tile + 1, 0)))
-            pairs.append((at(clip, tile + 1, 0), at(clip, tile, 1)))
+            core = (tile + 1) % 2
+            pairs.append((at(clip, tile, core), at(clip, tile + 1, core)))
+            pairs.append((at(clip, tile + 1, core), at(clip, tile, core)))
         if clips > 1:
-            pairs.append((at(clip, 0, 0), at((clip + 1) % clips, 0, 0)))
-            pairs.append((at(clip, tiles - 1, 1), at((clip + 1) % clips, tiles - 1, 1)))
+            for tile, core in ((0, 0), (tiles - 1, tiles % 2)):
+                pairs.append((at(clip, tile, core), at((clip + 1) % clips, tile, core)))
     return lax.ppermute(value, ("clip", "tile", "chan"), pairs)
 
 
@@ -372,17 +388,20 @@
         [pltpu.VMEM((early + 1, half, columns, width), bf16)],
         front, beyond_front, passed, passed_beyond, packed_outer, bias_first, ahead_outer, second_weight, bias_last, partial,
     )
-    taken_second = cycle(given_second, "chan")
-    kept_first, given_first = call(
-        last_kernel, [part, part], [VMEM] * 5, [], handed_inner, handed_outer, second_weight, bias_last, left
-    )
-    taken_first = cycle(given_first, "chan")
+    whole = shape((early,) + part.shape, bf16)
+    kept, given = call(
+        last_kernel,
+        [whole, whole],
+        [VMEM] * 7,
+        [],
+        handed_inner, handed_outer, second_weight, bias_last, left, kept_second, given_second,
+    )
     (latents,) = call(
         join_kernel,
         [shape((early, rows, columns, second_bias.shape[0]), bf16)],
-        [VMEM] * 4,
-        [pltpu.SemaphoreType.DMA((4,))],
-        kept_first, taken_first, kept_second, taken_second,
+        [VMEM] * 2,
+        [pltpu.SemaphoreType.DMA((2,))],
+        kept, cycle(given, "chan"),
         out_specs=[ANY],
     )
     return latents

time: 20.4 us -> 19.4 us (0.951)
  starting transfers between devices: 10.3 us -> 9.46 us
  Pallas kernels: 8.06 us -> 7.62 us
  waiting for transfers between devices: 1.82 us -> 2.13 us
    ppermute x7 -> x6, starting transfers between devices: 6.73 us -> 5.92 us  [cycle(): lax.ppermute(value, axis, [(i, (i + 1) % count) for i in range(count)])]
    pallas_call x8, Pallas kernels: 8.06 us -> 7.62 us  [call(): pl.pallas_call(kernel, out_shape=outs, in_specs=ins, out_specs=[VMEM] * l...]
    ppermute x7 -> x6, waiting for transfers between devices: 1.82 us -> 2.12 us  [cycle(): lax.ppermute(value, axis, [(i, (i + 1) % count) for i in range(count)])]
  transfers between devices with their start and end apart: 10 -> 9, of which waited for: 3 -> 3; matrix products, arithmetic and copies ran while one was open for 0% -> 0% of each run, Pallas kernels for 27% -> 28%
where the time goes in v5:
time: 19.4 us; the launch traced here: 19.3 us
  starting transfers between devices  9.46 us (49%)
  Pallas kernels  7.62 us (39%)
  waiting for transfers between devices  2.13 us (11%)
    pallas_call x8, Pallas kernels, call(): pl.pallas_call(kernel, out_shape=outs, in_specs=ins, out_specs=[VMEM] * l...  7.62 us
    ppermute x6, starting transfers between devices, cycle(): lax.ppermute(value, axis, [(i, (i + 1) % count) for i in range(count)])  5.92 us
    ppermute x3, starting transfers between devices, across_border(): return lax.ppermute(value, ('clip', 'tile', 'chan'), pairs)  3.55 us
    ppermute x6, waiting for transfers between devices, cycle(): lax.ppermute(value, axis, [(i, (i + 1) % count) for i in range(count)])  2.12 us
  transfers between devices with their start and end apart: 9, of which 3 were waited for; matrix products, arithmetic and copies ran while one was open for 0% of the time, Pallas kernels for 28%

profile of v5, /device:TPU:0, one launch (start us, length us, event | category | flops | bytes accessed | tf_op | source)
XLA Modules:
  0.0 19.3 jit_solution(15875431493455668204)
XLA Ops:
  0.0 1.3 %shard_map.55 = (bf16[2,2,128,128]{3,2,1,0:T(8,128)(2,1)S(1)}, bf16[2,2,128,128]{3,2,1,0:T(8,128)(2,1)S(1)}, bf16[2,2,128,128]{3,2,1,0:T(8,128)(2,1)S(1)}, bf16[...) custom-call(bf16[4,4,128,128]{3,2,1,0:T(8,128)(2,1)} %video.1, bf16[1728,128]{1,0:T(8,128)(2,1)} %bitcast.5, ...), custom_call_target="tpu_custom_call" | custom-call | flops 1000 | bytes 1000 | tf_op jit(solution)/shard_map/pallas_call | solution.py:316
  1.3 0.5 %collective-permute-start = (bf16[1744,128]{1,0:T(8,128)(2,1)S(1)}, bf16[1744,128]{1,0:T(8,128)(2,1)S(1)}, u32[]{:S(2)}, u32[]{:S(2)}) collective-permute-start(bf16[1744,128]{1,0:T(8,128)(2,1)S(1)} %get-tuple-element.26.own), channel_id=1, source_target_pairs={{0,1},{1,0},{2,3},{3,2},{4,5},{5,4},{6,7},{7,6},{8,9},{9,8},{10,11... | collective-permute-start | bytes 1339400 | tf_op jit(solution)/shard_map/ppermute | solution.py:288
  1.9 2.6 %collective-permute-start.2 = (bf16[2,2,128,128]{3,2,1,0:T(8,128)(2,1)S(1)}, bf16[2,2,128,128]{3,2,1,0:T(8,128)(2,1)S(1)}, u32[]{:S(2)}, u32[]{:S(2)}) collective-permute-start(bf16[2,2,128,128]{3,2,1,0:T(8,128)(2,1)S(1)} %get-tuple-element.23.late), channel_id=1, source_target_pairs={{0,2},{2,0},{1,3},{3,1},{4,6},{6,4},{5,7},{7,5},{8,10},{10,8},{9,1... | collective-permute-start | bytes 393224 | tf_op jit(solution)/shard_map/ppermute | solution.py:288
  4.4 1.5 %collective-permute-start.4 = (bf16[2,2,128,128]{3,2,1,0:T(8,128)(2,1)S(1)}, bf16[2,2,128,128]{3,2,1,0:T(8,128)(2,1)S(1)}, u32[]{:S(2)}, u32[]{:S(2)}) collective-permute-start(bf16[2,2,128,128]{3,2,1,0:T(8,128)(2,1)S(1)} %get-tuple-element.22.front.own), channel_id=1, source_target_pairs={{1,5},{5,1},{4,8},{8,4},{9,13},{13,9},{0,16},{12,28},{17,21},{21,1... | collective-permute-start | bytes 393224 | tf_op jit(solution)/shard_map/ppermute | solution.py:303
  5.9 0.5 %collective-permute-start.5 = (bf16[2,2,128,128]{3,2,1,0:T(8,128)(2,1)S(1)}, bf16[2,2,128,128]{3,2,1,0:T(8,128)(2,1)S(1)}, u32[]{:S(2)}, u32[]{:S(2)}) collective-permute-start(bf16[2,2,128,128]{3,2,1,0:T(8,128)(2,1)S(1)} %get-tuple-element.23.late), channel_id=1, source_target_pairs={{1,5},{5,1},{4,8},{8,4},{9,13},{13,9},{0,16},{12,28},{17,21},{21,1... | collective-permute-start | bytes 393224 | tf_op jit(solution)/shard_map/ppermute | solution.py:303
  6.5 0.1 collective-permute-start.3
  6.5 0.0 collective-permute-done.other
  6.5 0.4 %shard_map.56 = (bf16[1536,768]{1,0:T(8,128)(2,1)S(1)}, bf16[1536,768]{1,0:T(8,128)(2,1)S(1)}, f32[1,256]{1,0:T(1,128)S(1)}, f32[1,256]{1,0:T(1,128)S(1)}) custom-call(bf16[1744,128]{1,0:T(8,128)(2,1)S(1)} %get-tuple-element.26.own, bf16[1744,128]{1,0:T(8,128)(2,1)S(1)} %collective-permute-done.other), custom_call_target="tpu_custom_call" | custom-call | flops 1000 | bytes 1000 | tf_op jit(solution)/shard_map/pallas_call | solution.py:316
  6.9 0.0 copy-start
  7.0 0.8 %shard_map.57.ahead = bf16[2,2,128,128]{3,2,1,0:T(8,128)(2,1)S(1)} custom-call(bf16[2,2,128,128]{3,2,1,0:T(8,128)(2,1)S(1)} %get-tuple-element.22.front.own, bf16[2,2,128,128]{3,2,1,0:T(8,128)(2,1)S(1)} %get-tuple-element.23.late, bf16[2,2,128,128]{3,2,1,0:T(8,128)(2,1)S(1)} %get-tuple-element.24.refs_0_.rest, ...), custom_call_target="tpu_custom_call" | custom-call | flops 1000 | bytes 1000 | tf_op jit(solution)/shard_map/pallas_call | solution.py:316
  7.8 1.7 %collective-permute-start.1 = (bf16[2,2,128,128]{3,2,1,0:T(8,128)(2,1)S(1)}, bf16[2,2,128,128]{3,2,1,0:T(8,128)(2,1)S(1)}, u32[]{:S(2)}, u32[]{:S(2)}) collective-permute-start(bf16[2,2,128,128]{3,2,1,0:T(8,128)(2,1)S(1)} %shard_map.57.ahead), channel_id=1, source_target_pairs={{0,2},{2,0},{1,3},{3,1},{4,6},{6,4},{5,7},{7,5},{8,10},{10,8},{9,1... | collective-permute-start | bytes 393224 | tf_op jit(solution)/shard_map/ppermute | solution.py:288
  9.5 0.0 collective-permute-done.2.passed
  9.5 1.5 %collective-permute-start.7 = (bf16[2,2,128,128]{3,2,1,0:T(8,128)(2,1)S(1)}, bf16[2,2,128,128]{3,2,1,0:T(8,128)(2,1)S(1)}, u32[]{:S(2)}, u32[]{:S(2)}) collective-permute-start(bf16[2,2,128,128]{3,2,1,0:T(8,128)(2,1)S(1)} %collective-permute-done.2.passed), channel_id=1, source_target_pairs={{1,5},{5,1},{4,8},{8,4},{9,13},{13,9},{0,16},{12,28},{17,21},{21,1... | collective-permute-start | bytes 393224 | tf_op jit(solution)/shard_map/ppermute | solution.py:303
  11.0 0.0 collective-permute-done.4.refs_0_.beyond
  11.0 0.8 %shard_map.59.ahead = bf16[2,2,128,128]{3,2,1,0:T(8,128)(2,1)S(1)} custom-call(bf16[2,2,128,128]{3,2,1,0:T(8,128)(2,1)S(1)} %get-tuple-element.22.front.own, bf16[2,2,128,128]{3,2,1,0:T(8,128)(2,1)S(1)} %get-tuple-element.23.late, bf16[2,2,128,128]{3,2,1,0:T(8,128)(2,1)S(1)} %collective-permute-done.4.refs_0_.beyond, ...), custom_call_target="tpu_custom_call" | custom-call | flops 1000 | bytes 1000 | tf_op jit(solution)/shard_map/pallas_call | solution.py:316
  11.9 1.0 %collective-permute-start.6 = (bf16[2,2,128,128]{3,2,1,0:T(8,128)(2,1)S(1)}, bf16[2,2,128,128]{3,2,1,0:T(8,128)(2,1)S(1)}, u32[]{:S(2)}, u32[]{:S(2)}) collective-permute-start(bf16[2,2,128,128]{3,2,1,0:T(8,128)(2,1)S(1)} %shard_map.59.ahead), channel_id=1, source_target_pairs={{0,2},{2,0},{1,3},{3,1},{4,6},{6,4},{5,7},{7,5},{8,10},{10,8},{9,1... | collective-permute-start | bytes 393224 | tf_op jit(solution)/shard_map/ppermute | solution.py:288
  12.9 1.7 %shard_map.58.partial = f32[2,2,128,256]{3,2,1,0:T(8,128)S(1)} custom-call(bf16[2,2,128,128]{3,2,1,0:T(8,128)(2,1)S(1)} %get-tuple-element.22.front.own, bf16[2,2,128,128]{3,2,1,0:T(8,128)(2,1)S(1)} %get-tuple-element.24.refs_0_.rest, bf16[2,2,128,128]{3,2,1,0:T(8,128)(2,1)S(1)} %collective-permute-done.2.passed, ...), custom_call_target="tpu_custom_call" | custom-call | flops 1000 | bytes 1000 | tf_op jit(solution)/shard_map/pallas_call | solution.py:316
  14.6 0.3 %collective-permute-done.1.handed_inner = bf16[2,2,128,128]{3,2,1,0:T(8,128)(2,1)S(1)} collective-permute-done((bf16[2,2,128,128]{3,2,1,0:T(8,128)(2,1)S(1)}, bf16[2,2,128,128]{3,2,1,0:T(8,128)(2,1)S(1)}, u32[]{:S(2)}, u32[]{:S(2)}) %collective-permute-start.1) | collective-permute-done | bytes 131104 | tf_op jit(solution)/shard_map/ppermute | solution.py:288
  14.9 1.7 %shard_map.60 = (bf16[2,128,128]{2,1,0:T(8,128)(2,1)S(1)}, bf16[2,128,128]{2,1,0:T(8,128)(2,1)S(1)}, f32[2,128,256]{2,1,0:T(8,128)S(1)}) custom-call(bf16[2,2,128,128]{3,2,1,0:T(8,128)(2,1)S(1)} %get-tuple-element.22.front.own, bf16[2,2,128,128]{3,2,1,0:T(8,128)(2,1)S(1)} %collective-permute-done.4.refs_0_.beyond, ...), custom_call_target="tpu_custom_call" | custom-call | flops 1000 | bytes 1000 | tf_op jit(solution)/shard_map/pallas_call | solution.py:316
  16.6 0.5 %collective-permute-done.6.handed_outer = bf16[2,2,128,128]{3,2,1,0:T(8,128)(2,1)S(1)} collective-permute-done((bf16[2,2,128,128]{3,2,1,0:T(8,128)(2,1)S(1)}, bf16[2,2,128,128]{3,2,1,0:T(8,128)(2,1)S(1)}, u32[]{:S(2)}, u32[]{:S(2)}) %collective-permute-start.6) | collective-permute-done | bytes 131104 | tf_op jit(solution)/shard_map/ppermute | solution.py:288
  17.1 0.1 shard_map.61
  17.2 0.1 collective-permute-start.8
  17.2 1.3 %collective-permute-done.8.taken = bf16[2,2,128,128]{3,2,1,0:T(8,128)(2,1)S(1)} collective-permute-done((bf16[2,2,128,128]{3,2,1,0:T(8,128)(2,1)S(1)}, bf16[2,2,128,128]{3,2,1,0:T(8,128)(2,1)S(1)}, u32[]{:S(2)}, u32[]{:S(2)}) %collective-permute-start.8) | collective-permute-done | bytes 131104 | tf_op jit(solution)/shard_map/ppermute | solution.py:288
  18.6 0.7 %shard_map.62 = bf16[2,4,128,128]{3,2,1,0:T(8,128)(2,1)} custom-call(bf16[2,2,128,128]{3,2,1,0:T(8,128)(2,1)S(1)} %get-tuple-element.37.kept, bf16[2,2,128,128]{3,2,1,0:T(8,128)(2,1)S(1)} %collective-permute-done.8.taken), custom_call_target="tpu_custom_call" | custom-call | flops 1000 | bytes 1000 | tf_op jit(solution)/shard_map/pallas_call | solution.py:316
  (4 shorter events, 0.0 us)
Async XLA Ops:
  1.3 5.2 %collective-permute-start = (bf16[1744,128]{1,0:T(8,128)(2,1)S(1)}, bf16[1744,128]{1,0:T(8,128)(2,1)S(1)}, u32[]{:S(2)}, u32[]{:S(2)}) collective-permute-start(bf16[1744,128]{1,0:T(8,128)(2,1)S(1)} %get-tuple-element.26.own), channel_id=1, source_target_pairs={{0,1},{1,0},{2,3},{3,2},{4,5},{5,4},{6,7},{7,6},{8,9},{9,8},{10,11... | collective-permute-start | bytes 1339400 | tf_op jit(solution)/shard_map/ppermute | solution.py:288
  1.9 7.7 %collective-permute-start.2 = (bf16[2,2,128,128]{3,2,1,0:T(8,128)(2,1)S(1)}, bf16[2,2,128,128]{3,2,1,0:T(8,128)(2,1)S(1)}, u32[]{:S(2)}, u32[]{:S(2)}) collective-permute-start(bf16[2,2,128,128]{3,2,1,0:T(8,128)(2,1)S(1)} %get-tuple-element.23.late), channel_id=1, source_target_pairs={{0,2},{2,0},{1,3},{3,1},{4,6},{6,4},{5,7},{7,5},{8,10},{10,8},{9,1... | collective-permute-start | bytes 393224 | tf_op jit(solution)/shard_map/ppermute | solution.py:288
  4.4 6.6 %collective-permute-start.4 = (bf16[2,2,128,128]{3,2,1,0:T(8,128)(2,1)S(1)}, bf16[2,2,128,128]{3,2,1,0:T(8,128)(2,1)S(1)}, u32[]{:S(2)}, u32[]{:S(2)}) collective-permute-start(bf16[2,2,128,128]{3,2,1,0:T(8,128)(2,1)S(1)} %get-tuple-element.22.front.own), channel_id=1, source_target_pairs={{1,5},{5,1},{4,8},{8,4},{9,13},{13,9},{0,16},{12,28},{17,21},{21,1... | collective-permute-start | bytes 393224 | tf_op jit(solution)/shard_map/ppermute | solution.py:303
  5.9 5.1 %collective-permute-start.5 = (bf16[2,2,128,128]{3,2,1,0:T(8,128)(2,1)S(1)}, bf16[2,2,128,128]{3,2,1,0:T(8,128)(2,1)S(1)}, u32[]{:S(2)}, u32[]{:S(2)}) collective-permute-start(bf16[2,2,128,128]{3,2,1,0:T(8,128)(2,1)S(1)} %get-tuple-element.23.late), channel_id=1, source_target_pairs={{1,5},{5,1},{4,8},{8,4},{9,13},{13,9},{0,16},{12,28},{17,21},{21,1... | collective-permute-start | bytes 393224 | tf_op jit(solution)/shard_map/ppermute | solution.py:303
  6.5 6.4 %collective-permute-start.3 = (bf16[2,2,128,128]{3,2,1,0:T(8,128)(2,1)S(1)}, bf16[2,2,128,128]{3,2,1,0:T(8,128)(2,1)S(1)}, u32[]{:S(2)}, u32[]{:S(2)}) collective-permute-start(bf16[2,2,128,128]{3,2,1,0:T(8,128)(2,1)S(1)} %get-tuple-element.25.refs_1_), channel_id=1, source_target_pairs={{0,2},{2,0},{1,3},{3,1},{4,6},{6,4},{5,7},{7,5},{8,10},{10,8},{9,1... | collective-permute-start | bytes 393224 | tf_op jit(solution)/shard_map/ppermute | solution.py:288
  6.9 5.9 %copy-start = (bf16[3,3,3,128,256]{4,3,2,1,0:T(8,128)(2,1)S(1)}, bf16[3,3,3,128,256]{4,3,2,1,0:T(8,128)(2,1)}, u32[]{:S(2)}) copy-start(bf16[3,3,3,128,256]{4,3,2,1,0:T(8,128)(2,1)} %second.5) | copy-start | bytes 5308420
  7.8 7.1 %collective-permute-start.1 = (bf16[2,2,128,128]{3,2,1,0:T(8,128)(2,1)S(1)}, bf16[2,2,128,128]{3,2,1,0:T(8,128)(2,1)S(1)}, u32[]{:S(2)}, u32[]{:S(2)}) collective-permute-start(bf16[2,2,128,128]{3,2,1,0:T(8,128)(2,1)S(1)} %shard_map.57.ahead), channel_id=1, source_target_pairs={{0,2},{2,0},{1,3},{3,1},{4,6},{6,4},{5,7},{7,5},{8,10},{10,8},{9,1... | collective-permute-start | bytes 393224 | tf_op jit(solution)/shard_map/ppermute | solution.py:288
  9.5 5.4 %collective-permute-start.7 = (bf16[2,2,128,128]{3,2,1,0:T(8,128)(2,1)S(1)}, bf16[2,2,128,128]{3,2,1,0:T(8,128)(2,1)S(1)}, u32[]{:S(2)}, u32[]{:S(2)}) collective-permute-start(bf16[2,2,128,128]{3,2,1,0:T(8,128)(2,1)S(1)} %collective-permute-done.2.passed), channel_id=1, source_target_pairs={{1,5},{5,1},{4,8},{8,4},{9,13},{13,9},{0,16},{12,28},{17,21},{21,1... | collective-permute-start | bytes 393224 | tf_op jit(solution)/shard_map/ppermute | solution.py:303
  11.9 5.2 %collective-permute-start.6 = (bf16[2,2,128,128]{3,2,1,0:T(8,128)(2,1)S(1)}, bf16[2,2,128,128]{3,2,1,0:T(8,128)(2,1)S(1)}, u32[]{:S(2)}, u32[]{:S(2)}) collective-permute-start(bf16[2,2,128,128]{3,2,1,0:T(8,128)(2,1)S(1)} %shard_map.59.ahead), channel_id=1, source_target_pairs={{0,2},{2,0},{1,3},{3,1},{4,6},{6,4},{5,7},{7,5},{8,10},{10,8},{9,1... | collective-permute-start | bytes 393224 | tf_op jit(solution)/shard_map/ppermute | solution.py:288
  17.2 1.4 %collective-permute-start.8 = (bf16[2,2,128,128]{3,2,1,0:T(8,128)(2,1)S(1)}, bf16[2,2,128,128]{3,2,1,0:T(8,128)(2,1)S(1)}, u32[]{:S(2)}, u32[]{:S(2)}) collective-permute-start(bf16[2,2,128,128]{3,2,1,0:T(8,128)(2,1)S(1)} %get-tuple-element.38), channel_id=1, source_target_pairs={{0,1},{1,0},{2,3},{3,2},{4,5},{5,4},{6,7},{7,6},{8,9},{9,8},{10,11... | collective-permute-start | bytes 393224 | tf_op jit(solution)/shard_map/ppermute | solution.py:288

commit v6 on v5

--- a/solution.py
+++ b/solution.py
@@ -12,6 +12,7 @@
 HBM = pl.BlockSpec(memory_space=pltpu.HBM)
 LIMIT = 20 * 1024 * 1024
 TAIL = 16
+SPARE = 16
 
 
 def silu(value):
@@ -19,13 +20,18 @@
     return half + half * jnp.tanh(half)
 
 
-def shifted_sum(parts, columns):
-    size, width = parts[0].shape
-    before, here, after = (part.reshape(size // columns, columns, width) for part in parts)
-    cell = lax.broadcasted_iota(jnp.int32, (1, columns, width), 1)
-    before = jnp.where(cell == 0, 0.0, pltpu.roll(before, 1, 1))
-    after = jnp.where(cell == columns - 1, 0.0, pltpu.roll(after, columns - 1, 1))
-    return (here + before + after).reshape(size, width)
+def shifted_sum(part, columns):
+    def cells(value):
+        size, width = value.shape
+        value = value.reshape(size // columns, columns, width)
+        return value, lax.broadcasted_iota(jnp.int32, (1, columns, width), 1)
+
+    before, cell = cells(part(0))
+    total = jnp.where(cell == 0, 0.0, pltpu.roll(before, 1, 1))
+    after, cell = cells(part(2))
+    total = total + jnp.where(cell == columns - 1, 0.0, pltpu.roll(after, columns - 1, 1))
+    here = part(1)
+    return here + total.reshape(here.shape)
 
 
 def lower_half():
@@ -50,18 +56,18 @@
     early, half = front.shape[:2]
     size = weight.shape[0]
     pairs = (
-        (video.at[:early, pl.ds(lower * half, half)], front),
-        (video.at[early:, pl.ds(lower * half, half)], late),
-        (video.at[:early, pl.ds((1 - lower) * half, half)], rest_front),
-        (video.at[early:, pl.ds((1 - lower) * half, half)], rest_late),
-        (weight, staged.at[0:size]),
         (first_bias, first_line),
         (second_bias, second_line),
+        (weight, staged.at[0:size]),
+        (video.at[early:, pl.ds(lower * half, half)], late),
+        (video.at[:early, pl.ds(lower * half, half)], front),
+        (video.at[early:, pl.ds((1 - lower) * half, half)], rest_late),
+        (video.at[:early, pl.ds((1 - lower) * half, half)], rest_front),
     )
     copies = [pltpu.make_async_copy(source, target, sems.at[k]) for k, (source, target) in enumerate(pairs)]
     for copy in copies:
         copy.start()
-    for copy in copies[5:]:
+    for copy in copies[:2]:
         copy.wait()
     width = staged.shape[1]
     first = first_line[...]
@@ -69,7 +75,7 @@
     rows = thirds(first) + thirds(second_line[...])
     rows.append(jnp.zeros((TAIL - len(rows), width), jnp.bfloat16))
     staged[size:] = jnp.concatenate(rows, axis=0)
-    for copy in copies[:5]:
+    for copy in copies[2:]:
         copy.wait()
 
 
@@ -86,9 +92,8 @@
         copy.wait()
 
 
-def pack_kernel(own, other, inner, outer, bias_first, bias_second):
+def pack_kernel(own, other, packed, bias_first, bias_second):
     core, lower = lax.axis_index("chan"), lower_half()
-    known = border_known()
     taps = 3
     rows = taps + 1
     width = own.shape[1]
@@ -120,14 +125,8 @@
             for i in range(rows):
                 pair = [full[i - j] if 0 <= i - j < taps else nothing for j in range(2)]
                 pair = jnp.concatenate(pair, axis=1)
-                upper = i < rows // 2
                 at = lax.rem(i + 2 * lower, rows) + a * rows
-                inner[pl.ds(pl.multiple_of(at * width, width), width), across] = pair
-                at = lax.rem(i + 2 * (1 - lower), rows) + a * rows
-                used = known | (lower == (1 if upper else 0))
-                outer[pl.ds(pl.multiple_of(at * width, width), width), across] = jnp.where(
-                    used, pair, jnp.zeros_like(pair)
-                )
+                packed[pl.ds(pl.multiple_of(at * width, width), width), across] = pair
 
 
 def first_layer(tile, frames, packed, bias):
@@ -143,24 +142,18 @@
     )
     double = packed.shape[1] // taps
     columns = left.shape[0] // len(frames)
-    parts = [
-        jnp.dot(left, packed[:, e * double : (e + 1) * double], preferred_element_type=jnp.float32)
-        for e in range(taps)
-    ]
-    return silu(shifted_sum(parts, columns) + bias).astype(jnp.bfloat16)
+    part = lambda e: jnp.dot(left, packed[:, e * double : (e + 1) * double], preferred_element_type=jnp.float32)
+    return silu(shifted_sum(part, columns) + bias).astype(jnp.bfloat16)
 
 
 def second_layer(terms, second):
     left = jnp.concatenate([tile for tile, _, _ in terms], axis=1)
-    parts = [
-        jnp.dot(
-            left,
-            jnp.concatenate([second[a, b, e] for _, a, b in terms], axis=0),
-            preferred_element_type=jnp.float32,
-        )
-        for e in range(second.shape[2])
-    ]
-    return shifted_sum(parts, left.shape[0])
+
+    def part(e):
+        right = jnp.concatenate([second[a, b, e] for _, a, b in terms], axis=0)
+        return jnp.dot(left, right, preferred_element_type=jnp.float32)
+
+    return shifted_sum(part, left.shape[0])
 
 
 def terms_of(tile, frames, late):
@@ -181,48 +174,70 @@
     return [known | (lower != j) for j in range(2)]
 
 
-def ahead_kernel(front, late, *refs, border):
-    *beside, packed, bias, hidden = refs
-    half, columns = front.shape[1:3]
-
-    def frame(parts, f):
-        return (parts[0], f) if f < parts[0].shape[0] else frame(parts[1:], f - parts[0].shape[0])
+def last_slab():
+    return lax.axis_index("slab") == lax.axis_size("slab") - 1
+
+
+def masked(row, *conditions):
+    for condition in conditions:
+        row = jnp.where(condition, row, jnp.zeros_like(row))
+    return row
+
+
+def ahead_kernel(*refs, border):
+    early_first, late_first, early_second, late_second, packed, bias, hidden, *sent = refs
+    early, half, columns = early_first.shape[:3]
+    unknown = [border_known()] if border else []
 
     def tile(f, k):
-        part, at = frame((front, late) if k < half else beside, f)
-        return part[at, k % half]
-
-    count = hidden.shape[0]
-    last = lax.axis_index("slab") == lax.axis_size("slab") - 1
+        first, second = (early_first, early_second) if f < early else (late_first, late_second)
+        return masked(first[f % early, k], *unknown) if k < half else second[f % early, k - half]
+
+    @pl.when(jnp.logical_not(last_slab()))
+    def _():
+        result = first_layer(tile, range(hidden.shape[0]), packed, bias[...])
+        put_rows(result, hidden, 0, columns, border_masks() if border else None)
+        for target in sent:
+            size = target.shape[0] - SPARE
+            target[:size] = hidden[...].reshape(size, target.shape[1])
+            target[size:] = jnp.zeros((SPARE, target.shape[1]), target.dtype)
+
+    @pl.when(last_slab())
+    def _():
+        for target in (hidden, *sent):
+            target[...] = jnp.zeros(target.shape, target.dtype)
+
+
+def behind(first, second, passed_first, passed_second, packed, bias, ahead, hidden, border):
+    early, half, columns = passed_first.shape[:3]
+    follows = lax.axis_index("slab") > 0
+    unknown = [border_known()] if border else []
+
+    def tile(f, k):
+        if f >= early:
+            part = (first if k < half else second)[f // early - 1]
+            return masked(part[f % early, k % half], *(unknown if k < half else []))
+        if k < half:
+            return masked(passed_first[f, k], follows, *unknown)
+        return masked(passed_second[f, k - half], follows)
 
     def fill(frames):
         result = first_layer(tile, range(frames), packed, bias[...])
         put_rows(result, hidden, 0, columns, border_masks() if border else None)
 
-    pl.when(jnp.logical_not(last))(lambda: fill(count))
-
-    @pl.when(last)
+    @pl.when(jnp.logical_not(last_slab()))
     def _():
-        fill(count - 1)
-        hidden[count - 1] = jnp.zeros(hidden.shape[1:], hidden.dtype)
-
-
-def behind(own, beside, passed, passed_beside, packed, bias, hidden, start, masks):
-    early, half, columns = passed.shape[:3]
-    follows = lax.axis_index("slab") > 0
-
-    def tile(f, k):
-        if f >= early:
-            return own[f - early, k] if k < half else beside[f - early, k - half]
-        row = passed[f, k] if k < half else passed_beside[f, k - half]
-        return jnp.where(follows, row, jnp.zeros_like(row))
-
-    put_rows(first_layer(tile, range(early), packed, bias[...]), hidden, start, columns, masks)
-
-
-def inner_kernel(own, rest, passed, passed_other, packed, bias, ahead, second, partial, hidden):
-    behind(own, rest, passed, passed_other, packed, bias, hidden, 0, None)
-    hidden[passed.shape[0]] = ahead[0]
+        fill(early)
+        hidden[early] = ahead[0]
+
+    pl.when(last_slab())(lambda: fill(early + 1))
+
+
+def inner_kernel(
+    front, late, rest_front, rest_late, passed, passed_other, packed, bias, ahead, second, partial, hidden
+):
+    halves = (front, late), (rest_front, rest_late)
+    behind(*halves, passed, passed_other, packed, bias, ahead, hidden, False)
 
     def store(t, row, value):
         partial[t, row] = value
@@ -247,10 +262,11 @@
 
 
 def outer_kernel(
-    own, beyond, passed, passed_beyond, packed, bias, ahead, second, bias_second, partial, kept, given, left, hidden
+    front, late, beyond_front, beyond_late, passed, passed_beyond, packed, bias, ahead, second, bias_second, partial,
+    kept, given, left, hidden,
 ):
-    behind(own, beyond, passed, passed_beyond, packed, bias, hidden, 0, border_masks())
-    hidden[passed.shape[0]] = ahead[0]
+    halves = (beyond_front, beyond_late), (front, late)
+    behind(*halves, passed_beyond, passed, packed, bias, ahead, hidden, True)
 
     def store(t, row, value):
         if t == 0:
@@ -272,7 +288,12 @@
 
     @pl.when(follows)
     def _():
-        inner_both, inner_one = terms_of(lambda n, j: handed_inner[n, j], frames, lower)
+        half, columns = handed_outer.shape[1:3]
+
+        def inner(n, j):
+            return handed_inner[pl.ds(pl.multiple_of((n * half + j) * columns, columns), columns)]
+
+        inner_both, inner_one = terms_of(inner, frames, lower)
         outer_both, outer_one = terms_of(lambda n, j: handed_outer[n, j], frames, 1 - lower)
         for row, terms in ((1 - lower, inner_both + outer_one), (lower, outer_both + inner_one)):
             finish(left[row] + second_layer(terms, second), bias_second, row, kept.at[0], given.at[0])
@@ -346,47 +367,49 @@
     )
     beyond_front, beyond_late = across_border(front), across_border(late)
     passed = cycle(late, "slab")
-    passed_other = cycle(rest_late, "slab")
     staged_other = cycle(staged, "chan")
     matrix = shape((taps * (taps + 1) * width, taps * 2 * width), bf16)
     channels = second_weight.shape[4]
-    packed, packed_outer, bias_first, bias_last = call(
+    packed, bias_first, bias_last = call(
         pack_kernel,
-        [matrix, matrix, shape((1, 2 * width), jnp.float32), shape((1, channels), jnp.float32)],
+        [matrix, shape((1, 2 * width), jnp.float32), shape((1, channels), jnp.float32)],
         [VMEM] * 2,
         [],
         staged, staged_other,
     )
-    (ahead_inner,) = call(
-        functools.partial(ahead_kernel, border=False), [short], [VMEM] * 6, [], front, late, rest_front, rest_late,
+    ahead_inner, sent = call(
+        functools.partial(ahead_kernel, border=False),
+        [short, shape((early * half * columns + SPARE, width), bf16)],
+        [VMEM] * 6, [], front, late, rest_front, rest_late,
         packed, bias_first
     )
-    handed_inner = cycle(ahead_inner, "slab")
+    handed_inner = cycle(sent, "slab")
     passed, _ = lax.optimization_barrier((passed, ahead_inner))
+    passed_other = cycle(passed, "chan")
     passed_beyond = across_border(passed)
     (ahead_outer,) = call(
         functools.partial(ahead_kernel, border=True),
         [short],
         [VMEM] * 6,
         [],
-        front, late, beyond_front, beyond_late, packed_outer, bias_first,
+        beyond_front, beyond_late, front, late, packed, bias_first,
     )
     handed_outer = cycle(ahead_outer, "slab")
     (partial,) = call(
         inner_kernel,
         [shape((early, half, columns, channels), jnp.float32)],
-        [VMEM] * 8,
+        [VMEM] * 10,
         [pltpu.VMEM((early + 1, half, columns, width), bf16)],
-        front, rest_front, passed, passed_other, packed, bias_first, ahead_inner, second_weight,
+        front, late, rest_front, rest_late, passed, passed_other, packed, bias_first, ahead_inner, second_weight,
     )
     part = shape((half, columns, second_bias.shape[0]), bf16)
     handed_inner, partial = lax.optimization_barrier((handed_inner, partial))
     kept_second, given_second, left = call(
         outer_kernel,
         [part, part, shape((half, columns, channels), jnp.float32)],
-        [VMEM] * 10,
+        [VMEM] * 12,
         [pltpu.VMEM((early + 1, half, columns, width), bf16)],
-        front, beyond_front, passed, passed_beyond, packed_outer, bias_first, ahead_outer, second_weight, bias_last, partial,
+        front, late, beyond_front, beyond_late, passed, passed_beyond, packed, bias_first, ahead_outer, second_weight, bias_last, partial,
     )
     whole = shape((early,) + part.shape, bf16)
     kept, given = call(

time: 19.4 us -> 19.2 us (0.990)
  waiting for transfers between devices: 2.13 us -> 4.85 us
  starting transfers between devices: 9.46 us -> 7.17 us
  Pallas kernels: 7.62 us -> 6.95 us
    ppermute x6, starting transfers between devices: 5.92 us -> 3.36 us  [cycle(): lax.ppermute(value, axis, [(i, (i + 1) % count) for i in range(count)])]
    ppermute x6, waiting for transfers between devices: 2.12 us -> 4.09 us  [cycle(): lax.ppermute(value, axis, [(i, (i + 1) % count) for i in range(count)])]
    ppermute x3, waiting for transfers between devices: 0.01 us -> 0.76 us  [across_border(): return lax.ppermute(value, ('clip', 'tile', 'chan'), pairs)]
    pallas_call x8, Pallas kernels: 7.62 us -> 6.95 us  [call(): pl.pallas_call(kernel, out_shape=outs, in_specs=ins, out_specs=[VMEM] * l...]
    ppermute x3, starting transfers between devices: 3.55 us -> 3.81 us  [across_border(): return lax.ppermute(value, ('clip', 'tile', 'chan'), pairs)]
  transfers between devices with their start and end apart: 9 -> 9, of which waited for: 3 -> 5; matrix products, arithmetic and copies ran while one was open for 0% -> 0% of each run, Pallas kernels for 28% -> 26%
where the time goes in v6:
time: 19.2 us; the launch traced here: 19.1 us
  starting transfers between devices  7.17 us (37%)
  Pallas kernels  6.95 us (36%)
  waiting for transfers between devices  4.85 us (25%)
    pallas_call x8, Pallas kernels, call(): pl.pallas_call(kernel, out_shape=outs, in_specs=ins, out_specs=[VMEM] * l...  6.95 us
    ppermute x6, waiting for transfers between devices, cycle(): lax.ppermute(value, axis, [(i, (i + 1) % count) for i in range(count)])  4.09 us
    ppermute x3, starting transfers between devices, across_border(): return lax.ppermute(value, ('clip', 'tile', 'chan'), pairs)  3.81 us
    ppermute x6, starting transfers between devices, cycle(): lax.ppermute(value, axis, [(i, (i + 1) % count) for i in range(count)])  3.36 us
    ppermute x3, waiting for transfers between devices, across_border(): return lax.ppermute(value, ('clip', 'tile', 'chan'), pairs)  0.76 us
  transfers between devices with their start and end apart: 9, of which 5 were waited for; matrix products, arithmetic and copies ran while one was open for 0% of the time, Pallas kernels for 26%

profile of v6, /device:TPU:0, one launch (start us, length us, event | category | flops | bytes accessed | tf_op | source)
XLA Modules:
  0.0 19.1 jit_solution(17910197256758899537)
XLA Ops:
  0.0 1.3 %shard_map.55 = (bf16[2,2,128,128]{3,2,1,0:T(8,128)(2,1)S(1)}, bf16[2,2,128,128]{3,2,1,0:T(8,128)(2,1)S(1)}, bf16[2,2,128,128]{3,2,1,0:T(8,128)(2,1)S(1)}, bf16[...) custom-call(bf16[4,4,128,128]{3,2,1,0:T(8,128)(2,1)} %video.1, bf16[1728,128]{1,0:T(8,128)(2,1)} %bitcast.5, ...), custom_call_target="tpu_custom_call" | custom-call | flops 1000 | bytes 1000 | tf_op jit(solution)/shard_map/pallas_call | solution.py:337
  1.3 0.5 %collective-permute-start = (bf16[1744,128]{1,0:T(8,128)(2,1)S(1)}, bf16[1744,128]{1,0:T(8,128)(2,1)S(1)}, u32[]{:S(2)}, u32[]{:S(2)}) collective-permute-start(bf16[1744,128]{1,0:T(8,128)(2,1)S(1)} %get-tuple-element.27.own), channel_id=1, source_target_pairs={{0,1},{1,0},{2,3},{3,2},{4,5},{5,4},{6,7},{7,6},{8,9},{9,8},{10,11... | collective-permute-start | bytes 1339400 | tf_op jit(solution)/shard_map/ppermute | solution.py:309
  1.8 2.6 %collective-permute-start.2 = (bf16[2,2,128,128]{3,2,1,0:T(8,128)(2,1)S(1)}, bf16[2,2,128,128]{3,2,1,0:T(8,128)(2,1)S(1)}, u32[]{:S(2)}, u32[]{:S(2)}) collective-permute-start(bf16[2,2,128,128]{3,2,1,0:T(8,128)(2,1)S(1)} %get-tuple-element.24.refs_1_.late.refs_3_), channel_id=1, source_target_pairs={{0,2},{2,0},{1,3},{3,1},{4,6},{6,4},{5,7},{7,5},{8,10},{10,8},{9,1... | collective-permute-start | bytes 393224 | tf_op jit(solution)/shard_map/ppermute | solution.py:309
  4.4 1.5 %collective-permute-start.5 = (bf16[2,2,128,128]{3,2,1,0:T(8,128)(2,1)S(1)}, bf16[2,2,128,128]{3,2,1,0:T(8,128)(2,1)S(1)}, u32[]{:S(2)}, u32[]{:S(2)}) collective-permute-start(bf16[2,2,128,128]{3,2,1,0:T(8,128)(2,1)S(1)} %get-tuple-element.24.refs_1_.late.refs_3_), channel_id=1, source_target_pairs={{1,5},{5,1},{4,8},{8,4},{9,13},{13,9},{0,16},{12,28},{17,21},{21,1... | collective-permute-start | bytes 393224 | tf_op jit(solution)/shard_map/ppermute | solution.py:324
  5.9 0.5 %collective-permute-start.4 = (bf16[2,2,128,128]{3,2,1,0:T(8,128)(2,1)S(1)}, bf16[2,2,128,128]{3,2,1,0:T(8,128)(2,1)S(1)}, u32[]{:S(2)}, u32[]{:S(2)}) collective-permute-start(bf16[2,2,128,128]{3,2,1,0:T(8,128)(2,1)S(1)} %get-tuple-element.23.refs_0_.front.refs_2_), channel_id=1, source_target_pairs={{1,5},{5,1},{4,8},{8,4},{9,13},{13,9},{0,16},{12,28},{17,21},{21,1... | collective-permute-start | bytes 393224 | tf_op jit(solution)/shard_map/ppermute | solution.py:324
  6.4 0.0 collective-permute-done.other
  6.4 0.3 %shard_map.56 = (bf16[1536,768]{1,0:T(8,128)(2,1)S(1)}, f32[1,256]{1,0:T(1,128)S(1)}, f32[1,256]{1,0:T(1,128)S(1)}) custom-call(bf16[1744,128]{1,0:T(8,128)(2,1)S(1)} %get-tuple-element.27.own, bf16[1744,128]{1,0:T(8,128)(2,1)S(1)} %collective-permute-done.other), custom_call_target="tpu_custom_call" | custom-call | flops 1000 | bytes 1000 | tf_op jit(solution)/shard_map/pallas_call | solution.py:337
  6.7 0.0 copy-start
  6.7 0.9 %shard_map.57 = (bf16[2,2,128,128]{3,2,1,0:T(8,128)(2,1)S(1)}, bf16[528,128]{1,0:T(8,128)(2,1)S(1)}) custom-call(bf16[2,2,128,128]{3,2,1,0:T(8,128)(2,1)S(1)} %get-tuple-element.23.refs_0_.front.refs_2_, bf16[2,2,128,128]{3,2,1,0:T(8,128)(2,1)S(1)} %get-tuple-element.24.refs_1_.late.refs_3_, ...), custom_call_target="tpu_custom_call" | custom-call | flops 1000 | bytes 1000 | tf_op jit(solution)/shard_map/pallas_call | solution.py:337
  7.6 0.1 collective-permute-start.1
  7.7 0.8 %collective-permute-done.2.passed = bf16[2,2,128,128]{3,2,1,0:T(8,128)(2,1)S(1)} collective-permute-done((bf16[2,2,128,128]{3,2,1,0:T(8,128)(2,1)S(1)}, bf16[2,2,128,128]{3,2,1,0:T(8,128)(2,1)S(1)}, u32[]{:S(2)}, u32[]{:S(2)}) %collective-permute-start.2) | collective-permute-done | bytes 131104 | tf_op jit(solution)/shard_map/ppermute | solution.py:309
  8.5 0.0 collective-permute-start.3
  8.5 1.8 %collective-permute-start.7 = (bf16[2,2,128,128]{3,2,1,0:T(8,128)(2,1)S(1)}, bf16[2,2,128,128]{3,2,1,0:T(8,128)(2,1)S(1)}, u32[]{:S(2)}, u32[]{:S(2)}) collective-permute-start(bf16[2,2,128,128]{3,2,1,0:T(8,128)(2,1)S(1)} %collective-permute-done.2.passed), channel_id=1, source_target_pairs={{1,5},{5,1},{4,8},{8,4},{9,13},{13,9},{0,16},{12,28},{17,21},{21,1... | collective-permute-start | bytes 393224 | tf_op jit(solution)/shard_map/ppermute | solution.py:324
  10.2 0.6 %collective-permute-done.4.refs_0_.beyond_front = bf16[2,2,128,128]{3,2,1,0:T(8,128)(2,1)S(1)} collective-permute-done((bf16[2,2,128,128]{3,2,1,0:T(8,128)(2,1)S(1)}, bf16[2,2,128,128]{3,2,1,0:T(8,128)(2,1)S(1)}, u32[]{:S(2)}, u32[]{:S(2)}) %collective-permute-start.4) | collective-permute-done | bytes 131104 | tf_op jit(solution)/shard_map/ppermute | solution.py:324
  10.8 0.8 %shard_map.59.ahead = bf16[2,2,128,128]{3,2,1,0:T(8,128)(2,1)S(1)} custom-call(bf16[2,2,128,128]{3,2,1,0:T(8,128)(2,1)S(1)} %collective-permute-done.4.refs_0_.beyond_front, bf16[2,2,128,128]{3,2,1,0:T(8,128)(2,1)S(1)} %collective-permute-done.5.refs_1_.beyond_late, bf16[2,2,128,128]{3,2,1,0:T(8,128)(2,1)S(1)} %get-tuple-element.23.refs_0_.front.refs_2_, ...), custom_call_target="tpu_custom_call" | custom-call | flops 1000 | bytes 1000 | tf_op jit(solution)/shard_map/pallas_call | solution.py:337
  11.7 0.1 collective-permute-start.6
  11.8 1.4 %shard_map.58.partial = f32[2,2,128,256]{3,2,1,0:T(8,128)S(1)} custom-call(bf16[2,2,128,128]{3,2,1,0:T(8,128)(2,1)S(1)} %get-tuple-element.23.refs_0_.front.refs_2_, bf16[2,2,128,128]{3,2,1,0:T(8,128)(2,1)S(1)} %get-tuple-element.24.refs_1_.late.refs_3_, bf16[2,2,128,128]{3,2,1,0:T(8,128)(2,1)S(1)} %get-tuple-element.25.refs_2_.rest_front, ...), custom_call_target="tpu_custom_call" | custom-call | flops 1000 | bytes 1000 | tf_op jit(solution)/shard_map/pallas_call | solution.py:337
  13.3 0.2 collective-permute-done.7.passed_beyond
  13.4 1.5 %shard_map.60 = (bf16[2,128,128]{2,1,0:T(8,128)(2,1)S(1)}, bf16[2,128,128]{2,1,0:T(8,128)(2,1)S(1)}, f32[2,128,256]{2,1,0:T(8,128)S(1)}) custom-call(bf16[2,2,128,128]{3,2,1,0:T(8,128)(2,1)S(1)} %get-tuple-element.23.refs_0_.front.refs_2_, bf16[2,2,128,128]{3,2,1,0:T(8,128)(2,1)S(1)} %get-tuple-element.24.refs_1_.late.refs_3_, ...), custom_call_target="tpu_custom_call" | custom-call | flops 1000 | bytes 1000 | tf_op jit(solution)/shard_map/pallas_call | solution.py:337
  14.9 2.0 %collective-permute-done.6.handed_outer = bf16[2,2,128,128]{3,2,1,0:T(8,128)(2,1)S(1)} collective-permute-done((bf16[2,2,128,128]{3,2,1,0:T(8,128)(2,1)S(1)}, bf16[2,2,128,128]{3,2,1,0:T(8,128)(2,1)S(1)}, u32[]{:S(2)}, u32[]{:S(2)}) %collective-permute-start.6) | collective-permute-done | bytes 131104 | tf_op jit(solution)/shard_map/ppermute | solution.py:309
  16.9 0.1 shard_map.61
  16.9 0.1 collective-permute-start.8
  17.0 1.3 %collective-permute-done.8.taken = bf16[2,2,128,128]{3,2,1,0:T(8,128)(2,1)S(1)} collective-permute-done((bf16[2,2,128,128]{3,2,1,0:T(8,128)(2,1)S(1)}, bf16[2,2,128,128]{3,2,1,0:T(8,128)(2,1)S(1)}, u32[]{:S(2)}, u32[]{:S(2)}) %collective-permute-start.8) | collective-permute-done | bytes 131104 | tf_op jit(solution)/shard_map/ppermute | solution.py:309
  18.4 0.7 %shard_map.62 = bf16[2,4,128,128]{3,2,1,0:T(8,128)(2,1)} custom-call(bf16[2,2,128,128]{3,2,1,0:T(8,128)(2,1)S(1)} %get-tuple-element.39.kept, bf16[2,2,128,128]{3,2,1,0:T(8,128)(2,1)S(1)} %collective-permute-done.8.taken), custom_call_target="tpu_custom_call" | custom-call | flops 1000 | bytes 1000 | tf_op jit(solution)/shard_map/pallas_call | solution.py:337
  (4 shorter events, 0.0 us)
Async XLA Ops:
  1.3 5.1 %collective-permute-start = (bf16[1744,128]{1,0:T(8,128)(2,1)S(1)}, bf16[1744,128]{1,0:T(8,128)(2,1)S(1)}, u32[]{:S(2)}, u32[]{:S(2)}) collective-permute-start(bf16[1744,128]{1,0:T(8,128)(2,1)S(1)} %get-tuple-element.27.own), channel_id=1, source_target_pairs={{0,1},{1,0},{2,3},{3,2},{4,5},{5,4},{6,7},{7,6},{8,9},{9,8},{10,11... | collective-permute-start | bytes 1339400 | tf_op jit(solution)/shard_map/ppermute | solution.py:309
  1.8 6.7 %collective-permute-start.2 = (bf16[2,2,128,128]{3,2,1,0:T(8,128)(2,1)S(1)}, bf16[2,2,128,128]{3,2,1,0:T(8,128)(2,1)S(1)}, u32[]{:S(2)}, u32[]{:S(2)}) collective-permute-start(bf16[2,2,128,128]{3,2,1,0:T(8,128)(2,1)S(1)} %get-tuple-element.24.refs_1_.late.refs_3_), channel_id=1, source_target_pairs={{0,2},{2,0},{1,3},{3,1},{4,6},{6,4},{5,7},{7,5},{8,10},{10,8},{9,1... | collective-permute-start | bytes 393224 | tf_op jit(solution)/shard_map/ppermute | solution.py:309
  4.4 5.9 %collective-permute-start.5 = (bf16[2,2,128,128]{3,2,1,0:T(8,128)(2,1)S(1)}, bf16[2,2,128,128]{3,2,1,0:T(8,128)(2,1)S(1)}, u32[]{:S(2)}, u32[]{:S(2)}) collective-permute-start(bf16[2,2,128,128]{3,2,1,0:T(8,128)(2,1)S(1)} %get-tuple-element.24.refs_1_.late.refs_3_), channel_id=1, source_target_pairs={{1,5},{5,1},{4,8},{8,4},{9,13},{13,9},{0,16},{12,28},{17,21},{21,1... | collective-permute-start | bytes 393224 | tf_op jit(solution)/shard_map/ppermute | solution.py:324
  5.9 5.0 %collective-permute-start.4 = (bf16[2,2,128,128]{3,2,1,0:T(8,128)(2,1)S(1)}, bf16[2,2,128,128]{3,2,1,0:T(8,128)(2,1)S(1)}, u32[]{:S(2)}, u32[]{:S(2)}) collective-permute-start(bf16[2,2,128,128]{3,2,1,0:T(8,128)(2,1)S(1)} %get-tuple-element.23.refs_0_.front.refs_2_), channel_id=1, source_target_pairs={{1,5},{5,1},{4,8},{8,4},{9,13},{13,9},{0,16},{12,28},{17,21},{21,1... | collective-permute-start | bytes 393224 | tf_op jit(solution)/shard_map/ppermute | solution.py:324
  6.7 5.1 %copy-start = (bf16[3,3,3,128,256]{4,3,2,1,0:T(8,128)(2,1)S(1)}, bf16[3,3,3,128,256]{4,3,2,1,0:T(8,128)(2,1)}, u32[]{:S(2)}) copy-start(bf16[3,3,3,128,256]{4,3,2,1,0:T(8,128)(2,1)} %second.5) | copy-start | bytes 5308420
  7.6 5.7 %collective-permute-start.1 = (bf16[528,128]{1,0:T(8,128)(2,1)S(1)}, bf16[528,128]{1,0:T(8,128)(2,1)S(1)}, u32[]{:S(2)}, u32[]{:S(2)}) collective-permute-start(bf16[528,128]{1,0:T(8,128)(2,1)S(1)} %get-tuple-element.30), channel_id=1, source_target_pairs={{0,2},{2,0},{1,3},{3,1},{4,6},{6,4},{5,7},{7,5},{8,10},{10,8},{9,1... | collective-permute-start | bytes 405512 | tf_op jit(solution)/shard_map/ppermute | solution.py:309
  8.5 3.4 %collective-permute-start.3 = (bf16[2,2,128,128]{3,2,1,0:T(8,128)(2,1)S(1)}, bf16[2,2,128,128]{3,2,1,0:T(8,128)(2,1)S(1)}, u32[]{:S(2)}, u32[]{:S(2)}) collective-permute-start(bf16[2,2,128,128]{3,2,1,0:T(8,128)(2,1)S(1)} %collective-permute-done.2.passed), channel_id=1, source_target_pairs={{0,1},{1,0},{2,3},{3,2},{4,5},{5,4},{6,7},{7,6},{8,9},{9,8},{10,11... | collective-permute-start | bytes 393224 | tf_op jit(solution)/shard_map/ppermute | solution.py:309
  8.5 5.0 %collective-permute-start.7 = (bf16[2,2,128,128]{3,2,1,0:T(8,128)(2,1)S(1)}, bf16[2,2,128,128]{3,2,1,0:T(8,128)(2,1)S(1)}, u32[]{:S(2)}, u32[]{:S(2)}) collective-permute-start(bf16[2,2,128,128]{3,2,1,0:T(8,128)(2,1)S(1)} %collective-permute-done.2.passed), channel_id=1, source_target_pairs={{1,5},{5,1},{4,8},{8,4},{9,13},{13,9},{0,16},{12,28},{17,21},{21,1... | collective-permute-start | bytes 393224 | tf_op jit(solution)/shard_map/ppermute | solution.py:324
  11.7 5.1 %collective-permute-start.6 = (bf16[2,2,128,128]{3,2,1,0:T(8,128)(2,1)S(1)}, bf16[2,2,128,128]{3,2,1,0:T(8,128)(2,1)S(1)}, u32[]{:S(2)}, u32[]{:S(2)}) collective-permute-start(bf16[2,2,128,128]{3,2,1,0:T(8,128)(2,1)S(1)} %shard_map.59.ahead), channel_id=1, source_target_pairs={{0,2},{2,0},{1,3},{3,1},{4,6},{6,4},{5,7},{7,5},{8,10},{10,8},{9,1... | collective-permute-start | bytes 393224 | tf_op jit(solution)/shard_map/ppermute | solution.py:309
  16.9 1.4 %collective-permute-start.8 = (bf16[2,2,128,128]{3,2,1,0:T(8,128)(2,1)S(1)}, bf16[2,2,128,128]{3,2,1,0:T(8,128)(2,1)S(1)}, u32[]{:S(2)}, u32[]{:S(2)}) collective-permute-start(bf16[2,2,128,128]{3,2,1,0:T(8,128)(2,1)S(1)} %get-tuple-element.40), channel_id=1, source_target_pairs={{0,1},{1,0},{2,3},{3,2},{4,5},{5,4},{6,7},{7,6},{8,9},{9,8},{10,11... | collective-permute-start | bytes 393224 | tf_op jit(solution)/shard_map/ppermute | solution.py:309

commit v7 on v6

--- a/solution.py
+++ b/solution.py
@@ -79,13 +79,14 @@
         copy.wait()
 
 
-def join_kernel(kept, taken, latents, sems):
+def join_kernel(*refs):
+    *parts, latents, sems = refs
     lower = lower_half()
-    half = kept.shape[1]
-    copies = [
-        pltpu.make_async_copy(part, latents.at[:, pl.ds(place * half, half)], sems.at[k])
-        for k, (part, place) in enumerate(((kept, lower), (taken, 1 - lower)))
-    ]
+    half = parts[0].shape[0]
+    copies = []
+    for k, part in enumerate(parts):
+        place = lower if k % 2 == 0 else 1 - lower
+        copies.append(pltpu.make_async_copy(part, latents.at[k // 2, pl.ds(place * half, half)], sems.at[k]))
     for copy in copies:
         copy.start()
     for copy in copies:
@@ -278,13 +279,11 @@
 
 
 def last_kernel(
-    handed_inner, handed_outer, second, bias_second, left, kept_second, given_second, kept, given
+    handed_inner, handed_outer, second, bias_second, left, kept, given
 ):
     lower = lower_half()
     follows = lax.axis_index("slab") > 0
     frames = [(0, 0), (1, 1)]
-    kept[1] = kept_second[...]
-    given[1] = given_second[...]
 
     @pl.when(follows)
     def _():
@@ -296,12 +295,12 @@
         inner_both, inner_one = terms_of(inner, frames, lower)
         outer_both, outer_one = terms_of(lambda n, j: handed_outer[n, j], frames, 1 - lower)
         for row, terms in ((1 - lower, inner_both + outer_one), (lower, outer_both + inner_one)):
-            finish(left[row] + second_layer(terms, second), bias_second, row, kept.at[0], given.at[0])
+            finish(left[row] + second_layer(terms, second), bias_second, row, kept, given)
 
     @pl.when(jnp.logical_not(follows))
     def _():
         for row in range(left.shape[0]):
-            finish(left[row], bias_second, row, kept.at[0], given.at[0])
+            finish(left[row], bias_second, row, kept, given)
 
 
 def cycle(value, axis):
@@ -411,20 +410,17 @@
         [pltpu.VMEM((early + 1, half, columns, width), bf16)],
         front, late, beyond_front, beyond_late, passed, passed_beyond, packed, bias_first, ahead_outer, second_weight, bias_last, partial,
     )
-    whole = shape((early,) + part.shape, bf16)
-    kept, given = call(
-        last_kernel,
-        [whole, whole],
-        [VMEM] * 7,
-        [],
-        handed_inner, handed_outer, second_weight, bias_last, left, kept_second, given_second,
+    taken_second = cycle(given_second, "chan")
+    left, taken_second = lax.optimization_barrier((left, taken_second))
+    kept_first, given_first = call(
+        last_kernel, [part, part], [VMEM] * 5, [], handed_inner, handed_outer, second_weight, bias_last, left
     )
     (latents,) = call(
         join_kernel,
         [shape((early, rows, columns, second_bias.shape[0]), bf16)],
-        [VMEM] * 2,
-        [pltpu.SemaphoreType.DMA((2,))],
-        kept, cycle(given, "chan"),
+        [VMEM] * 4,
+        [pltpu.SemaphoreType.DMA((4,))],
+        kept_first, cycle(given_first, "chan"), kept_second, taken_second,
         out_specs=[ANY],
     )
     return latents

time: 19.2 us -> 19.1 us (level)
    ppermute x6 -> x7, waiting for transfers between devices: 4.09 us -> 3.92 us  [cycle(): lax.ppermute(value, axis, [(i, (i + 1) % count) for i in range(count)])]
    ppermute x6 -> x7, starting transfers between devices: 3.36 us -> 3.43 us  [cycle(): lax.ppermute(value, axis, [(i, (i + 1) % count) for i in range(count)])]
  transfers between devices with their start and end apart: 9 -> 10, of which waited for: 5 -> 6; matrix products, arithmetic and copies ran while one was open for 0% -> 0% of each run, Pallas kernels for 26% -> 26%
where the time goes in v7:
time: 19.1 us; the launch traced here: 19 us
  starting transfers between devices  7.24 us (38%)
  Pallas kernels  6.95 us (36%)
  waiting for transfers between devices  4.68 us (25%)
    pallas_call x8, Pallas kernels, call(): pl.pallas_call(kernel, out_shape=outs, in_specs=ins, out_specs=[VMEM] * l...  6.95 us
    ppermute x7, waiting for transfers between devices, cycle(): lax.ppermute(value, axis, [(i, (i + 1) % count) for i in range(count)])  3.92 us
    ppermute x3, starting transfers between devices, across_border(): return lax.ppermute(value, ('clip', 'tile', 'chan'), pairs)  3.81 us
    ppermute x7, starting transfers between devices, cycle(): lax.ppermute(value, axis, [(i, (i + 1) % count) for i in range(count)])  3.43 us
    ppermute x3, waiting for transfers between devices, across_border(): return lax.ppermute(value, ('clip', 'tile', 'chan'), pairs)  0.76 us
  transfers between devices with their start and end apart: 10, of which 6 were waited for; matrix products, arithmetic and copies ran while one was open for 0% of the time, Pallas kernels for 26%

profile of v7, /device:TPU:0, one launch (start us, length us, event | category | flops | bytes accessed | tf_op | source)
XLA Modules:
  0.0 19.0 jit_solution(14845464817838451678)
XLA Ops:
  0.0 1.3 %shard_map.55 = (bf16[2,2,128,128]{3,2,1,0:T(8,128)(2,1)S(1)}, bf16[2,2,128,128]{3,2,1,0:T(8,128)(2,1)S(1)}, bf16[2,2,128,128]{3,2,1,0:T(8,128)(2,1)S(1)}, bf16[...) custom-call(bf16[4,4,128,128]{3,2,1,0:T(8,128)(2,1)} %video.1, bf16[1728,128]{1,0:T(8,128)(2,1)} %bitcast.5, ...), custom_call_target="tpu_custom_call" | custom-call | flops 1000 | bytes 1000 | tf_op jit(solution)/shard_map/pallas_call | solution.py:336
  1.3 0.5 %collective-permute-start = (bf16[1744,128]{1,0:T(8,128)(2,1)S(1)}, bf16[1744,128]{1,0:T(8,128)(2,1)S(1)}, u32[]{:S(2)}, u32[]{:S(2)}) collective-permute-start(bf16[1744,128]{1,0:T(8,128)(2,1)S(1)} %get-tuple-element.29.own), channel_id=1, source_target_pairs={{0,1},{1,0},{2,3},{3,2},{4,5},{5,4},{6,7},{7,6},{8,9},{9,8},{10,11... | collective-permute-start | bytes 1339400 | tf_op jit(solution)/shard_map/ppermute | solution.py:308
  1.8 2.6 %collective-permute-start.2 = (bf16[2,2,128,128]{3,2,1,0:T(8,128)(2,1)S(1)}, bf16[2,2,128,128]{3,2,1,0:T(8,128)(2,1)S(1)}, u32[]{:S(2)}, u32[]{:S(2)}) collective-permute-start(bf16[2,2,128,128]{3,2,1,0:T(8,128)(2,1)S(1)} %get-tuple-element.26.refs_1_.late.refs_3_), channel_id=1, source_target_pairs={{0,2},{2,0},{1,3},{3,1},{4,6},{6,4},{5,7},{7,5},{8,10},{10,8},{9,1... | collective-permute-start | bytes 393224 | tf_op jit(solution)/shard_map/ppermute | solution.py:308
  4.4 1.5 %collective-permute-start.5 = (bf16[2,2,128,128]{3,2,1,0:T(8,128)(2,1)S(1)}, bf16[2,2,128,128]{3,2,1,0:T(8,128)(2,1)S(1)}, u32[]{:S(2)}, u32[]{:S(2)}) collective-permute-start(bf16[2,2,128,128]{3,2,1,0:T(8,128)(2,1)S(1)} %get-tuple-element.26.refs_1_.late.refs_3_), channel_id=1, source_target_pairs={{1,5},{5,1},{4,8},{8,4},{9,13},{13,9},{0,16},{12,28},{17,21},{21,1... | collective-permute-start | bytes 393224 | tf_op jit(solution)/shard_map/ppermute | solution.py:323
  5.9 0.5 %collective-permute-start.4 = (bf16[2,2,128,128]{3,2,1,0:T(8,128)(2,1)S(1)}, bf16[2,2,128,128]{3,2,1,0:T(8,128)(2,1)S(1)}, u32[]{:S(2)}, u32[]{:S(2)}) collective-permute-start(bf16[2,2,128,128]{3,2,1,0:T(8,128)(2,1)S(1)} %get-tuple-element.25.refs_0_.front.refs_2_), channel_id=1, source_target_pairs={{1,5},{5,1},{4,8},{8,4},{9,13},{13,9},{0,16},{12,28},{17,21},{21,1... | collective-permute-start | bytes 393224 | tf_op jit(solution)/shard_map/ppermute | solution.py:323
  6.4 0.3 %shard_map.56 = (bf16[1536,768]{1,0:T(8,128)(2,1)S(1)}, f32[1,256]{1,0:T(1,128)S(1)}, f32[1,256]{1,0:T(1,128)S(1)}) custom-call(bf16[1744,128]{1,0:T(8,128)(2,1)S(1)} %get-tuple-element.29.own, bf16[1744,128]{1,0:T(8,128)(2,1)S(1)} %collective-permute-done.other), custom_call_target="tpu_custom_call" | custom-call | flops 1000 | bytes 1000 | tf_op jit(solution)/shard_map/pallas_call | solution.py:336
  6.7 0.0 copy-start
  6.7 0.9 %shard_map.57 = (bf16[2,2,128,128]{3,2,1,0:T(8,128)(2,1)S(1)}, bf16[528,128]{1,0:T(8,128)(2,1)S(1)}) custom-call(bf16[2,2,128,128]{3,2,1,0:T(8,128)(2,1)S(1)} %get-tuple-element.25.refs_0_.front.refs_2_, bf16[2,2,128,128]{3,2,1,0:T(8,128)(2,1)S(1)} %get-tuple-element.26.refs_1_.late.refs_3_, ...), custom_call_target="tpu_custom_call" | custom-call | flops 1000 | bytes 1000 | tf_op jit(solution)/shard_map/pallas_call | solution.py:336
  7.6 0.1 collective-permute-start.1
  7.7 0.8 %collective-permute-done.2.passed = bf16[2,2,128,128]{3,2,1,0:T(8,128)(2,1)S(1)} collective-permute-done((bf16[2,2,128,128]{3,2,1,0:T(8,128)(2,1)S(1)}, bf16[2,2,128,128]{3,2,1,0:T(8,128)(2,1)S(1)}, u32[]{:S(2)}, u32[]{:S(2)}) %collective-permute-start.2) | collective-permute-done | bytes 131104 | tf_op jit(solution)/shard_map/ppermute | solution.py:308
  8.5 1.8 %collective-permute-start.7 = (bf16[2,2,128,128]{3,2,1,0:T(8,128)(2,1)S(1)}, bf16[2,2,128,128]{3,2,1,0:T(8,128)(2,1)S(1)}, u32[]{:S(2)}, u32[]{:S(2)}) collective-permute-start(bf16[2,2,128,128]{3,2,1,0:T(8,128)(2,1)S(1)} %collective-permute-done.2.passed), channel_id=1, source_target_pairs={{1,5},{5,1},{4,8},{8,4},{9,13},{13,9},{0,16},{12,28},{17,21},{21,1... | collective-permute-start | bytes 393224 | tf_op jit(solution)/shard_map/ppermute | solution.py:323
  10.2 0.6 %collective-permute-done.4.refs_0_.beyond_front = bf16[2,2,128,128]{3,2,1,0:T(8,128)(2,1)S(1)} collective-permute-done((bf16[2,2,128,128]{3,2,1,0:T(8,128)(2,1)S(1)}, bf16[2,2,128,128]{3,2,1,0:T(8,128)(2,1)S(1)}, u32[]{:S(2)}, u32[]{:S(2)}) %collective-permute-start.4) | collective-permute-done | bytes 131104 | tf_op jit(solution)/shard_map/ppermute | solution.py:323
  10.8 0.8 %shard_map.59.ahead = bf16[2,2,128,128]{3,2,1,0:T(8,128)(2,1)S(1)} custom-call(bf16[2,2,128,128]{3,2,1,0:T(8,128)(2,1)S(1)} %collective-permute-done.4.refs_0_.beyond_front, bf16[2,2,128,128]{3,2,1,0:T(8,128)(2,1)S(1)} %collective-permute-done.5.refs_1_.beyond_late, bf16[2,2,128,128]{3,2,1,0:T(8,128)(2,1)S(1)} %get-tuple-element.25.refs_0_.front.refs_2_, ...), custom_call_target="tpu_custom_call" | custom-call | flops 1000 | bytes 1000 | tf_op jit(solution)/shard_map/pallas_call | solution.py:336
  11.7 0.1 collective-permute-start.6
  11.8 1.4 %shard_map.58.partial = f32[2,2,128,256]{3,2,1,0:T(8,128)S(1)} custom-call(bf16[2,2,128,128]{3,2,1,0:T(8,128)(2,1)S(1)} %get-tuple-element.25.refs_0_.front.refs_2_, bf16[2,2,128,128]{3,2,1,0:T(8,128)(2,1)S(1)} %get-tuple-element.26.refs_1_.late.refs_3_, bf16[2,2,128,128]{3,2,1,0:T(8,128)(2,1)S(1)} %get-tuple-element.27.refs_2_.rest_front, ...), custom_call_target="tpu_custom_call" | custom-call | flops 1000 | bytes 1000 | tf_op jit(solution)/shard_map/pallas_call | solution.py:336
  13.3 0.2 collective-permute-done.7.passed_beyond
  13.4 1.5 %shard_map.60 = (bf16[2,128,128]{2,1,0:T(8,128)(2,1)S(1)}, bf16[2,128,128]{2,1,0:T(8,128)(2,1)S(1)}, f32[2,128,256]{2,1,0:T(8,128)S(1)}) custom-call(bf16[2,2,128,128]{3,2,1,0:T(8,128)(2,1)S(1)} %get-tuple-element.25.refs_0_.front.refs_2_, bf16[2,2,128,128]{3,2,1,0:T(8,128)(2,1)S(1)} %get-tuple-element.26.refs_1_.late.refs_3_, ...), custom_call_target="tpu_custom_call" | custom-call | flops 1000 | bytes 1000 | tf_op jit(solution)/shard_map/pallas_call | solution.py:336
  14.9 0.1 collective-permute-start.8
  15.0 1.2 %collective-permute-done.8.refs_3_ = bf16[2,128,128]{2,1,0:T(8,128)(2,1)S(1)} collective-permute-done((bf16[2,128,128]{2,1,0:T(8,128)(2,1)S(1)}, bf16[2,128,128]{2,1,0:T(8,128)(2,1)S(1)}, u32[]{:S(2)}, u32[]{:S(2)}) %collective-permute-start.8) | collective-permute-done | bytes 65568 | tf_op jit(solution)/shard_map/ppermute | solution.py:308
  16.2 0.6 %collective-permute-done.6.handed_outer = bf16[2,2,128,128]{3,2,1,0:T(8,128)(2,1)S(1)} collective-permute-done((bf16[2,2,128,128]{3,2,1,0:T(8,128)(2,1)S(1)}, bf16[2,2,128,128]{3,2,1,0:T(8,128)(2,1)S(1)}, u32[]{:S(2)}, u32[]{:S(2)}) %collective-permute-start.6) | collective-permute-done | bytes 131104 | tf_op jit(solution)/shard_map/ppermute | solution.py:308
  16.9 0.1 shard_map.61
  16.9 0.1 collective-permute-start.9
  17.0 1.2 %collective-permute-done.9.refs_1_ = bf16[2,128,128]{2,1,0:T(8,128)(2,1)S(1)} collective-permute-done((bf16[2,128,128]{2,1,0:T(8,128)(2,1)S(1)}, bf16[2,128,128]{2,1,0:T(8,128)(2,1)S(1)}, u32[]{:S(2)}, u32[]{:S(2)}) %collective-permute-start.9) | collective-permute-done | bytes 65568 | tf_op jit(solution)/shard_map/ppermute | solution.py:308
  18.2 0.7 %shard_map.62 = bf16[2,4,128,128]{3,2,1,0:T(8,128)(2,1)} custom-call(bf16[2,128,128]{2,1,0:T(8,128)(2,1)S(1)} %get-tuple-element.41.refs_0_, bf16[2,128,128]{2,1,0:T(8,128)(2,1)S(1)} %collective-permute-done.9.refs_1_, bf16[2,128,128]{2,1,0:T(8,128)(2,1)S(1)} %get-tuple-element.43.refs_2_, bf16[2,128,128]{2,1,0:T(8,128)(2,1)S(1)} %collective-permute-done.8.refs_3_), custom_call_target="tpu_custom_call" | custom-call | flops 1000 | bytes 1000 | tf_op jit(solution)/shard_map/pallas_call | solution.py:336
  (6 shorter events, 0.0 us)
Async XLA Ops:
  1.3 5.1 %collective-permute-start = (bf16[1744,128]{1,0:T(8,128)(2,1)S(1)}, bf16[1744,128]{1,0:T(8,128)(2,1)S(1)}, u32[]{:S(2)}, u32[]{:S(2)}) collective-permute-start(bf16[1744,128]{1,0:T(8,128)(2,1)S(1)} %get-tuple-element.29.own), channel_id=1, source_target_pairs={{0,1},{1,0},{2,3},{3,2},{4,5},{5,4},{6,7},{7,6},{8,9},{9,8},{10,11... | collective-permute-start | bytes 1339400 | tf_op jit(solution)/shard_map/ppermute | solution.py:308
  1.8 6.7 %collective-permute-start.2 = (bf16[2,2,128,128]{3,2,1,0:T(8,128)(2,1)S(1)}, bf16[2,2,128,128]{3,2,1,0:T(8,128)(2,1)S(1)}, u32[]{:S(2)}, u32[]{:S(2)}) collective-permute-start(bf16[2,2,128,128]{3,2,1,0:T(8,128)(2,1)S(1)} %get-tuple-element.26.refs_1_.late.refs_3_), channel_id=1, source_target_pairs={{0,2},{2,0},{1,3},{3,1},{4,6},{6,4},{5,7},{7,5},{8,10},{10,8},{9,1... | collective-permute-start | bytes 393224 | tf_op jit(solution)/shard_map/ppermute | solution.py:308
  4.4 5.9 %collective-permute-start.5 = (bf16[2,2,128,128]{3,2,1,0:T(8,128)(2,1)S(1)}, bf16[2,2,128,128]{3,2,1,0:T(8,128)(2,1)S(1)}, u32[]{:S(2)}, u32[]{:S(2)}) collective-permute-start(bf16[2,2,128,128]{3,2,1,0:T(8,128)(2,1)S(1)} %get-tuple-element.26.refs_1_.late.refs_3_), channel_id=1, source_target_pairs={{1,5},{5,1},{4,8},{8,4},{9,13},{13,9},{0,16},{12,28},{17,21},{21,1... | collective-permute-start | bytes 393224 | tf_op jit(solution)/shard_map/ppermute | solution.py:323
  5.9 5.0 %collective-permute-start.4 = (bf16[2,2,128,128]{3,2,1,0:T(8,128)(2,1)S(1)}, bf16[2,2,128,128]{3,2,1,0:T(8,128)(2,1)S(1)}, u32[]{:S(2)}, u32[]{:S(2)}) collective-permute-start(bf16[2,2,128,128]{3,2,1,0:T(8,128)(2,1)S(1)} %get-tuple-element.25.refs_0_.front.refs_2_), channel_id=1, source_target_pairs={{1,5},{5,1},{4,8},{8,4},{9,13},{13,9},{0,16},{12,28},{17,21},{21,1... | collective-permute-start | bytes 393224 | tf_op jit(solution)/shard_map/ppermute | solution.py:323
  6.7 5.1 %copy-start = (bf16[3,3,3,128,256]{4,3,2,1,0:T(8,128)(2,1)S(1)}, bf16[3,3,3,128,256]{4,3,2,1,0:T(8,128)(2,1)}, u32[]{:S(2)}) copy-start(bf16[3,3,3,128,256]{4,3,2,1,0:T(8,128)(2,1)} %second.5) | copy-start | bytes 5308420
  7.6 5.7 %collective-permute-start.1 = (bf16[528,128]{1,0:T(8,128)(2,1)S(1)}, bf16[528,128]{1,0:T(8,128)(2,1)S(1)}, u32[]{:S(2)}, u32[]{:S(2)}) collective-permute-start(bf16[528,128]{1,0:T(8,128)(2,1)S(1)} %get-tuple-element.32), channel_id=1, source_target_pairs={{0,2},{2,0},{1,3},{3,1},{4,6},{6,4},{5,7},{7,5},{8,10},{10,8},{9,1... | collective-permute-start | bytes 405512 | tf_op jit(solution)/shard_map/ppermute | solution.py:308
  8.5 3.4 %collective-permute-start.3 = (bf16[2,2,128,128]{3,2,1,0:T(8,128)(2,1)S(1)}, bf16[2,2,128,128]{3,2,1,0:T(8,128)(2,1)S(1)}, u32[]{:S(2)}, u32[]{:S(2)}) collective-permute-start(bf16[2,2,128,128]{3,2,1,0:T(8,128)(2,1)S(1)} %collective-permute-done.2.passed), channel_id=1, source_target_pairs={{0,1},{1,0},{2,3},{3,2},{4,5},{5,4},{6,7},{7,6},{8,9},{9,8},{10,11... | collective-permute-start | bytes 393224 | tf_op jit(solution)/shard_map/ppermute | solution.py:308
  8.5 5.0 %collective-permute-start.7 = (bf16[2,2,128,128]{3,2,1,0:T(8,128)(2,1)S(1)}, bf16[2,2,128,128]{3,2,1,0:T(8,128)(2,1)S(1)}, u32[]{:S(2)}, u32[]{:S(2)}) collective-permute-start(bf16[2,2,128,128]{3,2,1,0:T(8,128)(2,1)S(1)} %collective-permute-done.2.passed), channel_id=1, source_target_pairs={{1,5},{5,1},{4,8},{8,4},{9,13},{13,9},{0,16},{12,28},{17,21},{21,1... | collective-permute-start | bytes 393224 | tf_op jit(solution)/shard_map/ppermute | solution.py:323
  11.7 5.1 %collective-permute-start.6 = (bf16[2,2,128,128]{3,2,1,0:T(8,128)(2,1)S(1)}, bf16[2,2,128,128]{3,2,1,0:T(8,128)(2,1)S(1)}, u32[]{:S(2)}, u32[]{:S(2)}) collective-permute-start(bf16[2,2,128,128]{3,2,1,0:T(8,128)(2,1)S(1)} %shard_map.59.ahead), channel_id=1, source_target_pairs={{0,2},{2,0},{1,3},{3,1},{4,6},{6,4},{5,7},{7,5},{8,10},{10,8},{9,1... | collective-permute-start | bytes 393224 | tf_op jit(solution)/shard_map/ppermute | solution.py:308
  14.9 1.3 %collective-permute-start.8 = (bf16[2,128,128]{2,1,0:T(8,128)(2,1)S(1)}, bf16[2,128,128]{2,1,0:T(8,128)(2,1)S(1)}, u32[]{:S(2)}, u32[]{:S(2)}) collective-permute-start(bf16[2,128,128]{2,1,0:T(8,128)(2,1)S(1)} %get-tuple-element.39), channel_id=1, source_target_pairs={{0,1},{1,0},{2,3},{3,2},{4,5},{5,4},{6,7},{7,6},{8,9},{9,8},{10,11... | collective-permute-start | bytes 196616 | tf_op jit(solution)/shard_map/ppermute | solution.py:308
  16.9 1.3 %collective-permute-start.9 = (bf16[2,128,128]{2,1,0:T(8,128)(2,1)S(1)}, bf16[2,128,128]{2,1,0:T(8,128)(2,1)S(1)}, u32[]{:S(2)}, u32[]{:S(2)}) collective-permute-start(bf16[2,128,128]{2,1,0:T(8,128)(2,1)S(1)} %get-tuple-element.42), channel_id=1, source_target_pairs={{0,1},{1,0},{2,3},{3,2},{4,5},{5,4},{6,7},{7,6},{8,9},{9,8},{10,11... | collective-permute-start | bytes 196616 | tf_op jit(solution)/shard_map/ppermute | solution.py:308

commit v8 on v7

--- a/solution.py
+++ b/solution.py
@@ -51,7 +51,7 @@
     return [high, middle, (left - middle.astype(jnp.float32)).astype(jnp.bfloat16)]
 
 
-def stage_kernel(video, weight, first_bias, second_bias, front, late, rest_front, rest_late, staged, first_line, second_line, sems):
+def stage_kernel(video, weight, first_bias, second_bias, front, late, rest, staged, first_line, second_line, sems):
     lower = lower_half()
     early, half = front.shape[:2]
     size = weight.shape[0]
@@ -61,8 +61,7 @@
         (weight, staged.at[0:size]),
         (video.at[early:, pl.ds(lower * half, half)], late),
         (video.at[:early, pl.ds(lower * half, half)], front),
-        (video.at[early:, pl.ds((1 - lower) * half, half)], rest_late),
-        (video.at[:early, pl.ds((1 - lower) * half, half)], rest_front),
+        (video.at[:, pl.ds((1 - lower) * half, half)], rest),
     )
     copies = [pltpu.make_async_copy(source, target, sems.at[k]) for k, (source, target) in enumerate(pairs)]
     for copy in copies:
@@ -188,11 +187,12 @@
 def ahead_kernel(*refs, border):
     early_first, late_first, early_second, late_second, packed, bias, hidden, *sent = refs
     early, half, columns = early_first.shape[:3]
+    ahead = late_second.shape[0] - early
     unknown = [border_known()] if border else []
 
     def tile(f, k):
         first, second = (early_first, early_second) if f < early else (late_first, late_second)
-        return masked(first[f % early, k], *unknown) if k < half else second[f % early, k - half]
+        return masked(first[f % early, k], *unknown) if k < half else second[f % early + (ahead if f >= early else 0), k - half]
 
     @pl.when(jnp.logical_not(last_slab()))
     def _():
@@ -217,7 +217,8 @@
     def tile(f, k):
         if f >= early:
             part = (first if k < half else second)[f // early - 1]
-            return masked(part[f % early, k % half], *(unknown if k < half else []))
+            at = f % early + (part.shape[0] - early if f >= 2 * early else 0)
+            return masked(part[at, k % half], *(unknown if k < half else []))
         if k < half:
             return masked(passed_first[f, k], follows, *unknown)
         return masked(passed_second[f, k - half], follows)
@@ -347,20 +348,19 @@
     short = shape((early, half, columns, width), bf16)
     turned = jnp.swapaxes(first_weight, 3, 4).reshape(-1, width)
     far = lambda value: pltpu.with_memory_space_constraint(value, pltpu.HBM)
-    front, late, rest_front, rest_late, staged = call(
+    front, late, rest, staged = call(
         stage_kernel,
         [
             pltpu.VMEM(short.shape, bf16),
             pltpu.VMEM(short.shape, bf16),
-            pltpu.VMEM(short.shape, bf16),
-            pltpu.VMEM(short.shape, bf16),
+            pltpu.VMEM((frames,) + short.shape[1:], bf16),
             pltpu.VMEM((turned.shape[0] + TAIL, width), bf16),
         ],
         [HBM] * 4,
         [
             pltpu.VMEM((1, first_bias.shape[0]), jnp.float32),
             pltpu.VMEM((1, second_bias.shape[0]), jnp.float32),
-            pltpu.SemaphoreType.DMA((7,)),
+            pltpu.SemaphoreType.DMA((6,)),
         ],
         far(video), far(turned), far(first_bias.reshape(1, -1)), far(second_bias.reshape(1, -1)),
     )
@@ -379,7 +379,7 @@
     ahead_inner, sent = call(
         functools.partial(ahead_kernel, border=False),
         [short, shape((early * half * columns + SPARE, width), bf16)],
-        [VMEM] * 6, [], front, late, rest_front, rest_late,
+        [VMEM] * 6, [], front, late, rest, rest,
         packed, bias_first
     )
     handed_inner = cycle(sent, "slab")
@@ -399,7 +399,7 @@
         [shape((early, half, columns, channels), jnp.float32)],
         [VMEM] * 10,
         [pltpu.VMEM((early + 1, half, columns, width), bf16)],
-        front, late, rest_front, rest_late, passed, passed_other, packed, bias_first, ahead_inner, second_weight,
+        front, late, rest, rest, passed, passed_other, packed, bias_first, ahead_inner, second_weight,
     )
     part = shape((half, columns, second_bias.shape[0]), bf16)
     handed_inner, partial = lax.optimization_barrier((handed_inner, partial))

time: 19.1 us -> 19.1 us (level)
  no operation moved by 1% of the time
where the time goes in v8:
time: 19.1 us; the launch traced here: 19 us
  starting transfers between devices  7.25 us (38%)
  Pallas kernels  6.92 us (36%)
  waiting for transfers between devices  4.69 us (25%)
    pallas_call x8, Pallas kernels, call(): pl.pallas_call(kernel, out_shape=outs, in_specs=ins, out_specs=[VMEM] * l...  6.92 us
    ppermute x7, waiting for transfers between devices, cycle(): lax.ppermute(value, axis, [(i, (i + 1) % count) for i in range(count)])  3.93 us
    ppermute x3, starting transfers between devices, across_border(): return lax.ppermute(value, ('clip', 'tile', 'chan'), pairs)  3.81 us
    ppermute x7, starting transfers between devices, cycle(): lax.ppermute(value, axis, [(i, (i + 1) % count) for i in range(count)])  3.44 us
    ppermute x3, waiting for transfers between devices, across_border(): return lax.ppermute(value, ('clip', 'tile', 'chan'), pairs)  0.76 us
  transfers between devices with their start and end apart: 10, of which 6 were waited for; matrix products, arithmetic and copies ran while one was open for 0% of the time, Pallas kernels for 26%

profile of v8, /device:TPU:0, one launch (start us, length us, event | category | flops | bytes accessed | tf_op | source)
XLA Modules:
  0.0 19.0 jit_solution(6104054371755714634)
XLA Ops:
  0.0 1.3 %shard_map.55 = (bf16[2,2,128,128]{3,2,1,0:T(8,128)(2,1)S(1)}, bf16[2,2,128,128]{3,2,1,0:T(8,128)(2,1)S(1)}, bf16[4,2,128,128]{3,2,1,0:T(8,128)(2,1)S(1)}, bf16[1744,128]{1,0:T(8,128)(2,1)S(1)}) custom-call(bf16[4,4,128,128]{3,2,1,0:T(8,128)(2,1)} %video.1, bf16[1728,128]{1,0:T(8,128)(2,1)} %bitcast.5, f32[1,64]{1,0:T(1,128)} %bitcast.6, f32[1,128]{1,0:T(1,128)} %bitcast.7), custom_call_target="tpu_custom_call" | custom-call | flops 1000 | bytes 1000 | tf_op jit(solution)/shard_map/pallas_call | solution.py:337
  1.3 0.5 %collective-permute-start = (bf16[1744,128]{1,0:T(8,128)(2,1)S(1)}, bf16[1744,128]{1,0:T(8,128)(2,1)S(1)}, u32[]{:S(2)}, u32[]{:S(2)}) collective-permute-start(bf16[1744,128]{1,0:T(8,128)(2,1)S(1)} %get-tuple-element.27.own), channel_id=1, source_target_pairs={{0,1},{1,0},{2,3},{3,2},{4,5},{5,4},{6,7},{7,6},{8,9},{9,8},{10,11... | collective-permute-start | bytes 1339400 | tf_op jit(solution)/shard_map/ppermute | solution.py:309
  1.8 2.6 %collective-permute-start.2 = (bf16[2,2,128,128]{3,2,1,0:T(8,128)(2,1)S(1)}, bf16[2,2,128,128]{3,2,1,0:T(8,128)(2,1)S(1)}, u32[]{:S(2)}, u32[]{:S(2)}) collective-permute-start(bf16[2,2,128,128]{3,2,1,0:T(8,128)(2,1)S(1)} %get-tuple-element.25.refs_1_.late.refs_3_), channel_id=1, source_target_pairs={{0,2},{2,0},{1,3},{3,1},{4,6},{6,4},{5,7},{7,5},{8,10},{10,8},{9,1... | collective-permute-start | bytes 393224 | tf_op jit(solution)/shard_map/ppermute | solution.py:309
  4.4 1.5 %collective-permute-start.5 = (bf16[2,2,128,128]{3,2,1,0:T(8,128)(2,1)S(1)}, bf16[2,2,128,128]{3,2,1,0:T(8,128)(2,1)S(1)}, u32[]{:S(2)}, u32[]{:S(2)}) collective-permute-start(bf16[2,2,128,128]{3,2,1,0:T(8,128)(2,1)S(1)} %get-tuple-element.25.refs_1_.late.refs_3_), channel_id=1, source_target_pairs={{1,5},{5,1},{4,8},{8,4},{9,13},{13,9},{0,16},{12,28},{17,21},{21,1... | collective-permute-start | bytes 393224 | tf_op jit(solution)/shard_map/ppermute | solution.py:324
  5.9 0.5 %collective-permute-start.4 = (bf16[2,2,128,128]{3,2,1,0:T(8,128)(2,1)S(1)}, bf16[2,2,128,128]{3,2,1,0:T(8,128)(2,1)S(1)}, u32[]{:S(2)}, u32[]{:S(2)}) collective-permute-start(bf16[2,2,128,128]{3,2,1,0:T(8,128)(2,1)S(1)} %get-tuple-element.24.refs_0_.front.refs_2_), channel_id=1, source_target_pairs={{1,5},{5,1},{4,8},{8,4},{9,13},{13,9},{0,16},{12,28},{17,21},{21,1... | collective-permute-start | bytes 393224 | tf_op jit(solution)/shard_map/ppermute | solution.py:324
  6.4 0.3 %shard_map.56 = (bf16[1536,768]{1,0:T(8,128)(2,1)S(1)}, f32[1,256]{1,0:T(1,128)S(1)}, f32[1,256]{1,0:T(1,128)S(1)}) custom-call(bf16[1744,128]{1,0:T(8,128)(2,1)S(1)} %get-tuple-element.27.own, bf16[1744,128]{1,0:T(8,128)(2,1)S(1)} %collective-permute-done.other), custom_call_target="tpu_custom_call" | custom-call | flops 1000 | bytes 1000 | tf_op jit(solution)/shard_map/pallas_call | solution.py:337
  6.7 0.0 copy-start
  6.7 0.9 %shard_map.57 = (bf16[2,2,128,128]{3,2,1,0:T(8,128)(2,1)S(1)}, bf16[528,128]{1,0:T(8,128)(2,1)S(1)}) custom-call(bf16[2,2,128,128]{3,2,1,0:T(8,128)(2,1)S(1)} %get-tuple-element.24.refs_0_.front.refs_2_, bf16[2,2,128,128]{3,2,1,0:T(8,128)(2,1)S(1)} %get-tuple-element.25.refs_1_.late.refs_3_, ...), custom_call_target="tpu_custom_call" | custom-call | flops 1000 | bytes 1000 | tf_op jit(solution)/shard_map/pallas_call | solution.py:337
  7.6 0.1 collective-permute-start.1
  7.7 0.8 %collective-permute-done.2.passed = bf16[2,2,128,128]{3,2,1,0:T(8,128)(2,1)S(1)} collective-permute-done((bf16[2,2,128,128]{3,2,1,0:T(8,128)(2,1)S(1)}, bf16[2,2,128,128]{3,2,1,0:T(8,128)(2,1)S(1)}, u32[]{:S(2)}, u32[]{:S(2)}) %collective-permute-start.2) | collective-permute-done | bytes 131104 | tf_op jit(solution)/shard_map/ppermute | solution.py:309
  8.5 1.8 %collective-permute-start.7 = (bf16[2,2,128,128]{3,2,1,0:T(8,128)(2,1)S(1)}, bf16[2,2,128,128]{3,2,1,0:T(8,128)(2,1)S(1)}, u32[]{:S(2)}, u32[]{:S(2)}) collective-permute-start(bf16[2,2,128,128]{3,2,1,0:T(8,128)(2,1)S(1)} %collective-permute-done.2.passed), channel_id=1, source_target_pairs={{1,5},{5,1},{4,8},{8,4},{9,13},{13,9},{0,16},{12,28},{17,21},{21,1... | collective-permute-start | bytes 393224 | tf_op jit(solution)/shard_map/ppermute | solution.py:324
  10.2 0.6 %collective-permute-done.4.refs_0_.beyond_front = bf16[2,2,128,128]{3,2,1,0:T(8,128)(2,1)S(1)} collective-permute-done((bf16[2,2,128,128]{3,2,1,0:T(8,128)(2,1)S(1)}, bf16[2,2,128,128]{3,2,1,0:T(8,128)(2,1)S(1)}, u32[]{:S(2)}, u32[]{:S(2)}) %collective-permute-start.4) | collective-permute-done | bytes 131104 | tf_op jit(solution)/shard_map/ppermute | solution.py:324
  10.8 0.8 %shard_map.59.ahead = bf16[2,2,128,128]{3,2,1,0:T(8,128)(2,1)S(1)} custom-call(bf16[2,2,128,128]{3,2,1,0:T(8,128)(2,1)S(1)} %collective-permute-done.4.refs_0_.beyond_front, bf16[2,2,128,128]{3,2,1,0:T(8,128)(2,1)S(1)} %collective-permute-done.5.refs_1_.beyond_late, bf16[2,2,128,128]{3,2,1,0:T(8,128)(2,1)S(1)} %get-tuple-element.24.refs_0_.front.refs_2_, ...), custom_call_target="tpu_custom_call" | custom-call | flops 1000 | bytes 1000 | tf_op jit(solution)/shard_map/pallas_call | solution.py:337
  11.7 0.1 collective-permute-start.6
  11.8 1.4 %shard_map.58.partial = f32[2,2,128,256]{3,2,1,0:T(8,128)S(1)} custom-call(bf16[2,2,128,128]{3,2,1,0:T(8,128)(2,1)S(1)} %get-tuple-element.24.refs_0_.front.refs_2_, bf16[2,2,128,128]{3,2,1,0:T(8,128)(2,1)S(1)} %get-tuple-element.25.refs_1_.late.refs_3_, bf16[4,2,128,128]{3,2,1,0:T(8,128)(2,1)S(1)} %get-tuple-element.26.refs_2_.refs_3_.rest_front.rest_late, ...), custom_call_target="tpu_custom_call" | custom-call | flops 1000 | bytes 1000 | tf_op jit(solution)/shard_map/pallas_call | solution.py:337
  13.3 0.2 collective-permute-done.7.passed_beyond
  13.4 1.5 %shard_map.60 = (bf16[2,128,128]{2,1,0:T(8,128)(2,1)S(1)}, bf16[2,128,128]{2,1,0:T(8,128)(2,1)S(1)}, f32[2,128,256]{2,1,0:T(8,128)S(1)}) custom-call(bf16[2,2,128,128]{3,2,1,0:T(8,128)(2,1)S(1)} %get-tuple-element.24.refs_0_.front.refs_2_, bf16[2,2,128,128]{3,2,1,0:T(8,128)(2,1)S(1)} %get-tuple-element.25.refs_1_.late.refs_3_, ...), custom_call_target="tpu_custom_call" | custom-call | flops 1000 | bytes 1000 | tf_op jit(solution)/shard_map/pallas_call | solution.py:337
  14.9 0.1 collective-permute-start.8
  15.0 1.2 %collective-permute-done.8.refs_3_ = bf16[2,128,128]{2,1,0:T(8,128)(2,1)S(1)} collective-permute-done((bf16[2,128,128]{2,1,0:T(8,128)(2,1)S(1)}, bf16[2,128,128]{2,1,0:T(8,128)(2,1)S(1)}, u32[]{:S(2)}, u32[]{:S(2)}) %collective-permute-start.8) | collective-permute-done | bytes 65568 | tf_op jit(solution)/shard_map/ppermute | solution.py:309
  16.2 0.6 %collective-permute-done.6.handed_outer = bf16[2,2,128,128]{3,2,1,0:T(8,128)(2,1)S(1)} collective-permute-done((bf16[2,2,128,128]{3,2,1,0:T(8,128)(2,1)S(1)}, bf16[2,2,128,128]{3,2,1,0:T(8,128)(2,1)S(1)}, u32[]{:S(2)}, u32[]{:S(2)}) %collective-permute-start.6) | collective-permute-done | bytes 131104 | tf_op jit(solution)/shard_map/ppermute | solution.py:309
  16.8 0.1 shard_map.61
  16.9 0.1 collective-permute-start.9
  17.0 1.2 %collective-permute-done.9.refs_1_ = bf16[2,128,128]{2,1,0:T(8,128)(2,1)S(1)} collective-permute-done((bf16[2,128,128]{2,1,0:T(8,128)(2,1)S(1)}, bf16[2,128,128]{2,1,0:T(8,128)(2,1)S(1)}, u32[]{:S(2)}, u32[]{:S(2)}) %collective-permute-start.9) | collective-permute-done | bytes 65568 | tf_op jit(solution)/shard_map/ppermute | solution.py:309
  18.2 0.7 %shard_map.62 = bf16[2,4,128,128]{3,2,1,0:T(8,128)(2,1)} custom-call(bf16[2,128,128]{2,1,0:T(8,128)(2,1)S(1)} %get-tuple-element.39.refs_0_, bf16[2,128,128]{2,1,0:T(8,128)(2,1)S(1)} %collective-permute-done.9.refs_1_, bf16[2,128,128]{2,1,0:T(8,128)(2,1)S(1)} %get-tuple-element.41.refs_2_, bf16[2,128,128]{2,1,0:T(8,128)(2,1)S(1)} %collective-permute-done.8.refs_3_), custom_call_target="tpu_custom_call" | custom-call | flops 1000 | bytes 1000 | tf_op jit(solution)/shard_map/pallas_call | solution.py:337
  (6 shorter events, 0.0 us)
Async XLA Ops:
  1.3 5.1 %collective-permute-start = (bf16[1744,128]{1,0:T(8,128)(2,1)S(1)}, bf16[1744,128]{1,0:T(8,128)(2,1)S(1)}, u32[]{:S(2)}, u32[]{:S(2)}) collective-permute-start(bf16[1744,128]{1,0:T(8,128)(2,1)S(1)} %get-tuple-element.27.own), channel_id=1, source_target_pairs={{0,1},{1,0},{2,3},{3,2},{4,5},{5,4},{6,7},{7,6},{8,9},{9,8},{10,11... | collective-permute-start | bytes 1339400 | tf_op jit(solution)/shard_map/ppermute | solution.py:309
  1.8 6.7 %collective-permute-start.2 = (bf16[2,2,128,128]{3,2,1,0:T(8,128)(2,1)S(1)}, bf16[2,2,128,128]{3,2,1,0:T(8,128)(2,1)S(1)}, u32[]{:S(2)}, u32[]{:S(2)}) collective-permute-start(bf16[2,2,128,128]{3,2,1,0:T(8,128)(2,1)S(1)} %get-tuple-element.25.refs_1_.late.refs_3_), channel_id=1, source_target_pairs={{0,2},{2,0},{1,3},{3,1},{4,6},{6,4},{5,7},{7,5},{8,10},{10,8},{9,1... | collective-permute-start | bytes 393224 | tf_op jit(solution)/shard_map/ppermute | solution.py:309
  4.4 5.9 %collective-permute-start.5 = (bf16[2,2,128,128]{3,2,1,0:T(8,128)(2,1)S(1)}, bf16[2,2,128,128]{3,2,1,0:T(8,128)(2,1)S(1)}, u32[]{:S(2)}, u32[]{:S(2)}) collective-permute-start(bf16[2,2,128,128]{3,2,1,0:T(8,128)(2,1)S(1)} %get-tuple-element.25.refs_1_.late.refs_3_), channel_id=1, source_target_pairs={{1,5},{5,1},{4,8},{8,4},{9,13},{13,9},{0,16},{12,28},{17,21},{21,1... | collective-permute-start | bytes 393224 | tf_op jit(solution)/shard_map/ppermute | solution.py:324
  5.9 5.0 %collective-permute-start.4 = (bf16[2,2,128,128]{3,2,1,0:T(8,128)(2,1)S(1)}, bf16[2,2,128,128]{3,2,1,0:T(8,128)(2,1)S(1)}, u32[]{:S(2)}, u32[]{:S(2)}) collective-permute-start(bf16[2,2,128,128]{3,2,1,0:T(8,128)(2,1)S(1)} %get-tuple-element.24.refs_0_.front.refs_2_), channel_id=1, source_target_pairs={{1,5},{5,1},{4,8},{8,4},{9,13},{13,9},{0,16},{12,28},{17,21},{21,1... | collective-permute-start | bytes 393224 | tf_op jit(solution)/shard_map/ppermute | solution.py:324
  6.7 5.1 %copy-start = (bf16[3,3,3,128,256]{4,3,2,1,0:T(8,128)(2,1)S(1)}, bf16[3,3,3,128,256]{4,3,2,1,0:T(8,128)(2,1)}, u32[]{:S(2)}) copy-start(bf16[3,3,3,128,256]{4,3,2,1,0:T(8,128)(2,1)} %second.5) | copy-start | bytes 5308420
  7.6 5.7 %collective-permute-start.1 = (bf16[528,128]{1,0:T(8,128)(2,1)S(1)}, bf16[528,128]{1,0:T(8,128)(2,1)S(1)}, u32[]{:S(2)}, u32[]{:S(2)}) collective-permute-start(bf16[528,128]{1,0:T(8,128)(2,1)S(1)} %get-tuple-element.30), channel_id=1, source_target_pairs={{0,2},{2,0},{1,3},{3,1},{4,6},{6,4},{5,7},{7,5},{8,10},{10,8},{9,1... | collective-permute-start | bytes 405512 | tf_op jit(solution)/shard_map/ppermute | solution.py:309
  8.4 3.4 %collective-permute-start.3 = (bf16[2,2,128,128]{3,2,1,0:T(8,128)(2,1)S(1)}, bf16[2,2,128,128]{3,2,1,0:T(8,128)(2,1)S(1)}, u32[]{:S(2)}, u32[]{:S(2)}) collective-permute-start(bf16[2,2,128,128]{3,2,1,0:T(8,128)(2,1)S(1)} %collective-permute-done.2.passed), channel_id=1, source_target_pairs={{0,1},{1,0},{2,3},{3,2},{4,5},{5,4},{6,7},{7,6},{8,9},{9,8},{10,11... | collective-permute-start | bytes 393224 | tf_op jit(solution)/shard_map/ppermute | solution.py:309
  8.5 5.0 %collective-permute-start.7 = (bf16[2,2,128,128]{3,2,1,0:T(8,128)(2,1)S(1)}, bf16[2,2,128,128]{3,2,1,0:T(8,128)(2,1)S(1)}, u32[]{:S(2)}, u32[]{:S(2)}) collective-permute-start(bf16[2,2,128,128]{3,2,1,0:T(8,128)(2,1)S(1)} %collective-permute-done.2.passed), channel_id=1, source_target_pairs={{1,5},{5,1},{4,8},{8,4},{9,13},{13,9},{0,16},{12,28},{17,21},{21,1... | collective-permute-start | bytes 393224 | tf_op jit(solution)/shard_map/ppermute | solution.py:324
  11.7 5.2 %collective-permute-start.6 = (bf16[2,2,128,128]{3,2,1,0:T(8,128)(2,1)S(1)}, bf16[2,2,128,128]{3,2,1,0:T(8,128)(2,1)S(1)}, u32[]{:S(2)}, u32[]{:S(2)}) collective-permute-start(bf16[2,2,128,128]{3,2,1,0:T(8,128)(2,1)S(1)} %shard_map.59.ahead), channel_id=1, source_target_pairs={{0,2},{2,0},{1,3},{3,1},{4,6},{6,4},{5,7},{7,5},{8,10},{10,8},{9,1... | collective-permute-start | bytes 393224 | tf_op jit(solution)/shard_map/ppermute | solution.py:309
  14.9 1.3 %collective-permute-start.8 = (bf16[2,128,128]{2,1,0:T(8,128)(2,1)S(1)}, bf16[2,128,128]{2,1,0:T(8,128)(2,1)S(1)}, u32[]{:S(2)}, u32[]{:S(2)}) collective-permute-start(bf16[2,128,128]{2,1,0:T(8,128)(2,1)S(1)} %get-tuple-element.37), channel_id=1, source_target_pairs={{0,1},{1,0},{2,3},{3,2},{4,5},{5,4},{6,7},{7,6},{8,9},{9,8},{10,11... | collective-permute-start | bytes 196616 | tf_op jit(solution)/shard_map/ppermute | solution.py:309
  16.9 1.3 %collective-permute-start.9 = (bf16[2,128,128]{2,1,0:T(8,128)(2,1)S(1)}, bf16[2,128,128]{2,1,0:T(8,128)(2,1)S(1)}, u32[]{:S(2)}, u32[]{:S(2)}) collective-permute-start(bf16[2,128,128]{2,1,0:T(8,128)(2,1)S(1)} %get-tuple-element.40), channel_id=1, source_target_pairs={{0,1},{1,0},{2,3},{3,2},{4,5},{5,4},{6,7},{7,6},{8,9},{9,8},{10,11... | collective-permute-start | bytes 196616 | tf_op jit(solution)/shard_map/ppermute | solution.py:309

commit v9 on v7

--- a/solution.py
+++ b/solution.py
@@ -58,11 +58,11 @@
     pairs = (
         (first_bias, first_line),
         (second_bias, second_line),
-        (weight, staged.at[0:size]),
         (video.at[early:, pl.ds(lower * half, half)], late),
         (video.at[:early, pl.ds(lower * half, half)], front),
         (video.at[early:, pl.ds((1 - lower) * half, half)], rest_late),
         (video.at[:early, pl.ds((1 - lower) * half, half)], rest_front),
+        (weight, staged.at[0:size]),
     )
     copies = [pltpu.make_async_copy(source, target, sems.at[k]) for k, (source, target) in enumerate(pairs)]
     for copy in copies:

time: 19.1 us -> 19.2 us (level)
  no operation moved by 1% of the time
where the time goes in v9:
time: 19.2 us; the launch traced here: 19.1 us
  starting transfers between devices  7.24 us (38%)
  Pallas kernels  7.03 us (37%)
  waiting for transfers between devices  4.69 us (24%)
    pallas_call x8, Pallas kernels, call(): pl.pallas_call(kernel, out_shape=outs, in_specs=ins, out_specs=[VMEM] * l...  7.03 us
    ppermute x7, waiting for transfers between devices, cycle(): lax.ppermute(value, axis, [(i, (i + 1) % count) for i in range(count)])  3.93 us
    ppermute x3, starting transfers between devices, across_border(): return lax.ppermute(value, ('clip', 'tile', 'chan'), pairs)  3.81 us
    ppermute x7, starting transfers between devices, cycle(): lax.ppermute(value, axis, [(i, (i + 1) % count) for i in range(count)])  3.43 us
    ppermute x3, waiting for transfers between devices, across_border(): return lax.ppermute(value, ('clip', 'tile', 'chan'), pairs)  0.77 us
  transfers between devices with their start and end apart: 10, of which 6 were waited for; matrix products, arithmetic and copies ran while one was open for 0% of the time, Pallas kernels for 26%

profile of v9, /device:TPU:0, one launch (start us, length us, event | category | flops | bytes accessed | tf_op | source)
XLA Modules:
  0.0 19.1 jit_solution(4143013925961897974)
XLA Ops:
  0.0 1.4 %shard_map.55 = (bf16[2,2,128,128]{3,2,1,0:T(8,128)(2,1)S(1)}, bf16[2,2,128,128]{3,2,1,0:T(8,128)(2,1)S(1)}, bf16[2,2,128,128]{3,2,1,0:T(8,128)(2,1)S(1)}, bf16[...) custom-call(bf16[4,4,128,128]{3,2,1,0:T(8,128)(2,1)} %video.1, bf16[1728,128]{1,0:T(8,128)(2,1)} %bitcast.5, ...), custom_call_target="tpu_custom_call" | custom-call | flops 1000 | bytes 1000 | tf_op jit(solution)/shard_map/pallas_call | solution.py:336
  1.4 0.5 %collective-permute-start = (bf16[1744,128]{1,0:T(8,128)(2,1)S(1)}, bf16[1744,128]{1,0:T(8,128)(2,1)S(1)}, u32[]{:S(2)}, u32[]{:S(2)}) collective-permute-start(bf16[1744,128]{1,0:T(8,128)(2,1)S(1)} %get-tuple-element.29.own), channel_id=1, source_target_pairs={{0,1},{1,0},{2,3},{3,2},{4,5},{5,4},{6,7},{7,6},{8,9},{9,8},{10,11... | collective-permute-start | bytes 1339400 | tf_op jit(solution)/shard_map/ppermute | solution.py:308
  1.9 2.6 %collective-permute-start.2 = (bf16[2,2,128,128]{3,2,1,0:T(8,128)(2,1)S(1)}, bf16[2,2,128,128]{3,2,1,0:T(8,128)(2,1)S(1)}, u32[]{:S(2)}, u32[]{:S(2)}) collective-permute-start(bf16[2,2,128,128]{3,2,1,0:T(8,128)(2,1)S(1)} %get-tuple-element.26.refs_1_.late.refs_3_), channel_id=1, source_target_pairs={{0,2},{2,0},{1,3},{3,1},{4,6},{6,4},{5,7},{7,5},{8,10},{10,8},{9,1... | collective-permute-start | bytes 393224 | tf_op jit(solution)/shard_map/ppermute | solution.py:308
  4.5 1.5 %collective-permute-start.5 = (bf16[2,2,128,128]{3,2,1,0:T(8,128)(2,1)S(1)}, bf16[2,2,128,128]{3,2,1,0:T(8,128)(2,1)S(1)}, u32[]{:S(2)}, u32[]{:S(2)}) collective-permute-start(bf16[2,2,128,128]{3,2,1,0:T(8,128)(2,1)S(1)} %get-tuple-element.26.refs_1_.late.refs_3_), channel_id=1, source_target_pairs={{1,5},{5,1},{4,8},{8,4},{9,13},{13,9},{0,16},{12,28},{17,21},{21,1... | collective-permute-start | bytes 393224 | tf_op jit(solution)/shard_map/ppermute | solution.py:323
  6.0 0.5 %collective-permute-start.4 = (bf16[2,2,128,128]{3,2,1,0:T(8,128)(2,1)S(1)}, bf16[2,2,128,128]{3,2,1,0:T(8,128)(2,1)S(1)}, u32[]{:S(2)}, u32[]{:S(2)}) collective-permute-start(bf16[2,2,128,128]{3,2,1,0:T(8,128)(2,1)S(1)} %get-tuple-element.25.refs_0_.front.refs_2_), channel_id=1, source_target_pairs={{1,5},{5,1},{4,8},{8,4},{9,13},{13,9},{0,16},{12,28},{17,21},{21,1... | collective-permute-start | bytes 393224 | tf_op jit(solution)/shard_map/ppermute | solution.py:323
  6.5 0.3 %shard_map.56 = (bf16[1536,768]{1,0:T(8,128)(2,1)S(1)}, f32[1,256]{1,0:T(1,128)S(1)}, f32[1,256]{1,0:T(1,128)S(1)}) custom-call(bf16[1744,128]{1,0:T(8,128)(2,1)S(1)} %get-tuple-element.29.own, bf16[1744,128]{1,0:T(8,128)(2,1)S(1)} %collective-permute-done.other), custom_call_target="tpu_custom_call" | custom-call | flops 1000 | bytes 1000 | tf_op jit(solution)/shard_map/pallas_call | solution.py:336
  6.8 0.0 copy-start
  6.8 0.9 %shard_map.57 = (bf16[2,2,128,128]{3,2,1,0:T(8,128)(2,1)S(1)}, bf16[528,128]{1,0:T(8,128)(2,1)S(1)}) custom-call(bf16[2,2,128,128]{3,2,1,0:T(8,128)(2,1)S(1)} %get-tuple-element.25.refs_0_.front.refs_2_, bf16[2,2,128,128]{3,2,1,0:T(8,128)(2,1)S(1)} %get-tuple-element.26.refs_1_.late.refs_3_, ...), custom_call_target="tpu_custom_call" | custom-call | flops 1000 | bytes 1000 | tf_op jit(solution)/shard_map/pallas_call | solution.py:336
  7.7 0.1 collective-permute-start.1
  7.8 0.8 %collective-permute-done.2.passed = bf16[2,2,128,128]{3,2,1,0:T(8,128)(2,1)S(1)} collective-permute-done((bf16[2,2,128,128]{3,2,1,0:T(8,128)(2,1)S(1)}, bf16[2,2,128,128]{3,2,1,0:T(8,128)(2,1)S(1)}, u32[]{:S(2)}, u32[]{:S(2)}) %collective-permute-start.2) | collective-permute-done | bytes 131104 | tf_op jit(solution)/shard_map/ppermute | solution.py:308
  8.5 1.8 %collective-permute-start.7 = (bf16[2,2,128,128]{3,2,1,0:T(8,128)(2,1)S(1)}, bf16[2,2,128,128]{3,2,1,0:T(8,128)(2,1)S(1)}, u32[]{:S(2)}, u32[]{:S(2)}) collective-permute-start(bf16[2,2,128,128]{3,2,1,0:T(8,128)(2,1)S(1)} %collective-permute-done.2.passed), channel_id=1, source_target_pairs={{1,5},{5,1},{4,8},{8,4},{9,13},{13,9},{0,16},{12,28},{17,21},{21,1... | collective-permute-start | bytes 393224 | tf_op jit(solution)/shard_map/ppermute | solution.py:323
  10.3 0.6 %collective-permute-done.4.refs_0_.beyond_front = bf16[2,2,128,128]{3,2,1,0:T(8,128)(2,1)S(1)} collective-permute-done((bf16[2,2,128,128]{3,2,1,0:T(8,128)(2,1)S(1)}, bf16[2,2,128,128]{3,2,1,0:T(8,128)(2,1)S(1)}, u32[]{:S(2)}, u32[]{:S(2)}) %collective-permute-start.4) | collective-permute-done | bytes 131104 | tf_op jit(solution)/shard_map/ppermute | solution.py:323
  10.9 0.8 %shard_map.59.ahead = bf16[2,2,128,128]{3,2,1,0:T(8,128)(2,1)S(1)} custom-call(bf16[2,2,128,128]{3,2,1,0:T(8,128)(2,1)S(1)} %collective-permute-done.4.refs_0_.beyond_front, bf16[2,2,128,128]{3,2,1,0:T(8,128)(2,1)S(1)} %collective-permute-done.5.refs_1_.beyond_late, bf16[2,2,128,128]{3,2,1,0:T(8,128)(2,1)S(1)} %get-tuple-element.25.refs_0_.front.refs_2_, ...), custom_call_target="tpu_custom_call" | custom-call | flops 1000 | bytes 1000 | tf_op jit(solution)/shard_map/pallas_call | solution.py:336
  11.8 0.1 collective-permute-start.6
  11.9 1.4 %shard_map.58.partial = f32[2,2,128,256]{3,2,1,0:T(8,128)S(1)} custom-call(bf16[2,2,128,128]{3,2,1,0:T(8,128)(2,1)S(1)} %get-tuple-element.25.refs_0_.front.refs_2_, bf16[2,2,128,128]{3,2,1,0:T(8,128)(2,1)S(1)} %get-tuple-element.26.refs_1_.late.refs_3_, bf16[2,2,128,128]{3,2,1,0:T(8,128)(2,1)S(1)} %get-tuple-element.27.refs_2_.rest_front, ...), custom_call_target="tpu_custom_call" | custom-call | flops 1000 | bytes 1000 | tf_op jit(solution)/shard_map/pallas_call | solution.py:336
  13.4 0.2 collective-permute-done.7.passed_beyond
  13.5 1.5 %shard_map.60 = (bf16[2,128,128]{2,1,0:T(8,128)(2,1)S(1)}, bf16[2,128,128]{2,1,0:T(8,128)(2,1)S(1)}, f32[2,128,256]{2,1,0:T(8,128)S(1)}) custom-call(bf16[2,2,128,128]{3,2,1,0:T(8,128)(2,1)S(1)} %get-tuple-element.25.refs_0_.front.refs_2_, bf16[2,2,128,128]{3,2,1,0:T(8,128)(2,1)S(1)} %get-tuple-element.26.refs_1_.late.refs_3_, ...), custom_call_target="tpu_custom_call" | custom-call | flops 1000 | bytes 1000 | tf_op jit(solution)/shard_map/pallas_call | solution.py:336
  15.0 0.1 collective-permute-start.8
  15.1 1.2 %collective-permute-done.8.refs_3_ = bf16[2,128,128]{2,1,0:T(8,128)(2,1)S(1)} collective-permute-done((bf16[2,128,128]{2,1,0:T(8,128)(2,1)S(1)}, bf16[2,128,128]{2,1,0:T(8,128)(2,1)S(1)}, u32[]{:S(2)}, u32[]{:S(2)}) %collective-permute-start.8) | collective-permute-done | bytes 65568 | tf_op jit(solution)/shard_map/ppermute | solution.py:308
  16.3 0.6 %collective-permute-done.6.handed_outer = bf16[2,2,128,128]{3,2,1,0:T(8,128)(2,1)S(1)} collective-permute-done((bf16[2,2,128,128]{3,2,1,0:T(8,128)(2,1)S(1)}, bf16[2,2,128,128]{3,2,1,0:T(8,128)(2,1)S(1)}, u32[]{:S(2)}, u32[]{:S(2)}) %collective-permute-start.6) | collective-permute-done | bytes 131104 | tf_op jit(solution)/shard_map/ppermute | solution.py:308
  16.9 0.1 shard_map.61
  17.0 0.1 collective-permute-start.9
  17.1 1.2 %collective-permute-done.9.refs_1_ = bf16[2,128,128]{2,1,0:T(8,128)(2,1)S(1)} collective-permute-done((bf16[2,128,128]{2,1,0:T(8,128)(2,1)S(1)}, bf16[2,128,128]{2,1,0:T(8,128)(2,1)S(1)}, u32[]{:S(2)}, u32[]{:S(2)}) %collective-permute-start.9) | collective-permute-done | bytes 65568 | tf_op jit(solution)/shard_map/ppermute | solution.py:308
  18.3 0.7 %shard_map.62 = bf16[2,4,128,128]{3,2,1,0:T(8,128)(2,1)} custom-call(bf16[2,128,128]{2,1,0:T(8,128)(2,1)S(1)} %get-tuple-element.41.refs_0_, bf16[2,128,128]{2,1,0:T(8,128)(2,1)S(1)} %collective-permute-done.9.refs_1_, bf16[2,128,128]{2,1,0:T(8,128)(2,1)S(1)} %get-tuple-element.43.refs_2_, bf16[2,128,128]{2,1,0:T(8,128)(2,1)S(1)} %collective-permute-done.8.refs_3_), custom_call_target="tpu_custom_call" | custom-call | flops 1000 | bytes 1000 | tf_op jit(solution)/shard_map/pallas_call | solution.py:336
  (6 shorter events, 0.0 us)
Async XLA Ops:
  1.4 5.1 %collective-permute-start = (bf16[1744,128]{1,0:T(8,128)(2,1)S(1)}, bf16[1744,128]{1,0:T(8,128)(2,1)S(1)}, u32[]{:S(2)}, u32[]{:S(2)}) collective-permute-start(bf16[1744,128]{1,0:T(8,128)(2,1)S(1)} %get-tuple-element.29.own), channel_id=1, source_target_pairs={{0,1},{1,0},{2,3},{3,2},{4,5},{5,4},{6,7},{7,6},{8,9},{9,8},{10,11... | collective-permute-start | bytes 1339400 | tf_op jit(solution)/shard_map/ppermute | solution.py:308
  1.9 6.7 %collective-permute-start.2 = (bf16[2,2,128,128]{3,2,1,0:T(8,128)(2,1)S(1)}, bf16[2,2,128,128]{3,2,1,0:T(8,128)(2,1)S(1)}, u32[]{:S(2)}, u32[]{:S(2)}) collective-permute-start(bf16[2,2,128,128]{3,2,1,0:T(8,128)(2,1)S(1)} %get-tuple-element.26.refs_1_.late.refs_3_), channel_id=1, source_target_pairs={{0,2},{2,0},{1,3},{3,1},{4,6},{6,4},{5,7},{7,5},{8,10},{10,8},{9,1... | collective-permute-start | bytes 393224 | tf_op jit(solution)/shard_map/ppermute | solution.py:308
  4.5 5.9 %collective-permute-start.5 = (bf16[2,2,128,128]{3,2,1,0:T(8,128)(2,1)S(1)}, bf16[2,2,128,128]{3,2,1,0:T(8,128)(2,1)S(1)}, u32[]{:S(2)}, u32[]{:S(2)}) collective-permute-start(bf16[2,2,128,128]{3,2,1,0:T(8,128)(2,1)S(1)} %get-tuple-element.26.refs_1_.late.refs_3_), channel_id=1, source_target_pairs={{1,5},{5,1},{4,8},{8,4},{9,13},{13,9},{0,16},{12,28},{17,21},{21,1... | collective-permute-start | bytes 393224 | tf_op jit(solution)/shard_map/ppermute | solution.py:323
  6.0 5.0 %collective-permute-start.4 = (bf16[2,2,128,128]{3,2,1,0:T(8,128)(2,1)S(1)}, bf16[2,2,128,128]{3,2,1,0:T(8,128)(2,1)S(1)}, u32[]{:S(2)}, u32[]{:S(2)}) collective-permute-start(bf16[2,2,128,128]{3,2,1,0:T(8,128)(2,1)S(1)} %get-tuple-element.25.refs_0_.front.refs_2_), channel_id=1, source_target_pairs={{1,5},{5,1},{4,8},{8,4},{9,13},{13,9},{0,16},{12,28},{17,21},{21,1... | collective-permute-start | bytes 393224 | tf_op jit(solution)/shard_map/ppermute | solution.py:323
  6.8 5.1 %copy-start = (bf16[3,3,3,128,256]{4,3,2,1,0:T(8,128)(2,1)S(1)}, bf16[3,3,3,128,256]{4,3,2,1,0:T(8,128)(2,1)}, u32[]{:S(2)}) copy-start(bf16[3,3,3,128,256]{4,3,2,1,0:T(8,128)(2,1)} %second.5) | copy-start | bytes 5308420
  7.7 5.7 %collective-permute-start.1 = (bf16[528,128]{1,0:T(8,128)(2,1)S(1)}, bf16[528,128]{1,0:T(8,128)(2,1)S(1)}, u32[]{:S(2)}, u32[]{:S(2)}) collective-permute-start(bf16[528,128]{1,0:T(8,128)(2,1)S(1)} %get-tuple-element.32), channel_id=1, source_target_pairs={{0,2},{2,0},{1,3},{3,1},{4,6},{6,4},{5,7},{7,5},{8,10},{10,8},{9,1... | collective-permute-start | bytes 405512 | tf_op jit(solution)/shard_map/ppermute | solution.py:308
  8.5 3.4 %collective-permute-start.3 = (bf16[2,2,128,128]{3,2,1,0:T(8,128)(2,1)S(1)}, bf16[2,2,128,128]{3,2,1,0:T(8,128)(2,1)S(1)}, u32[]{:S(2)}, u32[]{:S(2)}) collective-permute-start(bf16[2,2,128,128]{3,2,1,0:T(8,128)(2,1)S(1)} %collective-permute-done.2.passed), channel_id=1, source_target_pairs={{0,1},{1,0},{2,3},{3,2},{4,5},{5,4},{6,7},{7,6},{8,9},{9,8},{10,11... | collective-permute-start | bytes 393224 | tf_op jit(solution)/shard_map/ppermute | solution.py:308
  8.5 5.0 %collective-permute-start.7 = (bf16[2,2,128,128]{3,2,1,0:T(8,128)(2,1)S(1)}, bf16[2,2,128,128]{3,2,1,0:T(8,128)(2,1)S(1)}, u32[]{:S(2)}, u32[]{:S(2)}) collective-permute-start(bf16[2,2,128,128]{3,2,1,0:T(8,128)(2,1)S(1)} %collective-permute-done.2.passed), channel_id=1, source_target_pairs={{1,5},{5,1},{4,8},{8,4},{9,13},{13,9},{0,16},{12,28},{17,21},{21,1... | collective-permute-start | bytes 393224 | tf_op jit(solution)/shard_map/ppermute | solution.py:323
  11.8 5.2 %collective-permute-start.6 = (bf16[2,2,128,128]{3,2,1,0:T(8,128)(2,1)S(1)}, bf16[2,2,128,128]{3,2,1,0:T(8,128)(2,1)S(1)}, u32[]{:S(2)}, u32[]{:S(2)}) collective-permute-start(bf16[2,2,128,128]{3,2,1,0:T(8,128)(2,1)S(1)} %shard_map.59.ahead), channel_id=1, source_target_pairs={{0,2},{2,0},{1,3},{3,1},{4,6},{6,4},{5,7},{7,5},{8,10},{10,8},{9,1... | collective-permute-start | bytes 393224 | tf_op jit(solution)/shard_map/ppermute | solution.py:308
  15.0 1.3 %collective-permute-start.8 = (bf16[2,128,128]{2,1,0:T(8,128)(2,1)S(1)}, bf16[2,128,128]{2,1,0:T(8,128)(2,1)S(1)}, u32[]{:S(2)}, u32[]{:S(2)}) collective-permute-start(bf16[2,128,128]{2,1,0:T(8,128)(2,1)S(1)} %get-tuple-element.39), channel_id=1, source_target_pairs={{0,1},{1,0},{2,3},{3,2},{4,5},{5,4},{6,7},{7,6},{8,9},{9,8},{10,11... | collective-permute-start | bytes 196616 | tf_op jit(solution)/shard_map/ppermute | solution.py:308
  17.0 1.3 %collective-permute-start.9 = (bf16[2,128,128]{2,1,0:T(8,128)(2,1)S(1)}, bf16[2,128,128]{2,1,0:T(8,128)(2,1)S(1)}, u32[]{:S(2)}, u32[]{:S(2)}) collective-permute-start(bf16[2,128,128]{2,1,0:T(8,128)(2,1)S(1)} %get-tuple-element.42), channel_id=1, source_target_pairs={{0,1},{1,0},{2,3},{3,2},{4,5},{5,4},{6,7},{7,6},{8,9},{9,8},{10,11... | collective-permute-start | bytes 196616 | tf_op jit(solution)/shard_map/ppermute | solution.py:308
